TPU v7x, 512 devices: a whole 4x8x8 slice. The times are simulated.
512 devices in a mesh: gz: 64 (over z, x, y_lo), gy: 8 (over y_hi, core).
Axes of the slice: x: 4, y: 8 (y_hi: 4, y_lo: 2; y = y_hi * 2 + y_lo), z: 8, core: 2. Of those that a mesh axis runs over, the one named last changes fastest.
Arguments:
- adjoint: float32 [3, 64, 1024, 1024], P(None, 'gz', None, 'gy'), may hold values from -6 to 6
- wind: bfloat16 [3, 64, 1024, 1024], P(None, 'gz', None, 'gy'), may hold values from -5 to 8
- classes: int32 [1024, 1024], P(None, 'gy'), may hold values from 0 to 15
- drag_coef: float32 [16], replicated, may hold values from 0.5 to 10
Outputs:
- adjoint_new: float32 [3, 64, 1024, 1024], P(None, 'gz', None, 'gy')
- sensitivity: float32 [16], replicated
All inputs are finite; a program needn't handle non-finite values. Where the computation divides by a largest or mean magnitude, that divisor is 1e-20 or more.
Results may differ from a plain program's by a relative error of at most 0.0035.
Values may be sent and summed in bfloat16 or wider, within the bound.
No kernel may reach another device: no remote copies, remote signals or barrier semaphores. Data moves between devices by JAX's collectives and lax.ppermute only.
A program may use at most 128 MiB of HBM per device.

v0:
```python
import math

import jax
import jax.numpy as jnp
from jax import lax
from jax.sharding import PartitionSpec as P

viscosity = 0.3
courant = 0.8
epsilon = 1e-06


def extended(x, sides, width):
    for axis, dim in sides:
        size, length = (lax.axis_size(axis), x.shape[dim])
        up = [(i, (i + 1) % size) for i in range(size - 1)]
        down = [(j, i) for i, j in up]
        last = lax.slice_in_dim(x, length - width, length, axis=dim)
        leading = lax.slice_in_dim(x, 0, width, axis=dim)
        before = lax.ppermute(last, axis, up)
        after = lax.ppermute(leading, axis, down)
        x = jnp.concatenate([before, x, after], axis=dim)
    return x


def spectral_tables(length):
    half_len = length // 2
    modes = jnp.arange(half_len, dtype=jnp.int32)
    points = jnp.arange(length, dtype=jnp.int32)
    phase_idx = modes[:, None] * points[None, :] % length
    angles = 2.0 * math.pi / length * phase_idx.astype(jnp.float32)
    cosine = jnp.cos(angles)
    sine = jnp.sin(angles)
    forward = jnp.concatenate([cosine, -sine], axis=0).astype(jnp.bfloat16)
    wave = 2.0 * math.pi / length * modes.astype(jnp.float32)
    weight = jnp.where(modes == 0, jnp.float32(1.0), jnp.float32(2.0)) / length
    first = jnp.concatenate(
        [-(weight * wave)[:, None] * sine, -(weight * wave)[:, None] * cosine], axis=0
    )
    second = jnp.concatenate(
        [-(weight * wave * wave)[:, None] * cosine, (weight * wave * wave)[:, None] * sine], axis=0
    )
    inverse = jnp.concatenate([first.T, second.T], axis=0).astype(jnp.bfloat16)
    return (forward, inverse)


def line_derivs(lines, length):
    fwd_y, inv_y = spectral_tables(length)
    spec_y = jnp.einsum("czxy,jy->czxj", lines, fwd_y, preferred_element_type=jnp.float32).astype(
        jnp.bfloat16
    )
    both_y = jnp.einsum("czxj,dj->czxd", spec_y, inv_y, preferred_element_type=jnp.float32)
    return (both_y[..., :length], both_y[..., length:])


def local(adjoint, wind, classes, drag_coef):
    planes = adjoint.shape[1]
    cells_x = adjoint.shape[2]
    local_y = adjoint.shape[3]
    cells_y = local_y * lax.axis_size("gy")
    total_z = planes * lax.axis_size("gz")
    class_count = drag_coef.shape[0]
    flow = wind.astype(jnp.float32)
    low = adjoint.astype(jnp.bfloat16)
    fwd_x, inv_x = spectral_tables(cells_x)
    spec_x = jnp.einsum("jx,czxy->czjy", fwd_x, low, preferred_element_type=jnp.float32).astype(
        jnp.bfloat16
    )
    both_x = jnp.einsum("dj,czjy->czdy", inv_x, spec_x, preferred_element_type=jnp.float32)
    deriv_x = both_x[:, :, :cells_x]
    second_x = both_x[:, :, cells_x:]
    lines = lax.all_to_all(low, "gy", split_axis=2, concat_axis=3, tiled=True)
    deriv_y, second_y = line_derivs(lines, cells_y)
    deriv_y, second_y = (
        lax.all_to_all(deriv_y, "gy", split_axis=3, concat_axis=2, tiled=True),
        lax.all_to_all(second_y, "gy", split_axis=3, concat_axis=2, tiled=True),
    )
    ydrift = (flow[1] * deriv_y + viscosity * second_y).astype(jnp.bfloat16)
    ydrift = lax.optimization_barrier(ydrift).astype(jnp.float32)
    padded = extended(adjoint.astype(jnp.bfloat16), (("gz", 1),), 1).astype(adjoint.dtype)
    below = padded[:, :-2]
    above = padded[:, 2:]
    deriv_z = (above - below) * 0.5
    second_z = above - 2.0 * adjoint + below
    levels = (lax.axis_index("gz") * planes + jnp.arange(planes, dtype=jnp.int32)).astype(
        jnp.float32
    )
    height = jnp.exp(-2.0 * (levels + 0.5) / total_z)[:, None, None]
    speed = jnp.sqrt(flow[0] * flow[0] + flow[1] * flow[1] + flow[2] * flow[2])
    onehot = classes[None] == jnp.arange(class_count, dtype=jnp.int32)[:, None, None]
    drag = jnp.sum(jnp.where(onehot, drag_coef[:, None, None], jnp.float32(0.0)), axis=0)
    rhs = (
        flow[0] * deriv_x
        + viscosity * second_x
        + ydrift
        + flow[2] * deriv_z
        + viscosity * second_z
        - drag * height * speed * adjoint
    )
    local_top = jnp.max(jnp.sum(jnp.abs(flow), axis=0))
    top = lax.pmax(local_top, ("gz", "gy"))
    step = courant / (top + epsilon)
    adjoint_new = adjoint + step * rhs
    weight_field = height * speed
    scale = 1.0 / math.sqrt(cells_x * cells_y * total_z / class_count)
    column = jnp.sum(weight_field * jnp.sum(adjoint_new * flow, axis=0), axis=0)
    totals = lax.psum(
        jnp.sum(jnp.where(onehot, column[None], jnp.float32(0.0)), axis=(1, 2)), ("gz", "gy")
    )
    sensitivity = -step * scale * totals
    return (adjoint_new, sensitivity)


def solution(mesh):
    return jax.shard_map(
        local,
        mesh=mesh,
        in_specs=(P(None, "gz", None, "gy"), P(None, "gz", None, "gy"), P(None, "gy"), P()),
        out_specs=(P(None, "gz", None, "gy"), P()),
        check_vma=False,
    )
```

profile of v0, /device:TPU:1, one launch (start us, length us, event | category | flops | bytes accessed | tf_op | source)
XLA Modules:
  0.0 406.1 jit_solution(13715445193087830267)
XLA Ops:
  0.6 1.9 copy.154
  4.1 10.3 %all-to-all-start = ((bf16[3,1,1024,128]{3,0,1,2:T(4,128)(2,1)}), bf16[3,1,1024,128]{3,0,1,2:T(4,128)(2,1)S(1)}, u32[]{:S(2)}, u32[]{:S(2)}) async-start(bf16[3,1,1024,128]{3,0,1,2:T(4,128)(2,1)} %copy.138), calls=%async_computation | async-start | bytes 2097152 | tf_op jit(solution)/shard_map/all_to_all | solution.py:72
  14.4 8.7 %multiply_convert_fusion = (bf16[512,1024]{1,0:T(8,128)(2,1)S(1)}, bf16[512,1024]{1,0:T(8,128)(2,1)S(1)}) fusion(f32[512]{0:T(512)S(1)} %fusion.31, f32[512]{0:T(512)S(1)} %fusion.34), kind=kLoop, calls=%fused_computation.15 | loop fusion | flops 9437184 | bytes 2101248 | tf_op jit(solution)/shard_map/convert.4
  24.6 8.6 %multiply_convert_fusion.3 = (bf16[512,1024]{1,0:T(8,128)(2,1)S(1)}, bf16[512,1024]{1,0:T(8,128)(2,1)S(1)}) fusion(f32[512]{0:T(512)S(1)} %fusion.33), kind=kLoop, calls=%fused_computation.18 | loop fusion | flops 9437184 | bytes 2099200 | tf_op jit(solution)/shard_map/convert.6
  34.8 9.2 %negate_convert_fusion = (bf16[512,1024]{1,0:T(8,128)(2,1)}, bf16[512,1024]{1,0:T(8,128)(2,1)}) fusion(), kind=kLoop, calls=%fused_computation.19 | loop fusion | flops 8912896 | bytes 2097152 | tf_op jit(solution)/shard_map/convert.9
  46.5 7.4 %convolution_bitcast_fusion = f32[3,1,128,2048]{3,2,0,1:T(8,128)} fusion(bf16[1024,1024]{0,1:T(8,128)(2,1)} %maximum_bitcast_fusion.5, bf16[1024,1024]{0,1:T(8,128)(2,1)} %maximum_bitcast_fusion.4, bf16[3,128,1024]{1,2,0:T(8,128)(2,1)S(1)} %bitcast.103, bf16[512,1024]{1,0:T(8,128)(2,1)} %get-tuple-element.29, bf16[512,1024]{1,0:T(8,128)(2,1)} %get-tuple-element.30), kind=kOutput, calls=%fused_computation.7 | convolution fusion | flops 2428895232 | bytes 10223616 | tf_op jit(solution)/shard_map/czxj,dj->czxd/dot_general | solution.py:52
  53.9 4.1 %fusion.40 = (f32[3,1,128,1024]{3,2,0,1:T(8,128)}, f32[3,1,128,1024]{3,2,0,1:T(8,128)}) fusion(f32[3,1,128,2048]{3,2,0,1:T(8,128)} %convolution_bitcast_fusion), kind=kLoop, calls=%fused_computation.76 | loop fusion | bytes 6291456 | tf_op jit(solution)/shard_map/slice | solution.py:53
  58.0 4.9 %copy.144 = f32[3,1,128,1024]{2,1,0,3:T(1,128)} copy(f32[3,1,128,1024]{3,2,0,1:T(8,128)} %get-tuple-element.18) | data formatting | bytes 3145728 | tf_op jit(solution)/shard_map/slice | solution.py:53
  62.9 7.2 %all-to-all-start.1 = ((f32[3,1,128,1024]{2,1,0,3:T(1,128)}), f32[3,1,128,1024]{2,1,0,3:T(1,128)}, u32[]{:S(2)}, u32[]{:S(2)}) async-start(f32[3,1,128,1024]{2,1,0,3:T(1,128)} %copy.144), calls=%async_computation.1 | async-start | bytes 3145728 | tf_op jit(solution)/shard_map/all_to_all | solution.py:75
  70.1 4.9 %copy.147 = f32[3,1,128,1024]{2,1,0,3:T(1,128)} copy(f32[3,1,128,1024]{3,2,0,1:T(8,128)} %get-tuple-element.19) | data formatting | bytes 3145728 | tf_op jit(solution)/shard_map/slice | solution.py:53
  75.0 32.9 %all-to-all-done.1 = f32[3,1,128,1024]{2,1,0,3:T(1,128)} async-done(((f32[3,1,128,1024]{2,1,0,3:T(1,128)}), f32[3,1,128,1024]{2,1,0,3:T(1,128)}, u32[]{:S(2)}, u32[]{:S(2)}) %all-to-all-start.1) | async-done | bytes 1572896 | tf_op jit(solution)/shard_map/all_to_all | solution.py:75
  107.9 4.9 %all-to-all-start.2 = ((f32[3,1,128,1024]{2,1,0,3:T(1,128)}), f32[3,1,128,1024]{2,1,0,3:T(1,128)}, u32[]{:S(2)}, u32[]{:S(2)}) async-start(f32[3,1,128,1024]{2,1,0,3:T(1,128)} %copy.147), calls=%async_computation.2 | async-start | bytes 3145728 | tf_op jit(solution)/shard_map/all_to_all | solution.py:76
  116.6 1.8 reduce_max.9
  118.3 4.9 %collective-permute-start = (bf16[3,1,1024,128]{2,3,0,1:T(8,128)(2,1)S(1)}, bf16[3,1,1024,128]{2,3,0,1:T(8,128)(2,1)}, u32[]{:S(2)}, u32[]{:S(2)}) collective-permute-start(bf16[3,1,1024,128]{2,3,0,1:T(8,128)(2,1)S(1)} %convert_element_type.87), channel_id=1, source_target_pairs={{0,8},{8,16},{16,24},{24,32},{32,40},{40,48},{48,56},{56,64},{64,7... | collective-permute-start | bytes 2359304 | tf_op jit(solution)/shard_map/ppermute | solution.py:20
  123.2 154.7 %pmax.7 = f32[]{:T(128)} all-reduce(f32[]{:T(128)} %reduce_max.9), channel_id=1, replica_groups=mesh['gz'=64,'gy'=8] {'gz','gy'}, use_global_device_ids=true, to_apply=%region_2.3 | all-reduce | flops 1 | bytes 8 | tf_op jit(solution)/shard_map/pmax | solution.py:101
  278.0 2.8 select_reduce_fusion.1
  280.7 2.0 copy.151
  286.9 7.4 %convolution_bitcast_fusion.1 = f32[3,1,2048,128]{2,3,0,1:T(8,128)} fusion(bf16[1024,1024]{0,1:T(8,128)(2,1)} %maximum_bitcast_fusion.5, bf16[1024,1024]{0,1:T(8,128)(2,1)} %maximum_bitcast_fusion.4, bf16[512,1024]{1,0:T(8,128)(2,1)} %get-tuple-element.29, bf16[512,1024]{1,0:T(8,128)(2,1)} %get-tuple-element.30, ...), kind=kOutput, calls=%fused_computation.8 | convolution fusion | flops 2428895232 | bytes 10223616 | tf_op jit(solution)/shard_map/dj,czjy->czdy/dot_general | solution.py:69
  294.3 1.9 multiply_bitcast_fusion
  296.2 2.7 copy.145
  298.9 1.7 copy_multiply_fusion
  301.1 1.7 copy-done.5
  303.0 3.5 multiply_reduce_fusion
  309.3 94.7 %psum.7 = f32[16]{0:T(128)S(1)} all-reduce(f32[16]{0:T(128)S(1)} %select_reduce_fusion), channel_id=1, replica_groups=mesh['gz'=64,'gy'=8] {'gz','gy'}, use_global_device_ids=true, to_apply=%region_6.7 | all-reduce | flops 16 | bytes 128 | tf_op jit(solution)/shard_map/psum | solution.py:107
  (49 shorter events, 19.9 us)
Async XLA Ops:
  4.1 40.0 %all-to-all-start = ((bf16[3,1,1024,128]{3,0,1,2:T(4,128)(2,1)}), bf16[3,1,1024,128]{3,0,1,2:T(4,128)(2,1)S(1)}, u32[]{:S(2)}, u32[]{:S(2)}) async-start(bf16[3,1,1024,128]{3,0,1,2:T(4,128)(2,1)} %copy.138), calls=%async_computation | async-start | bytes 2097152 | tf_op jit(solution)/shard_map/all_to_all | solution.py:72
  62.9 45.0 %all-to-all-start.1 = ((f32[3,1,128,1024]{2,1,0,3:T(1,128)}), f32[3,1,128,1024]{2,1,0,3:T(1,128)}, u32[]{:S(2)}, u32[]{:S(2)}) async-start(f32[3,1,128,1024]{2,1,0,3:T(1,128)} %copy.144), calls=%async_computation.1 | async-start | bytes 3145728 | tf_op jit(solution)/shard_map/all_to_all | solution.py:75
  107.9 191.0 %all-to-all-start.2 = ((f32[3,1,128,1024]{2,1,0,3:T(1,128)}), f32[3,1,128,1024]{2,1,0,3:T(1,128)}, u32[]{:S(2)}, u32[]{:S(2)}) async-start(f32[3,1,128,1024]{2,1,0,3:T(1,128)} %copy.147), calls=%async_computation.2 | async-start | bytes 3145728 | tf_op jit(solution)/shard_map/all_to_all | solution.py:76
  112.8 165.2 %copy-start.12 = (f32[16]{0:T(128)S(1)}, f32[16]{0:T(128)}, u32[]{:S(2)}) copy-start(f32[16]{0:T(128)} %param.7) | copy-start | bytes 196
  112.8 188.3 %collective-permute-start.1 = (bf16[3,1,1024,128]{2,3,0,1:T(8,128)(2,1)S(1)}, bf16[3,1,1024,128]{2,3,0,1:T(8,128)(2,1)}, u32[]{:S(2)}, u32[]{:S(2)}) collective-permute-start(bf16[3,1,1024,128]{2,3,0,1:T(8,128)(2,1)S(1)} %convert_element_type.87), channel_id=1, source_target_pairs={{8,0},{16,8},{24,16},{32,24},{40,32},{48,40},{56,48},{64,56},{72,6... | collective-permute-start | bytes 2359304 | tf_op jit(solution)/shard_map/ppermute | solution.py:21
  118.3 182.8 %collective-permute-start = (bf16[3,1,1024,128]{2,3,0,1:T(8,128)(2,1)S(1)}, bf16[3,1,1024,128]{2,3,0,1:T(8,128)(2,1)}, u32[]{:S(2)}, u32[]{:S(2)}) collective-permute-start(bf16[3,1,1024,128]{2,3,0,1:T(8,128)(2,1)S(1)} %convert_element_type.87), channel_id=1, source_target_pairs={{0,8},{8,16},{16,24},{24,32},{32,40},{40,48},{48,56},{56,64},{64,7... | collective-permute-start | bytes 2359304 | tf_op jit(solution)/shard_map/ppermute | solution.py:20
  283.5 2.1 copy-start.11
  283.9 1.3 copy-start
  283.9 1.7 copy-start.4
  298.9 1.9 copy-start.3
  298.9 2.0 copy-start.9
  298.9 2.2 copy-start.8
  300.9 1.9 copy-start.5
  300.9 2.0 copy-start.6
  300.9 2.2 copy-start.7
  303.0 3.5 copy-start.1
  306.5 1.7 copy-start.10
  306.5 97.5 %copy-start.2 = (f32[3,1,1024,128]{2,3,0,1:T(8,128)S(1)}, f32[3,1,1024,128]{2,3,0,1:T(8,128)}, u32[]{:S(2)}) copy-start(f32[3,1,1024,128]{2,3,0,1:T(8,128)} %get-tuple-element.17) | copy-start | bytes 4718596
where the time goes:
time: 407 us; the launch traced here: 406 us
  blocking collectives  249 us (61%)
  other arithmetic  47.3 us (12%)
  waiting for transfers between devices  32.9 us (8%)
  local copies, waits for them, and re-layouts  31.3 us (8%)
  starting transfers between devices  28.7 us (7%)
  matrix products  14.8 us (4%)
    pmax x1, blocking collectives, local(): top = lax.pmax(local_top, ('gz', 'gy'))  155 us
    psum x1, blocking collectives, local(): lax.psum(jnp.sum(jnp.where(onehot, column[None], jnp.float32(0.0)), axis=...  94.7 us
    all_to_all x1, waiting for transfers between devices, local(): lax.all_to_all(deriv_y, 'gy', split_axis=3, concat_axis=2, tiled=True)  32.9 us
    another operation x3, other arithmetic  26.5 us
    slice x3, local copies, waits for them, and re-layouts, line_derivs(): return (both_y[..., :length], both_y[..., length:])  13.8 us
    all_to_all x1, starting transfers between devices, local(): lines = lax.all_to_all(low, 'gy', split_axis=2, concat_axis=3, tiled=True)  10.3 us
    unnamed x29, local copies, waits for them, and re-layouts  8.74 us
  transfers between devices with their start and end apart: 5, of which 1 were waited for; matrix products, arithmetic and copies ran while one was open for 15% of the time, Pallas kernels for 0%

commit v1 on v0

v1 whole, which is shorter than its diff:
```python
import functools
import math

import jax
import jax.numpy as jnp
import ml_dtypes
import numpy as np
from jax import lax
from jax.experimental import pallas as pl
from jax.experimental.pallas import tpu as pltpu
from jax.sharding import PartitionSpec as P

viscosity = 0.3
courant = 0.8
epsilon = 1e-06
LANES = 128
TILE = 256
VMEM_BYTES = 48 * 1024 * 1024
f32 = jnp.float32
bf16 = jnp.bfloat16


@functools.lru_cache(maxsize=None)
def tables(length):
    half = length // 2
    modes = np.arange(half)
    points = np.arange(length)
    angles = (2.0 * np.pi / length) * ((modes[:, None] * points[None, :]) % length)
    cosine, sine = np.cos(angles), np.sin(angles)
    forward = np.concatenate([cosine, -sine], axis=0)
    wave = (2.0 * np.pi / length) * modes
    weight = np.where(modes == 0, 1.0, 2.0) / length
    w1, w2 = (weight * wave)[:, None], (weight * wave * wave)[:, None]
    first = np.concatenate([-w1 * sine, -w1 * cosine], axis=0).T
    second = np.concatenate([-w2 * cosine, w2 * sine], axis=0).T
    low = lambda a: np.ascontiguousarray(a).astype(ml_dtypes.bfloat16)
    return low(forward), low(first), low(second)


def params(sem="arbitrary", n=1):
    return pltpu.CompilerParams(dimension_semantics=(sem,) * n, vmem_limit_bytes=VMEM_BYTES)


def full(shape):
    return pl.BlockSpec(shape, lambda i: (0,) * len(shape))


SMEM = pl.BlockSpec(memory_space=pltpu.SMEM)


def dot(a, b):
    return jnp.dot(a, b, preferred_element_type=f32)


def pack_kernel(adj, wind, send, *lows):
    for c in range(3):
        low = adj[c].astype(bf16)
        send[0, c] = low
        lows[c][...] = low
    send[0, 3] = wind[0]


def pack(adj, wind, parts):
    _, nx, ny = adj.shape
    rows = nx // parts
    return pl.pallas_call(
        pack_kernel,
        grid=(parts,),
        in_specs=[
            pl.BlockSpec((3, rows, ny), lambda i: (0, i, 0)),
            pl.BlockSpec((1, rows, ny), lambda i: (1, i, 0)),
        ],
        out_specs=[pl.BlockSpec((1, 4, rows, ny), lambda i: (i, 0, 0, 0))]
        + [pl.BlockSpec((rows, ny), lambda i: (i, 0))] * 3,
        out_shape=[jax.ShapeDtypeStruct((parts, 4, rows, ny), bf16)]
        + [jax.ShapeDtypeStruct((nx, ny), bf16)] * 3,
        compiler_params=params(),
        cost_estimate=pl.CostEstimate(flops=0, bytes_accessed=nx * ny * 24, transcendentals=0),
        name="pack",
    )(adj, wind)


def class_sums(column, cls, acc, count):
    for k in range(count):
        kept = jnp.where(cls == k, column, 0.0)
        acc[k] += jnp.sum(kept.reshape(-1, 8, kept.shape[-1]), axis=0)


def to_lanes(acc, count, offset):
    per = jnp.sum(acc[...], axis=1)
    per = jnp.sum(per, axis=1, keepdims=True)
    row = lax.broadcasted_iota(jnp.int32, (count, LANES), 0)
    lane = lax.broadcasted_iota(jnp.int32, (count, LANES), 1)
    return jnp.sum(jnp.where(lane == row + offset, per, 0.0), axis=0, keepdims=True)


def x_kernel(steps, count, scal, coef, fwd, inv, l0, l1, l2, adj, wind, cls_ref, rhs, sums, low, spec, acc, top):
    i = pl.program_id(0)
    ny = l0.shape[1]

    @pl.when(i == 0)
    def _():
        for c, ref in enumerate((l0, l1, l2)):
            low[:, c * ny:(c + 1) * ny] = ref[...]
        acc[...] = jnp.zeros_like(acc)
        top[...] = jnp.zeros_like(top)

    @pl.when(i < steps)
    def _():
        spec[pl.ds(pl.multiple_of(i * TILE, TILE), TILE), :] = dot(fwd[...], low[...]).astype(bf16)

    @pl.when(i >= steps)
    def _():
        dx = dot(inv[0, :TILE], spec[...])
        dxx = dot(inv[0, TILE:], spec[...])
        cls = cls_ref[...]
        w = [wind[c].astype(f32) for c in range(3)]
        speed = jnp.sqrt(w[0] * w[0] + w[1] * w[1] + w[2] * w[2])
        weight = scal[0] * speed
        drag = jnp.zeros_like(speed)
        for k in range(count):
            drag = jnp.where(cls == k, coef[k], drag)
        damp = drag * weight + 2.0 * viscosity
        total = jnp.zeros_like(speed)
        for c in range(3):
            a = adj[c]
            total += a * w[c]
            cols = slice(c * ny, (c + 1) * ny)
            rhs[c] = w[0] * dx[:, cols] + viscosity * dxx[:, cols] - damp * a
        class_sums(weight * total, cls, acc, count)
        size = jnp.abs(w[0]) + jnp.abs(w[1]) + jnp.abs(w[2])
        top[...] = jnp.maximum(top[...], jnp.max(size.reshape(-1, 8, ny), axis=0))

    @pl.when(i == pl.num_programs(0) - 1)
    def _():
        lane = lax.broadcasted_iota(jnp.int32, (1, LANES), 1)
        peak = jnp.max(jnp.max(top[...], axis=0, keepdims=True), axis=1, keepdims=True)
        sums[...] = jnp.where(lane == 2 * count, peak, to_lanes(acc, count, 0))


def x_part(scal, coef, fwd, inv, lows, adj, wind, classes):
    _, nx, ny = adj.shape
    count = coef.shape[0]
    steps = nx // TILE
    late = lambda i: jnp.maximum(i - steps, 0)
    return pl.pallas_call(
        functools.partial(x_kernel, steps, count),
        grid=(2 * steps,),
        in_specs=[SMEM, SMEM,
                  pl.BlockSpec((TILE, nx), lambda i: (jnp.minimum(i, steps - 1), 0)),
                  pl.BlockSpec((1, 2 * TILE, nx), lambda i: (late(i), 0, 0))]
        + [full((nx, ny))] * 3
        + [pl.BlockSpec((3, TILE, ny), lambda i: (0, late(i), 0)),
           pl.BlockSpec((3, TILE, ny), lambda i: (0, late(i), 0)),
           pl.BlockSpec((TILE, ny), lambda i: (late(i), 0))],
        out_specs=[pl.BlockSpec((3, TILE, ny), lambda i: (0, late(i), 0)), full((1, LANES))],
        out_shape=[jax.ShapeDtypeStruct((3, nx, ny), f32), jax.ShapeDtypeStruct((1, LANES), f32)],
        scratch_shapes=[pltpu.VMEM((nx, 3 * ny), bf16), pltpu.VMEM((nx, 3 * ny), bf16),
                        pltpu.VMEM((count, 8, ny), f32), pltpu.VMEM((8, ny), f32)],
        compiler_params=params(),
        cost_estimate=pl.CostEstimate(flops=6 * nx * nx * 3 * ny, bytes_accessed=12 * 1024 * 1024, transcendentals=0),
        name="x_part",
    )(scal, coef, fwd, inv, *lows, adj, wind, classes)


def y_kernel(steps, recv, fwd, inv, out, lines, spec):
    i = pl.program_id(0)
    parts, _, rows, ny = recv.shape

    @pl.when(i == 0)
    def _():
        for s in range(parts):
            for c in range(3):
                lines[c * rows:(c + 1) * rows, s * ny:(s + 1) * ny] = recv[s, c]

    @pl.when(i < steps)
    def _():
        spec[:, pl.ds(pl.multiple_of(i * TILE, TILE), TILE)] = dot(lines[...], fwd[...]).astype(bf16)

    @pl.when(i >= steps)
    def _():
        dy = dot(spec[...], inv[0, :, :TILE])
        dyy = dot(spec[...], inv[0, :, TILE:])
        per = TILE // ny
        for s in range(per):
            w1 = recv[(i - steps) * per + s, 3].astype(f32)
            cols = slice(s * ny, (s + 1) * ny)
            for c in range(3):
                at = slice(c * rows, (c + 1) * rows)
                out[s, c] = (w1 * dy[at, cols] + viscosity * dyy[at, cols]).astype(bf16)


def y_part(recv, fwd, inv):
    parts, _, rows, ny = recv.shape
    n = parts * ny
    steps = n // TILE
    late = lambda i: jnp.maximum(i - steps, 0)
    return pl.pallas_call(
        functools.partial(y_kernel, steps),
        grid=(2 * steps,),
        in_specs=[full(recv.shape),
                  pl.BlockSpec((n, TILE), lambda i: (0, jnp.minimum(i, steps - 1))),
                  pl.BlockSpec((1, n, 2 * TILE), lambda i: (late(i), 0, 0))],
        out_specs=pl.BlockSpec((TILE // ny, 3, rows, ny), lambda i: (late(i), 0, 0, 0)),
        out_shape=jax.ShapeDtypeStruct((parts, 3, rows, ny), bf16),
        scratch_shapes=[pltpu.VMEM((3 * rows, n), bf16), pltpu.VMEM((3 * rows, n), bf16)],
        compiler_params=params(),
        cost_estimate=pl.CostEstimate(flops=6 * n * n * 3 * rows, bytes_accessed=8 * 1024 * 1024, transcendentals=0),
        name="y_part",
    )(recv, fwd, inv)


def join_kernel(count, scal, early, part, wind, cls_ref, drift, p0, p1, p2, q0, q1, q2, rhs, sums, acc):
    i = pl.program_id(0)

    @pl.when(i == 0)
    def _():
        acc[...] = jnp.zeros_like(acc)

    w = [wind[c].astype(f32) for c in range(3)]
    speed = jnp.sqrt(w[0] * w[0] + w[1] * w[1] + w[2] * w[2])
    slope = (0.5 * scal[1]) * w[2]
    total = jnp.zeros_like(speed)
    for c, (p, q) in enumerate(((p0, q0), (p1, q1), (p2, q2))):
        near, far = p[...].astype(f32), q[...].astype(f32)
        r = part[c] + drift[0, c].astype(f32) + slope * (near - far) + viscosity * (near + far)
        rhs[c] = r
        total += r * w[c]
    class_sums(scal[0] * speed * total, cls_ref[...], acc, count)

    @pl.when(i == pl.num_programs(0) - 1)
    def _():
        sums[...] = early[...] + to_lanes(acc, count, count)


def join(scal, early, part, wind, classes, drift, near, far, count):
    parts, _, rows, ny = drift.shape
    nx = parts * rows
    three = pl.BlockSpec((3, rows, ny), lambda i: (0, i, 0))
    plane = pl.BlockSpec((rows, ny), lambda i: (i, 0))
    return pl.pallas_call(
        functools.partial(join_kernel, count),
        grid=(parts,),
        in_specs=[SMEM, full((1, LANES)), three, three, plane,
                  pl.BlockSpec((1, 3, rows, ny), lambda i: (i, 0, 0, 0))] + [plane] * 6,
        out_specs=[three, full((1, LANES))],
        out_shape=[jax.ShapeDtypeStruct((3, nx, ny), f32), jax.ShapeDtypeStruct((1, LANES), f32)],
        scratch_shapes=[pltpu.VMEM((count, 8, ny), f32)],
        compiler_params=params(),
        cost_estimate=pl.CostEstimate(flops=100 * nx * ny, bytes_accessed=8 * 1024 * 1024, transcendentals=0),
        name="join",
    )(scal, early, part, wind, classes, drift, *near, *far)


def finish_kernel(count, scale, got, adj, rhs, new, sens):
    rows = got[...].reshape(-1, LANES)
    lane = lax.broadcasted_iota(jnp.int32, (1, LANES), 1)
    sums = jnp.sum(rows, axis=0, keepdims=True)
    tops = jnp.max(rows, axis=0, keepdims=True)
    top = jnp.max(jnp.where(lane == 2 * count, tops, 0.0), axis=1, keepdims=True)
    step = courant / (top + epsilon)
    for c in range(3):
        new[c] = adj[c] + step * rhs[c]

    @pl.when(pl.program_id(0) == 0)
    def _():
        later = pltpu.roll(sums, LANES - count, 1)
        sens[...] = -step * scale * (sums + step * later)


def finish(got, adj, rhs, count, scale):
    _, nx, ny = adj.shape
    parts = 4
    three = pl.BlockSpec((3, nx // parts, ny), lambda i: (0, i, 0))
    return pl.pallas_call(
        functools.partial(finish_kernel, count, scale),
        grid=(parts,),
        in_specs=[full(got.shape), three, three],
        out_specs=[three, full((1, LANES))],
        out_shape=[jax.ShapeDtypeStruct(adj.shape, f32), jax.ShapeDtypeStruct((1, LANES), f32)],
        compiler_params=params(),
        cost_estimate=pl.CostEstimate(flops=10 * nx * ny, bytes_accessed=5 * 1024 * 1024, transcendentals=0),
        name="finish",
    )(got, adj, rhs)


def swap(x, axes):
    return lax.all_to_all(x, axes, split_axis=0, concat_axis=0, tiled=True)


def local(adjoint, wind, classes, drag_coef):
    gz, gy = lax.axis_size("gz"), lax.axis_size("gy")
    _, _, nx, ny = adjoint.shape
    total_y = ny * gy
    count = drag_coef.shape[0]
    adj = adjoint.reshape(3, nx, ny)
    wnd = wind.reshape(3, nx, ny)

    fx, d1x, d2x = tables(nx)
    fy, d1y, d2y = tables(total_y)
    inv_x = np.concatenate([d1x.reshape(-1, TILE, nx), d2x.reshape(-1, TILE, nx)], axis=1)
    per = lambda d: d.reshape(-1, TILE, total_y).transpose(0, 2, 1)
    inv_y = np.concatenate([per(d1y), per(d2y)], axis=2)
    fwd_y = np.ascontiguousarray(fy.T)

    me = lax.axis_index("gz")
    height = jnp.exp(-2.0 * (me.astype(f32) + 0.5) / gz)
    sign = jnp.where(me % 2 == 0, 1.0, -1.0).astype(f32)
    scal = jnp.stack([height, sign])

    send, *lows = pack(adj, wnd, gy)
    recv = swap(send, "gy")

    pair = [(i, i ^ 1) for i in range(gz)]
    onward = [(i, i + 2) for i in range(0, gz - 2, 2)] + [(i, i - 2) for i in range(3, gz, 2)]
    near = [lax.ppermute(low, "gz", pair) for low in lows]
    far = [lax.ppermute(low, "gz", onward) for low in near]

    part, early = x_part(scal, drag_coef, jnp.asarray(fx), jnp.asarray(inv_x), lows, adj, wnd, classes)
    drift = swap(y_part(recv, jnp.asarray(fwd_y), jnp.asarray(inv_y)), "gy")
    rhs, sums = join(scal, early, part, wnd, classes, drift, near, far, count)

    everyone = gz * gy
    got = swap(jnp.broadcast_to(sums[None], (everyone, 1, LANES)), ("gz", "gy"))
    scale = 1.0 / math.sqrt(nx * total_y * gz / count)
    new, sens = finish(got, adj, rhs, count, scale)
    return new.reshape(adjoint.shape), sens[0, :count]


def solution(mesh):
    return jax.shard_map(
        local,
        mesh=mesh,
        in_specs=(P(None, "gz", None, "gy"), P(None, "gz", None, "gy"), P(None, "gy"), P()),
        out_specs=(P(None, "gz", None, "gy"), P()),
        check_vma=False,
    )
```

time: 407 us -> 162 us (0.40)
  blocking collectives: 249 us -> 74.4 us
  other arithmetic: 47.3 us -> 0.08 us
  Pallas kernels: 0 us -> 25 us
  matrix products: 14.8 us -> 0 us
  local copies, waits for them, and re-layouts: 31.3 us -> 17.3 us
  waiting for transfers between devices: 32.9 us -> 21.7 us
  starting transfers between devices: 28.7 us -> 21.6 us
    pmax x1 -> x0, blocking collectives: 155 us -> none  [local(): top = lax.pmax(local_top, ('gz', 'gy'))]
    psum x1 -> x0, blocking collectives: 94.7 us -> none  [local(): lax.psum(jnp.sum(jnp.where(onehot, column[None], jnp.float32(0.0)), axis=...]
    all_to_all x0 -> x2, blocking collectives: none -> 74.4 us  [swap(): return lax.all_to_all(x, axes, split_axis=0, concat_axis=0, tiled=True)]
    all_to_all x3 -> x1, waiting for transfers between devices: 32.9 us -> 0.01 us  [swap(): return lax.all_to_all(x, axes, split_axis=0, concat_axis=0, tiled=True)]
    another operation x3 -> x1, other arithmetic: 26.5 us -> 0.08 us  [local(): scal = jnp.stack([height, sign])]
    pallas_call x0 -> x5, Pallas kernels: none -> 25 us  [the longest x1 8.98 us: x_part(): pl.pallas_call(functools.partial(x_kernel, steps, count), grid=(2 * steps...]
    ppermute x2 -> x6, waiting for transfers between devices: 0.01 us -> 21.7 us  [the longest x3 21.7 us: local(): near = [lax.ppermute(low, 'gz', pair) for low in lows]]
    all_to_all x3 -> x1, starting transfers between devices: 22.4 us -> 4.26 us  [swap(): return lax.all_to_all(x, axes, split_axis=0, concat_axis=0, tiled=True)]
  transfers between devices with their start and end apart: 5 -> 7, of which waited for: 1 -> 3; matrix products, arithmetic and copies ran while one was open for 15% -> 0% of each run, Pallas kernels for 0% -> 6%
where the time goes in v1:
time: 162 us; the launch traced here: 161 us
  blocking collectives  74.4 us (46%)
  Pallas kernels  25 us (15%)
  waiting for transfers between devices  21.7 us (13%)
  starting transfers between devices  21.6 us (13%)
  local copies, waits for them, and re-layouts  17.3 us (11%)
    all_to_all x2, blocking collectives, swap(): return lax.all_to_all(x, axes, split_axis=0, concat_axis=0, tiled=True)  74.4 us
    ppermute x3, waiting for transfers between devices, local(): near = [lax.ppermute(low, 'gz', pair) for low in lows]  21.7 us
    unnamed x44, local copies, waits for them, and re-layouts  16.6 us
    ppermute x3, starting transfers between devices, local(): far = [lax.ppermute(low, 'gz', onward) for low in near]  9.19 us
    pallas_call x1, Pallas kernels, x_part(): pl.pallas_call(functools.partial(x_kernel, steps, count), grid=(2 * steps...  8.98 us
    ppermute x3, starting transfers between devices, local(): near = [lax.ppermute(low, 'gz', pair) for low in lows]  8.16 us
    pallas_call x1, Pallas kernels, y_part(): pl.pallas_call(functools.partial(y_kernel, steps), grid=(2 * steps,), in_...  6.98 us
    pallas_call x1, Pallas kernels, join(): pl.pallas_call(functools.partial(join_kernel, count), grid=(parts,), in_s...  5.32 us
  transfers between devices with their start and end apart: 7, of which 3 were waited for; matrix products, arithmetic and copies ran while one was open for 0% of the time, Pallas kernels for 6%

profile of v1, /device:TPU:1, one launch (start us, length us, event | category | flops | bytes accessed | tf_op | source)
XLA Modules:
  0.0 160.9 jit_solution(7403478815341185992)
XLA Ops:
  0.6 1.4 copy-done
  2.0 1.1 copy-done.2
  5.7 36.7 %all_to_all.15.recv = bf16[8,4,128,128]{3,2,1,0:T(8,128)(2,1)S(1)} all-to-all(bf16[8,4,128,128]{3,2,1,0:T(8,128)(2,1)S(1)} %get-tuple-element.17), channel_id=1, replica_groups=mesh['gz'=64,'gy'=8] {'gy'}, dimensions={0} | all-to-all | bytes 2097152 | tf_op jit(solution)/shard_map/all_to_all | solution.py:288
  42.5 7.0 %y_part.1 = bf16[8,3,128,128]{3,2,1,0:T(8,128)(2,1)S(1)} custom-call(bf16[8,4,128,128]{3,2,1,0:T(8,128)(2,1)S(1)} %all_to_all.15.recv, bf16[1024,1024]{1,0:T(8,128)(2,1)S(1)} %copy-done.21, bf16[4,1024,512]{2,1,0:T(8,128)(2,1)} %constant.42.clone.inv), custom_call_target="tpu_custom_call" | custom-call | flops 2415919104 | bytes 8388608 | tf_op jit(solution)/shard_map/y_part/pallas_call | solution.py:198
  50.4 4.3 %all-to-all-start.1 = ((bf16[8,3,128,128]{3,2,1,0:T(8,128)(2,1)}), bf16[8,3,128,128]{3,2,1,0:T(8,128)(2,1)S(1)}, u32[]{:S(2)}, u32[]{:S(2)}) async-start(bf16[8,3,128,128]{3,2,1,0:T(8,128)(2,1)} %copy-done.7), calls=%async_computation.1 | async-start | bytes 1572864 | tf_op jit(solution)/shard_map/all_to_all | solution.py:288
  54.6 2.9 %collective-permute-start = (bf16[1024,128]{1,0:T(8,128)(2,1)}, bf16[1024,128]{1,0:T(8,128)(2,1)S(1)}, u32[]{:S(2)}, u32[]{:S(2)}) collective-permute-start(bf16[1024,128]{1,0:T(8,128)(2,1)} %copy-done.8), channel_id=1, source_target_pairs={{0,8},{8,0},{16,24},{24,16},{32,40},{40,32},{48,56},{56,48},{64,72... | collective-permute-start | bytes 786440 | tf_op jit(solution)/shard_map/ppermute | solution.py:316
  57.5 2.4 %collective-permute-start.1 = (bf16[1024,128]{1,0:T(8,128)(2,1)}, bf16[1024,128]{1,0:T(8,128)(2,1)}, u32[]{:S(2)}, u32[]{:S(2)}) collective-permute-start(bf16[1024,128]{1,0:T(8,128)(2,1)} %copy-done.10), channel_id=1, source_target_pairs={{0,8},{8,0},{16,24},{24,16},{32,40},{40,32},{48,56},{56,48},{64,72... | collective-permute-start | bytes 786440 | tf_op jit(solution)/shard_map/ppermute | solution.py:316
  59.9 2.9 %collective-permute-start.2 = (bf16[1024,128]{1,0:T(8,128)(2,1)}, bf16[1024,128]{1,0:T(8,128)(2,1)}, u32[]{:S(2)}, u32[]{:S(2)}) collective-permute-start(bf16[1024,128]{1,0:T(8,128)(2,1)} %copy-done.12), channel_id=1, source_target_pairs={{0,8},{8,0},{16,24},{24,16},{32,40},{40,32},{48,56},{56,48},{64,72... | collective-permute-start | bytes 786440 | tf_op jit(solution)/shard_map/ppermute | solution.py:316
  62.9 16.5 %collective-permute-done.p0 = bf16[1024,128]{1,0:T(8,128)(2,1)S(1)} collective-permute-done((bf16[1024,128]{1,0:T(8,128)(2,1)}, bf16[1024,128]{1,0:T(8,128)(2,1)S(1)}, u32[]{:S(2)}, u32[]{:S(2)}) %collective-permute-start) | collective-permute-done | bytes 262176 | tf_op jit(solution)/shard_map/ppermute | solution.py:316
  79.3 3.1 %collective-permute-start.3 = (bf16[1024,128]{1,0:T(8,128)(2,1)S(1)}, bf16[1024,128]{1,0:T(8,128)(2,1)S(1)}, u32[]{:S(2)}, u32[]{:S(2)}) collective-permute-start(bf16[1024,128]{1,0:T(8,128)(2,1)S(1)} %collective-permute-done.p0), channel_id=1, source_target_pairs={{0,16},{16,32},{32,48},{48,64},{64,80},{80,96},{96,112},{112,128},... | collective-permute-start | bytes 786440 | tf_op jit(solution)/shard_map/ppermute | solution.py:317
  82.4 2.7 %collective-permute-done.1.p1 = bf16[1024,128]{1,0:T(8,128)(2,1)} collective-permute-done((bf16[1024,128]{1,0:T(8,128)(2,1)}, bf16[1024,128]{1,0:T(8,128)(2,1)}, u32[]{:S(2)}, u32[]{:S(2)}) %collective-permute-start.1) | collective-permute-done | bytes 262176 | tf_op jit(solution)/shard_map/ppermute | solution.py:316
  85.1 3.1 %collective-permute-start.4 = (bf16[1024,128]{1,0:T(8,128)(2,1)}, bf16[1024,128]{1,0:T(8,128)(2,1)S(1)}, u32[]{:S(2)}, u32[]{:S(2)}) collective-permute-start(bf16[1024,128]{1,0:T(8,128)(2,1)} %collective-permute-done.1.p1), channel_id=1, source_target_pairs={{0,16},{16,32},{32,48},{48,64},{64,80},{80,96},{96,112},{112,128},... | collective-permute-start | bytes 786440 | tf_op jit(solution)/shard_map/ppermute | solution.py:317
  88.1 2.5 %collective-permute-done.2.p2 = bf16[1024,128]{1,0:T(8,128)(2,1)} collective-permute-done((bf16[1024,128]{1,0:T(8,128)(2,1)}, bf16[1024,128]{1,0:T(8,128)(2,1)}, u32[]{:S(2)}, u32[]{:S(2)}) %collective-permute-start.2) | collective-permute-done | bytes 262176 | tf_op jit(solution)/shard_map/ppermute | solution.py:316
  90.7 3.1 %collective-permute-start.5 = (bf16[1024,128]{1,0:T(8,128)(2,1)}, bf16[1024,128]{1,0:T(8,128)(2,1)S(1)}, u32[]{:S(2)}, u32[]{:S(2)}) collective-permute-start(bf16[1024,128]{1,0:T(8,128)(2,1)} %collective-permute-done.2.p2), channel_id=1, source_target_pairs={{0,16},{16,32},{32,48},{48,64},{64,80},{80,96},{96,112},{112,128},... | collective-permute-start | bytes 786440 | tf_op jit(solution)/shard_map/ppermute | solution.py:317
  93.8 1.0 copy-done.4
  94.9 0.9 copy-done.9
  95.8 0.9 copy-done.11
  96.8 0.9 copy-done.13
  97.7 9.0 %x_part.1 = (f32[3,1024,128]{2,1,0:T(8,128)S(1)}, f32[1,128]{1,0:T(1,128)S(1)}) custom-call(f32[2]{0:T(128)S(1)} %pad_maximum_fusion.scal, f32[16]{0:T(128)S(1)} %copy-done.20, bf16[1024,1024]{1,0:T(8,128)(2,1)} %constant.39.clone.fwd, bf16[4,512,1024]{2,1,0:T(8,128)(2,1)} %constant.40.clone.inv, bf16[1024,128]{1,0:T(8,128)(2,1)S(1)} %copy-done.9, ...), custom_call_target="tpu_custom_call" | custom-call | flops 2415919104 | bytes 12582912 | tf_op jit(solution)/shard_map/x_part/pallas_call | solution.py:146
  106.7 1.1 copy-done.6
  110.0 1.0 copy-done.5
  113.9 5.3 %join.1 = (f32[3,1024,128]{2,1,0:T(8,128)S(1)}, f32[1,128]{1,0:T(1,128)S(1)}) custom-call(f32[2]{0:T(128)S(1)} %pad_maximum_fusion.scal, f32[1,128]{1,0:T(1,128)S(1)} %get-tuple-element.15.early, f32[3,1024,128]{2,1,0:T(8,128)} %copy-done.6, bf16[3,1024,128]{2,1,0:T(8,128)(2,1)S(1)} %bitcast.15, s32[1024,128]{1,0:T(8,128)S(1)} %copy-done.5, ...), custom_call_target="tpu_custom_call" | custom-call | flops 13107200 | bytes 8388608 | tf_op jit(solution)/shard_map/join/pallas_call | solution.py:241
  119.4 37.7 %all_to_all.16.got = f32[512,1,128]{2,1,0:T(1,128)S(1)} all-to-all(f32[512,1,128]{2,1,0:T(1,128)S(1)} %broadcast_in_dim.9), channel_id=1, replica_groups=mesh['gz'=64,'gy'=8] {'gz','gy'}, dimensions={0} | all-to-all | bytes 524288 | tf_op jit(solution)/shard_map/all_to_all | solution.py:288
  157.1 3.3 %finish.1 = (f32[3,1024,128]{2,1,0:T(8,128)}, f32[1,128]{1,0:T(1,128)S(1)}) custom-call(f32[512,1,128]{2,1,0:T(1,128)S(1)} %all_to_all.16.got, f32[3,1024,128]{2,1,0:T(8,128)S(1)} %bitcast.12, f32[3,1024,128]{2,1,0:T(8,128)S(1)} %get-tuple-element.19.rhs), custom_call_target="tpu_custom_call" | custom-call | flops 1310720 | bytes 5242880 | tf_op jit(solution)/shard_map/finish/pallas_call | solution.py:275
  (44 shorter events, 9.2 us)
Async XLA Ops:
  0.6 1.4 copy-start
  2.0 1.1 copy-start.2
  3.2 39.3 %copy-start.21 = (bf16[1024,1024]{1,0:T(8,128)(2,1)S(1)}, bf16[1024,1024]{1,0:T(8,128)(2,1)}, u32[]{:S(2)}) copy-start(bf16[1024,1024]{1,0:T(8,128)(2,1)} %constant.41.clone.fwd) | copy-start | bytes 6291460
  42.5 51.4 %copy-start.3 = (bf16[3,1,1024,128]{3,2,1,0:T(8,128)(2,1)S(1)}, bf16[3,1,1024,128]{3,2,1,0:T(8,128)(2,1)}, u32[]{:S(2)}) copy-start(bf16[3,1,1024,128]{3,2,1,0:T(8,128)(2,1)} %param.9) | copy-start | bytes 2359300
  42.5 51.4 %copy-start.20 = (f32[16]{0:T(128)S(1)}, f32[16]{0:T(128)}, u32[]{:S(2)}) copy-start(f32[16]{0:T(128)} %coef.1) | copy-start | bytes 196
  49.5 0.9 copy-start.7
  50.4 43.5 %copy-start.1 = (f32[3,1,1024,128]{3,2,1,0:T(8,128)S(1)}, f32[3,1,1024,128]{3,2,1,0:T(8,128)}, u32[]{:S(2)}) copy-start(f32[3,1,1024,128]{3,2,1,0:T(8,128)} %param.8) | copy-start | bytes 4718596
  50.4 59.6 %all-to-all-start.1 = ((bf16[8,3,128,128]{3,2,1,0:T(8,128)(2,1)}), bf16[8,3,128,128]{3,2,1,0:T(8,128)(2,1)S(1)}, u32[]{:S(2)}, u32[]{:S(2)}) async-start(bf16[8,3,128,128]{3,2,1,0:T(8,128)(2,1)} %copy-done.7), calls=%async_computation.1 | async-start | bytes 1572864 | tf_op jit(solution)/shard_map/all_to_all | solution.py:288
  54.6 24.7 %collective-permute-start = (bf16[1024,128]{1,0:T(8,128)(2,1)}, bf16[1024,128]{1,0:T(8,128)(2,1)S(1)}, u32[]{:S(2)}, u32[]{:S(2)}) collective-permute-start(bf16[1024,128]{1,0:T(8,128)(2,1)} %copy-done.8), channel_id=1, source_target_pairs={{0,8},{8,0},{16,24},{24,16},{32,40},{40,32},{48,56},{56,48},{64,72... | collective-permute-start | bytes 786440 | tf_op jit(solution)/shard_map/ppermute | solution.py:316
  57.5 27.6 %collective-permute-start.1 = (bf16[1024,128]{1,0:T(8,128)(2,1)}, bf16[1024,128]{1,0:T(8,128)(2,1)}, u32[]{:S(2)}, u32[]{:S(2)}) collective-permute-start(bf16[1024,128]{1,0:T(8,128)(2,1)} %copy-done.10), channel_id=1, source_target_pairs={{0,8},{8,0},{16,24},{24,16},{32,40},{40,32},{48,56},{56,48},{64,72... | collective-permute-start | bytes 786440 | tf_op jit(solution)/shard_map/ppermute | solution.py:316
  59.9 30.8 %collective-permute-start.2 = (bf16[1024,128]{1,0:T(8,128)(2,1)}, bf16[1024,128]{1,0:T(8,128)(2,1)}, u32[]{:S(2)}, u32[]{:S(2)}) collective-permute-start(bf16[1024,128]{1,0:T(8,128)(2,1)} %copy-done.12), channel_id=1, source_target_pairs={{0,8},{8,0},{16,24},{24,16},{32,40},{40,32},{48,56},{56,48},{64,72... | collective-permute-start | bytes 786440 | tf_op jit(solution)/shard_map/ppermute | solution.py:316
  79.3 28.5 %collective-permute-start.3 = (bf16[1024,128]{1,0:T(8,128)(2,1)S(1)}, bf16[1024,128]{1,0:T(8,128)(2,1)S(1)}, u32[]{:S(2)}, u32[]{:S(2)}) collective-permute-start(bf16[1024,128]{1,0:T(8,128)(2,1)S(1)} %collective-permute-done.p0), channel_id=1, source_target_pairs={{0,16},{16,32},{32,48},{48,64},{64,80},{80,96},{96,112},{112,128},... | collective-permute-start | bytes 786440 | tf_op jit(solution)/shard_map/ppermute | solution.py:317
  85.1 23.5 %collective-permute-start.4 = (bf16[1024,128]{1,0:T(8,128)(2,1)}, bf16[1024,128]{1,0:T(8,128)(2,1)S(1)}, u32[]{:S(2)}, u32[]{:S(2)}) collective-permute-start(bf16[1024,128]{1,0:T(8,128)(2,1)} %collective-permute-done.1.p1), channel_id=1, source_target_pairs={{0,16},{16,32},{32,48},{48,64},{64,80},{80,96},{96,112},{112,128},... | collective-permute-start | bytes 786440 | tf_op jit(solution)/shard_map/ppermute | solution.py:317
  90.7 18.6 %collective-permute-start.5 = (bf16[1024,128]{1,0:T(8,128)(2,1)}, bf16[1024,128]{1,0:T(8,128)(2,1)S(1)}, u32[]{:S(2)}, u32[]{:S(2)}) collective-permute-start(bf16[1024,128]{1,0:T(8,128)(2,1)} %collective-permute-done.2.p2), channel_id=1, source_target_pairs={{0,16},{16,32},{32,48},{48,64},{64,80},{80,96},{96,112},{112,128},... | collective-permute-start | bytes 786440 | tf_op jit(solution)/shard_map/ppermute | solution.py:317
  93.8 1.0 copy-start.4
  94.9 0.9 copy-start.9
  95.8 0.9 copy-start.11
  96.8 0.9 copy-start.13
  106.7 1.1 copy-start.6
  108.6 0.7 copy-start.16
  110.0 1.0 copy-start.5
  111.1 0.9 copy-start.15
  112.0 0.9 copy-start.17
  113.0 0.9 copy-start.19
  (5 other events, 3.6 us)

commit v2 on v1

v2 whole, which is shorter than its diff:
```python
import functools
import math

import jax
import jax.numpy as jnp
import ml_dtypes
import numpy as np
from jax import lax
from jax.experimental import pallas as pl
from jax.experimental.pallas import tpu as pltpu
from jax.sharding import PartitionSpec as P

viscosity = 0.3
courant = 0.8
epsilon = 1e-06
LANES = 128
TILE = 256
VMEM_MIB = 16
f32 = jnp.float32
bf16 = jnp.bfloat16


@functools.lru_cache(maxsize=None)
def tables(length):
    half = length // 2
    modes = np.arange(half)
    points = np.arange(length)
    angles = (2.0 * np.pi / length) * ((modes[:, None] * points[None, :]) % length)
    cosine, sine = np.cos(angles), np.sin(angles)
    forward = np.concatenate([cosine, -sine], axis=0)
    wave = (2.0 * np.pi / length) * modes
    weight = np.where(modes == 0, 1.0, 2.0) / length
    w1, w2 = (weight * wave)[:, None], (weight * wave * wave)[:, None]
    first = np.concatenate([-w1 * sine, -w1 * cosine], axis=0).T
    second = np.concatenate([-w2 * cosine, w2 * sine], axis=0).T
    low = lambda a: np.ascontiguousarray(a).astype(ml_dtypes.bfloat16)
    return low(forward), low(first), low(second)


@functools.lru_cache(maxsize=None)
def line_tables(length):
    half = length // 2
    modes = np.arange(half)
    angles = (2.0 * np.pi / length) * ((modes[:, None] * np.arange(length)[None, :]) % length)
    wave = (2.0 * np.pi / length) * modes
    weight = np.where(modes == 0, 1.0, 2.0) / length
    first = -(weight * wave) @ np.sin(angles)
    second = -(weight * wave * wave) @ np.cos(angles)
    gap = np.arange(half)[None, :] - np.arange(half)[:, None]
    made = []
    for row in (first, second):
        a, b = row[gap % length], row[(gap + half) % length]
        made += [0.5 * (a + b), 0.5 * (a - b)]
    every = np.stack(made).reshape(4, half, half // TILE, TILE).transpose(2, 0, 1, 3)
    return np.ascontiguousarray(every).astype(ml_dtypes.bfloat16)


CHUNKS = 4


def params(mib=VMEM_MIB, **more):
    return pltpu.CompilerParams(vmem_limit_bytes=mib * 1024 * 1024, **more)


def begin(copies, sems, first=0):
    made = [pltpu.make_async_copy(src, dst, sems.at[first + n]) for n, (src, dst) in enumerate(copies)]
    for copy in made:
        copy.start()
    return made


def finish_all(made):
    for copy in made:
        copy.wait()


def full(shape):
    return pl.BlockSpec(shape, lambda i: (0,) * len(shape))


SMEM = pl.BlockSpec(memory_space=pltpu.SMEM)
HBM = pl.BlockSpec(memory_space=pltpu.HBM)
SMALL = pl.BlockSpec(memory_space=pltpu.VMEM)
near_by = functools.partial(pltpu.with_memory_space_constraint, memory_space=pltpu.VMEM)
far_off = functools.partial(pltpu.with_memory_space_constraint, memory_space=pltpu.HBM)


def dot(a, b):
    return jnp.dot(a, b, preferred_element_type=f32)


def pack_kernel(adj, wind, send, lows, adj_v, wind_v, send_v, lows_v, sem_in, sem_out):
    parts, _, rows, _ = send.shape
    per = parts // CHUNKS
    loads, stores = [], []
    for k in range(CHUNKS):
        at = pl.ds(k * per * rows, per * rows)
        loads.append(begin([(adj.at[:, at], adj_v.at[:, at]), (wind.at[1, at], wind_v.at[at])], sem_in, 2 * k))
    for k in range(CHUNKS):
        finish_all(loads[k])
        for s in range(k * per, (k + 1) * per):
            at = slice(s * rows, (s + 1) * rows)
            for c in range(3):
                low = adj_v[c, at].astype(bf16)
                send_v[s, c] = low
                lows_v[c, at] = low
            send_v[s, 3] = wind_v[at]
        at, part = pl.ds(k * per * rows, per * rows), pl.ds(k * per, per)
        stores += begin([(send_v.at[part], send.at[part]), (lows_v.at[:, at], lows.at[:, at])], sem_out, 2 * k)
    finish_all(stores)


def pack(adj, wind, parts):
    _, nx, ny = adj.shape
    rows = nx // parts
    sent, kept = (parts, 4, rows, ny), (3, nx, ny)
    return pl.pallas_call(
        pack_kernel,
        in_specs=[HBM, HBM],
        out_specs=[HBM, HBM],
        out_shape=[pltpu.HBM(sent, bf16), pltpu.HBM(kept, bf16)],
        scratch_shapes=[pltpu.VMEM(kept, f32), pltpu.VMEM((nx, ny), bf16), pltpu.VMEM(sent, bf16), pltpu.VMEM(kept, bf16),
                        pltpu.SemaphoreType.DMA((2 * CHUNKS,)), pltpu.SemaphoreType.DMA((2 * CHUNKS,))],
        compiler_params=params(),
        cost_estimate=pl.CostEstimate(flops=0, bytes_accessed=nx * ny * 32, transcendentals=0),
        name="pack",
    )(far_off(adj), far_off(wind))


def class_sums(column, cls, acc, count):
    for k in range(count):
        kept = jnp.where(cls == k, column, 0.0)
        acc[k] += jnp.sum(kept.reshape(-1, 8, kept.shape[-1]), axis=0)


def to_lanes(acc, count, offset):
    per = jnp.sum(acc[...], axis=1)
    per = jnp.sum(per, axis=1, keepdims=True)
    row = lax.broadcasted_iota(jnp.int32, (count, LANES), 0)
    lane = lax.broadcasted_iota(jnp.int32, (count, LANES), 1)
    return jnp.sum(jnp.where(lane == row + offset, per, 0.0), axis=0, keepdims=True)


def x_kernel(steps, count, scal, coef, fwd, inv, lows, adj, wind, cls_ref, rhs, sums, low, spec, acc, top):
    i = pl.program_id(0)
    ny = lows.shape[2]

    @pl.when(i == 0)
    def _():
        for c in range(3):
            low[:, c * ny:(c + 1) * ny] = lows[c]
        acc[...] = jnp.zeros_like(acc)
        top[...] = jnp.zeros_like(top)

    @pl.when(i < steps)
    def _():
        spec[pl.ds(pl.multiple_of(i * TILE, TILE), TILE), :] = dot(fwd[...], low[...]).astype(bf16)

    @pl.when(i >= steps)
    def _():
        dx = dot(inv[0, :TILE], spec[...])
        dxx = dot(inv[0, TILE:], spec[...])
        cls = cls_ref[...]
        w = [wind[c].astype(f32) for c in range(3)]
        speed = jnp.sqrt(w[0] * w[0] + w[1] * w[1] + w[2] * w[2])
        weight = scal[0] * speed
        drag = jnp.zeros_like(speed)
        for k in range(count):
            drag = jnp.where(cls == k, coef[k], drag)
        damp = drag * weight + 2.0 * viscosity
        total = jnp.zeros_like(speed)
        for c in range(3):
            a = adj[c]
            total += a * w[c]
            cols = slice(c * ny, (c + 1) * ny)
            rhs[c] = w[0] * dx[:, cols] + viscosity * dxx[:, cols] - damp * a
        class_sums(weight * total, cls, acc, count)
        size = jnp.abs(w[0]) + jnp.abs(w[1]) + jnp.abs(w[2])
        top[...] = jnp.maximum(top[...], jnp.max(size.reshape(-1, 8, ny), axis=0))

    @pl.when(i == pl.num_programs(0) - 1)
    def _():
        lane = lax.broadcasted_iota(jnp.int32, (1, LANES), 1)
        peak = jnp.max(jnp.max(top[...], axis=0, keepdims=True), axis=1, keepdims=True)
        sums[...] = jnp.where(lane == 2 * count, peak, to_lanes(acc, count, 0))


def x_part(scal, coef, fwd, inv, lows, adj, wind, classes):
    _, nx, ny = adj.shape
    count = coef.shape[0]
    steps = nx // TILE
    late = lambda i: jnp.maximum(i - steps, 0)
    return pl.pallas_call(
        functools.partial(x_kernel, steps, count),
        grid=(2 * steps,),
        in_specs=[SMEM, SMEM,
                  pl.BlockSpec((TILE, nx), lambda i: (jnp.minimum(i, steps - 1), 0)),
                  pl.BlockSpec((1, 2 * TILE, nx), lambda i: (late(i), 0, 0))]
        + [full((3, nx, ny))]
        + [pl.BlockSpec((3, TILE, ny), lambda i: (0, late(i), 0)),
           pl.BlockSpec((3, TILE, ny), lambda i: (0, late(i), 0)),
           pl.BlockSpec((TILE, ny), lambda i: (late(i), 0))],
        out_specs=[pl.BlockSpec((3, TILE, ny), lambda i: (0, late(i), 0)), full((1, LANES))],
        out_shape=[pltpu.HBM((3, nx, ny), f32), jax.ShapeDtypeStruct((1, LANES), f32)],
        scratch_shapes=[pltpu.VMEM((nx, 3 * ny), bf16), pltpu.VMEM((nx, 3 * ny), bf16),
                        pltpu.VMEM((count, 8, ny), f32), pltpu.VMEM((8, ny), f32)],
        compiler_params=params(60, dimension_semantics=("arbitrary",)),
        cost_estimate=pl.CostEstimate(flops=6 * nx * nx * 3 * ny, bytes_accessed=12 * 1024 * 1024, transcendentals=0),
        name="x_part",
    )(scal, coef, fwd, inv, far_off(lows), adj, wind, classes)


def y_kernel(after, recv, table, out, plus, minus, table_v, out_v, sem_t, sem_o):
    parts, _, rows, ny = recv.shape
    half, steps = parts // 2, table.shape[0]
    tiles = begin([(table.at[t], table_v.at[t]) for t in range(steps)], sem_t)
    for s in range(half):
        for c in range(3):
            u, v = recv[s, c].astype(f32), recv[s + half, c].astype(f32)
            at = (slice(c * rows, (c + 1) * rows), slice(s * ny, (s + 1) * ny))
            plus[at] = (u + v).astype(bf16)
            minus[at] = (u - v).astype(bf16)
    per = TILE // ny
    stores = []
    for t in range(steps):
        tiles[t].wait()
        for c in range(3):
            at = slice(c * rows, (c + 1) * rows)
            p1, q1 = dot(plus[at], table_v[t, 0]), dot(minus[at], table_v[t, 1])
            p2, q2 = dot(plus[at], table_v[t, 2]), dot(minus[at], table_v[t, 3])
            for dy, dyy, base in ((p1 + q1, p2 + q2, t * per), (p1 - q1, p2 - q2, half + t * per)):
                for s in range(per):
                    cols = slice(s * ny, (s + 1) * ny)
                    w1 = recv[base + s, 3].astype(f32)
                    out_v[base + s, c] = (w1 * dy[:, cols] + viscosity * dyy[:, cols]).astype(bf16)
        ends = [pl.ds(base, per) for base in (t * per, half + t * per)]
        stores += begin([(out_v.at[e], out.at[e]) for e in ends], sem_o, 2 * t)
    finish_all(stores)


def y_part(after, recv, table):
    parts, _, rows, ny = recv.shape
    n, steps = parts * ny, table.shape[0]
    sent = (parts, 3, rows, ny)
    dma = pltpu.SemaphoreType.DMA
    return pl.pallas_call(
        y_kernel,
        in_specs=[SMALL, SMALL, HBM],
        out_specs=HBM,
        out_shape=pltpu.HBM(sent, bf16),
        scratch_shapes=[pltpu.VMEM((3 * rows, n // 2), bf16), pltpu.VMEM((3 * rows, n // 2), bf16),
                        pltpu.VMEM(table.shape, bf16), pltpu.VMEM(sent, bf16), dma((steps,)), dma((2 * steps,))],
        compiler_params=params(),
        cost_estimate=pl.CostEstimate(flops=2 * n * n * 3 * rows, bytes_accessed=4 * 1024 * 1024, transcendentals=0),
        name="y_part",
    )(after, near_by(recv), far_off(table))


def speed_of(w):
    return jnp.sqrt(w[0] * w[0] + w[1] * w[1] + w[2] * w[2])


def z_kernel(count, scal, early, part, wind, cls_ref, near, far, rhs, sums, acc):
    i = pl.program_id(0)

    @pl.when(i == 0)
    def _():
        acc[...] = jnp.zeros_like(acc)

    w = [wind[c].astype(f32) for c in range(3)]
    slope = (0.5 * scal[1]) * w[2]
    total = jnp.zeros_like(slope)
    for c in range(3):
        p, q = near[c].astype(f32), far[c].astype(f32)
        r = part[c] + slope * (p - q) + viscosity * (p + q)
        rhs[c] = r
        total += r * w[c]
    class_sums(scal[0] * speed_of(w) * total, cls_ref[...], acc, count)

    @pl.when(i == pl.num_programs(0) - 1)
    def _():
        sums[...] = early[...] + to_lanes(acc, count, count)


def z_part(scal, early, part, wind, classes, near, far, count):
    _, nx, ny = part.shape
    rows = nx // CHUNKS
    three = pl.BlockSpec((3, rows, ny), lambda i: (0, i, 0))
    return pl.pallas_call(
        functools.partial(z_kernel, count),
        grid=(CHUNKS,),
        in_specs=[SMEM, full((1, LANES)), three, three, pl.BlockSpec((rows, ny), lambda i: (i, 0)), three, three],
        out_specs=[three, full((1, LANES))],
        out_shape=[pltpu.HBM((3, nx, ny), f32), jax.ShapeDtypeStruct((1, LANES), f32)],
        scratch_shapes=[pltpu.VMEM((count, 8, ny), f32)],
        compiler_params=params(dimension_semantics=("arbitrary",)),
        cost_estimate=pl.CostEstimate(flops=100 * nx * ny, bytes_accessed=8 * 1024 * 1024, transcendentals=0),
        name="z_part",
    )(scal, early, far_off(part), far_off(wind), far_off(classes), far_off(near), far_off(far))


def join_kernel(count, scal, early, part, wind, classes, adj, drift, rhs, adj_v, sums,
                part_v, wind_v, cls_v, acc, sem_in, sem_adj):
    parts, _, rows, _ = drift.shape
    per = parts // CHUNKS
    loads = []
    for k in range(CHUNKS):
        at = pl.ds(k * per * rows, per * rows)
        loads.append(begin([(wind.at[:, at], wind_v.at[:, at]), (classes.at[at], cls_v.at[at]),
                            (part.at[:, at], part_v.at[:, at])], sem_in, 3 * k))
    kept = begin([(adj, adj_v)], sem_adj)
    acc[...] = jnp.zeros_like(acc)
    for k in range(CHUNKS):
        finish_all(loads[k])
        for s in range(k * per, (k + 1) * per):
            at = slice(s * rows, (s + 1) * rows)
            w = [wind_v[c, at].astype(f32) for c in range(3)]
            total = jnp.zeros_like(w[0])
            for c in range(3):
                d = drift[s, c].astype(f32)
                rhs[c, at] = part_v[c, at] + d
                total += d * w[c]
            class_sums(scal[0] * speed_of(w) * total, cls_v[at], acc, count)
    sums[...] = jnp.broadcast_to((early[...] + to_lanes(acc, count, count))[None], sums.shape)
    finish_all(kept)


def join(scal, early, part, wind, classes, adj, drift, count):
    parts, _, rows, ny = drift.shape
    nx = parts * rows
    whole = (3, nx, ny)
    dma = pltpu.SemaphoreType.DMA
    return pl.pallas_call(
        functools.partial(join_kernel, count),
        in_specs=[SMEM, SMALL, HBM, HBM, HBM, HBM, SMALL],
        out_specs=[SMALL, SMALL, SMALL],
        out_shape=[pltpu.VMEM(whole, f32), pltpu.VMEM(whole, f32), jax.ShapeDtypeStruct((parts, 1, LANES), f32)],
        scratch_shapes=[pltpu.VMEM(whole, f32), pltpu.VMEM(whole, bf16), pltpu.VMEM((nx, ny), jnp.int32),
                        pltpu.VMEM((count, 8, ny), f32), dma((3 * CHUNKS,)), dma((1,))],
        compiler_params=params(),
        cost_estimate=pl.CostEstimate(flops=100 * nx * ny, bytes_accessed=8 * 1024 * 1024, transcendentals=0),
        name="join",
    )(scal, early, far_off(part), far_off(wind), far_off(classes), far_off(adj), near_by(drift))


def merge(rows, count):
    lane = lax.broadcasted_iota(jnp.int32, (1, LANES), 1)
    return jnp.where(lane == 2 * count, jnp.max(rows, axis=0), jnp.sum(rows, axis=0))


def fold_kernel(count, got, out):
    out[...] = jnp.broadcast_to(merge(got[...], count)[None], out.shape)


def fold(got, size, count):
    return pl.pallas_call(
        functools.partial(fold_kernel, count),
        out_shape=jax.ShapeDtypeStruct((size, 1, LANES), f32),
        compiler_params=params(4),
        name="fold",
    )(got)


def finish_kernel(count, scale, got, adj, rhs, new, sens, new_v, sems):
    nx = adj.shape[1]
    rows = nx // CHUNKS
    sums = merge(got[...], count)
    lane = lax.broadcasted_iota(jnp.int32, (1, LANES), 1)
    top = jnp.max(jnp.where(lane == 2 * count, sums, 0.0), axis=1, keepdims=True)
    step = courant / (top + epsilon)
    stores = []
    for k in range(CHUNKS):
        at = slice(k * rows, (k + 1) * rows)
        for c in range(3):
            new_v[c, at] = adj[c, at] + step * rhs[c, at]
        at = pl.ds(k * rows, rows)
        stores += begin([(new_v.at[:, at], new.at[:, at])], sems, k)
    later = pltpu.roll(sums, LANES - count, 1)
    sens[...] = (-step * scale * (sums + step * later))[:, :count]
    finish_all(stores)


def finish(got, adj, rhs, count, scale):
    return pl.pallas_call(
        functools.partial(finish_kernel, count, scale),
        in_specs=[SMALL, SMALL, SMALL],
        out_specs=[HBM, SMALL],
        out_shape=[pltpu.HBM(adj.shape, f32), jax.ShapeDtypeStruct((1, count), f32)],
        scratch_shapes=[pltpu.VMEM(adj.shape, f32), pltpu.SemaphoreType.DMA((CHUNKS,))],
        compiler_params=params(),
        cost_estimate=pl.CostEstimate(flops=2 * adj.size, bytes_accessed=12 * adj.size, transcendentals=0),
        name="finish",
    )(got, near_by(adj), near_by(rhs))


def swap(x, axes):
    return lax.all_to_all(x, axes, split_axis=0, concat_axis=0, tiled=True)


def local(adjoint, wind, classes, drag_coef):
    gz, gy = lax.axis_size("gz"), lax.axis_size("gy")
    _, _, nx, ny = adjoint.shape
    total_y = ny * gy
    count = drag_coef.shape[0]
    adj = adjoint.reshape(3, nx, ny)
    wnd = wind.reshape(3, nx, ny)

    fx, d1x, d2x = tables(nx)
    inv_x = np.concatenate([d1x.reshape(-1, TILE, nx), d2x.reshape(-1, TILE, nx)], axis=1)

    me = lax.axis_index("gz")
    height = jnp.exp(-2.0 * (me.astype(f32) + 0.5) / gz)
    sign = jnp.where(me % 2 == 0, 1.0, -1.0).astype(f32)
    scal = jnp.stack([height, sign])

    send, lows = pack(adj, wnd, gy)
    recv = swap(send, "gy")

    pair = [(i, i ^ 1) for i in range(gz)]
    onward = [(i, i + 2) for i in range(0, gz - 2, 2)] + [(i, i - 2) for i in range(3, gz, 2)]
    near = lax.ppermute(lows, "gz", pair)
    far = lax.ppermute(near, "gz", onward)

    part, early = x_part(scal, drag_coef, jnp.asarray(fx), jnp.asarray(inv_x), lows, adj, wnd, classes)
    drift = swap(y_part(early, recv, jnp.asarray(line_tables(total_y))), "gy")
    part, early = z_part(scal, early, part, wnd, classes, near, far, count)
    rhs, adj, sums = join(scal, early, part, wnd, classes, adj, drift, count)

    got = swap(fold(swap(sums, "gy"), gz, count), "gz")
    scale = 1.0 / math.sqrt(nx * total_y * gz / count)
    new, sens = finish(got, adj, rhs, count, scale)
    return new.reshape(adjoint.shape), sens.reshape(count)


def solution(mesh):
    return jax.shard_map(
        local,
        mesh=mesh,
        in_specs=(P(None, "gz", None, "gy"), P(None, "gz", None, "gy"), P(None, "gy"), P()),
        out_specs=(P(None, "gz", None, "gy"), P()),
        check_vma=False,
    )
```

time: 162 us -> 129 us (0.80)
  blocking collectives: 74.4 us -> 40.2 us
  waiting for transfers between devices: 21.7 us -> 38.3 us
  local copies, waits for them, and re-layouts: 17.3 us -> 1.57 us
    all_to_all x2, blocking collectives: 74.4 us -> 40.2 us  [swap(): return lax.all_to_all(x, axes, split_axis=0, concat_axis=0, tiled=True)]
    unnamed x44 -> x12, local copies, waits for them, and re-layouts: 16.6 us -> 1.57 us
    all_to_all x1 -> x2, waiting for transfers between devices: 0.01 us -> 13.3 us  [swap(): return lax.all_to_all(x, axes, split_axis=0, concat_axis=0, tiled=True)]
    ppermute x6 -> x2, starting transfers between devices: 17.3 us -> 4.99 us  [the longest x1 3.08 us: local(): far = lax.ppermute(near, 'gz', onward)]
    all_to_all x1 -> x2, starting transfers between devices: 4.26 us -> 15 us  [swap(): return lax.all_to_all(x, axes, split_axis=0, concat_axis=0, tiled=True)]
    ppermute x6 -> x2, waiting for transfers between devices: 21.7 us -> 25 us  [the longest x1 16 us: local(): far = lax.ppermute(near, 'gz', onward)]
    pallas_call x1, Pallas kernels: 8.98 us -> 10.7 us  [x_part(): pl.pallas_call(functools.partial(x_kernel, steps, count), grid=(2 * steps...]
    pallas_call x4 -> x6, Pallas kernels: 16 us -> 15.9 us  [the longest x1 5.05 us: z_part(): pl.pallas_call(functools.partial(z_kernel, count), grid=(CHUNKS,), in_spe...]
  transfers between devices with their start and end apart: 7 -> 4, of which waited for: 3 -> 3; matrix products, arithmetic and copies ran while one was open for 0% -> 0% of each run, Pallas kernels for 6% -> 15%
where the time goes in v2:
time: 129 us; the launch traced here: 128 us
  blocking collectives  40.2 us (31%)
  waiting for transfers between devices  38.3 us (30%)
  Pallas kernels  26.6 us (21%)
  starting transfers between devices  20 us (16%)
  local copies, waits for them, and re-layouts  1.57 us (1%)
    all_to_all x2, blocking collectives, swap(): return lax.all_to_all(x, axes, split_axis=0, concat_axis=0, tiled=True)  40.2 us
    ppermute x1, waiting for transfers between devices, local(): far = lax.ppermute(near, 'gz', onward)  16 us
    all_to_all x2, starting transfers between devices, swap(): return lax.all_to_all(x, axes, split_axis=0, concat_axis=0, tiled=True)  15 us
    all_to_all x2, waiting for transfers between devices, swap(): return lax.all_to_all(x, axes, split_axis=0, concat_axis=0, tiled=True)  13.3 us
    pallas_call x1, Pallas kernels, x_part(): pl.pallas_call(functools.partial(x_kernel, steps, count), grid=(2 * steps...  10.7 us
    ppermute x1, waiting for transfers between devices, local(): near = lax.ppermute(lows, 'gz', pair)  8.99 us
    pallas_call x1, Pallas kernels, z_part(): pl.pallas_call(functools.partial(z_kernel, count), grid=(CHUNKS,), in_spe...  5.05 us
    pallas_call x1, Pallas kernels, y_part(): pl.pallas_call(y_kernel, in_specs=[SMALL, SMALL, HBM], out_specs=HBM, out...  3.31 us
  transfers between devices with their start and end apart: 4, of which 3 were waited for; matrix products, arithmetic and copies ran while one was open for 0% of the time, Pallas kernels for 15%

profile of v2, /device:TPU:1, one launch (start us, length us, event | category | flops | bytes accessed | tf_op | source)
XLA Modules:
  0.0 128.0 jit_solution(15656975414842854294)
XLA Ops:
  0.6 2.4 %pack.1 = (bf16[8,4,128,128]{3,2,1,0:T(8,128)(2,1)}, bf16[3,1024,128]{2,1,0:T(8,128)(2,1)}) custom-call(f32[3,1024,128]{2,1,0:T(8,128)} %bitcast.8, bf16[3,1024,128]{2,1,0:T(8,128)(2,1)} %bitcast.11), custom_call_target="tpu_custom_call" | custom-call | bytes 4194304 | tf_op jit(solution)/shard_map/pack/pallas_call | solution.py:117
  3.1 0.0 copy-start.4
  3.1 10.5 %all-to-all-start = ((bf16[8,4,128,128]{3,2,1,0:T(8,128)(2,1)}), bf16[8,4,128,128]{3,2,1,0:T(8,128)(2,1)S(1)}, u32[]{:S(2)}, u32[]{:S(2)}) async-start(bf16[8,4,128,128]{3,2,1,0:T(8,128)(2,1)} %get-tuple-element.18), calls=%async_computation | async-start | bytes 2097152 | tf_op jit(solution)/shard_map/all_to_all | solution.py:397
  13.5 0.0 copy-done.4
  13.6 1.9 %collective-permute-start = (bf16[3,1024,128]{2,1,0:T(8,128)(2,1)S(1)}, bf16[3,1024,128]{2,1,0:T(8,128)(2,1)S(1)}, u32[]{:S(2)}, u32[]{:S(2)}) collective-permute-start(bf16[3,1024,128]{2,1,0:T(8,128)(2,1)S(1)} %copy-done.4), channel_id=1, source_target_pairs={{0,8},{8,0},{16,24},{24,16},{32,40},{40,32},{48,56},{56,48},{64,72... | collective-permute-start | bytes 2359304 | tf_op jit(solution)/shard_map/ppermute | solution.py:421
  15.5 0.6 pad_maximum_fusion.scal
  16.1 10.7 %x_part.1 = (f32[3,1024,128]{2,1,0:T(8,128)}, f32[1,128]{1,0:T(1,128)}) custom-call(f32[2]{0:T(128)} %pad_maximum_fusion.scal, f32[16]{0:T(128)} %coef.1, bf16[1024,1024]{1,0:T(8,128)(2,1)} %constant.37.clone.fwd, bf16[4,512,1024]{2,1,0:T(8,128)(2,1)} %constant.38.clone.inv, bf16[3,1024,128]{2,1,0:T(8,128)(2,1)} %get-tuple-element.13.lows, ...), custom_call_target="tpu_custom_call" | custom-call | flops 2415919104 | bytes 12582912 | tf_op jit(solution)/shard_map/x_part/pallas_call | solution.py:193
  26.8 13.3 %all-to-all-done.recv = bf16[8,4,128,128]{3,2,1,0:T(8,128)(2,1)S(1)} async-done(((bf16[8,4,128,128]{3,2,1,0:T(8,128)(2,1)}), bf16[8,4,128,128]{3,2,1,0:T(8,128)(2,1)S(1)}, u32[]{:S(2)}, u32[]{:S(2)}) %all-to-all-start) | async-done | bytes 1048608 | tf_op jit(solution)/shard_map/all_to_all | solution.py:397
  40.0 0.7 copy-done.1
  40.7 3.3 %y_part.1 = bf16[8,3,128,128]{3,2,1,0:T(8,128)(2,1)} custom-call(f32[1,128]{1,0:T(1,128)S(1)} %copy-done.1, bf16[8,4,128,128]{3,2,1,0:T(8,128)(2,1)S(1)} %all-to-all-done.recv, bf16[2,4,512,256]{3,2,1,0:T(8,128)(2,1)} %constant.39.clone.table), custom_call_target="tpu_custom_call" | custom-call | flops 805306368 | bytes 4194304 | tf_op jit(solution)/shard_map/y_part/pallas_call | solution.py:246
  44.0 0.0 copy-start
  44.0 0.0 copy-start.2
  44.0 4.5 %all-to-all-start.1 = ((bf16[8,3,128,128]{3,2,1,0:T(8,128)(2,1)}), bf16[8,3,128,128]{3,2,1,0:T(8,128)(2,1)S(1)}, u32[]{:S(2)}, u32[]{:S(2)}) async-start(bf16[8,3,128,128]{3,2,1,0:T(8,128)(2,1)} %y_part.1), calls=%async_computation.1 | async-start | bytes 1572864 | tf_op jit(solution)/shard_map/all_to_all | solution.py:397
  48.6 9.0 %collective-permute-done.near = bf16[3,1024,128]{2,1,0:T(8,128)(2,1)S(1)} collective-permute-done((bf16[3,1024,128]{2,1,0:T(8,128)(2,1)S(1)}, bf16[3,1024,128]{2,1,0:T(8,128)(2,1)S(1)}, u32[]{:S(2)}, u32[]{:S(2)}) %collective-permute-start) | collective-permute-done | bytes 786464 | tf_op jit(solution)/shard_map/ppermute | solution.py:421
  57.6 3.1 %collective-permute-start.1 = (bf16[3,1024,128]{2,1,0:T(8,128)(2,1)S(1)}, bf16[3,1024,128]{2,1,0:T(8,128)(2,1)S(1)}, u32[]{:S(2)}, u32[]{:S(2)}) collective-permute-start(bf16[3,1024,128]{2,1,0:T(8,128)(2,1)S(1)} %collective-permute-done.near), channel_id=1, source_target_pairs={{0,16},{16,32},{32,48},{48,64},{64,80},{80,96},{96,112},{112,128},... | collective-permute-start | bytes 2359304 | tf_op jit(solution)/shard_map/ppermute | solution.py:422
  60.6 16.0 %collective-permute-done.1.far = bf16[3,1024,128]{2,1,0:T(8,128)(2,1)S(1)} collective-permute-done((bf16[3,1024,128]{2,1,0:T(8,128)(2,1)S(1)}, bf16[3,1024,128]{2,1,0:T(8,128)(2,1)S(1)}, u32[]{:S(2)}, u32[]{:S(2)}) %collective-permute-start.1) | collective-permute-done | bytes 786464 | tf_op jit(solution)/shard_map/ppermute | solution.py:422
  76.7 0.9 copy-done.5
  77.6 0.0 copy-done
  77.6 5.0 %z_part.1 = (f32[3,1024,128]{2,1,0:T(8,128)}, f32[1,128]{1,0:T(1,128)S(1)}) custom-call(f32[2]{0:T(128)S(1)} %copy-done, f32[1,128]{1,0:T(1,128)S(1)} %copy-done.2, f32[3,1024,128]{2,1,0:T(8,128)} %get-tuple-element.15.part, bf16[3,1024,128]{2,1,0:T(8,128)(2,1)} %bitcast.13, s32[1024,128]{1,0:T(8,128)} %classes.1, bf16[3,1024,128]{2,1,0:T(8,128)(2,1)} %copy-done.3, ...), custom_call_target="tpu_custom_call" | custom-call | flops 13107200 | bytes 8388608 | tf_op jit(solution)/shard_map/z_part/pallas_call | solution.py:289
  82.7 0.0 all-to-all-done.1.drift
  82.7 3.3 %join.1 = (f32[3,1024,128]{2,1,0:T(8,128)S(1)}, f32[3,1024,128]{2,1,0:T(8,128)S(1)}, f32[8,1,128]{2,1,0:T(1,128)S(1)}) custom-call(f32[2]{0:T(128)S(1)} %copy-done, f32[1,128]{1,0:T(1,128)S(1)} %get-tuple-element.16.early, f32[3,1024,128]{2,1,0:T(8,128)} %get-tuple-element.17.part, bf16[3,1024,128]{2,1,0:T(8,128)(2,1)} %bitcast.14, s32[1024,128]{1,0:T(8,128)} %classes.1, ...), custom_call_target="tpu_custom_call" | custom-call | flops 13107200 | bytes 8388608 | tf_op jit(solution)/shard_map/join/pallas_call | solution.py:333
  85.9 14.6 %all_to_all.20.got = f32[8,1,128]{2,1,0:T(1,128)S(1)} all-to-all(f32[8,1,128]{2,1,0:T(1,128)S(1)} %get-tuple-element.19), channel_id=1, replica_groups=mesh['gz'=64,'gy'=8] {'gy'}, dimensions={0} | all-to-all | bytes 8192 | tf_op jit(solution)/shard_map/all_to_all | solution.py:397
  100.6 25.6 %all_to_all.21.got = f32[64,1,128]{2,1,0:T(1,128)S(1)} all-to-all(f32[64,1,128]{2,1,0:T(1,128)S(1)} %fold.1), channel_id=1, replica_groups=mesh['gz'=64,'gy'=8] {'gz'}, dimensions={0} | all-to-all | bytes 65536 | tf_op jit(solution)/shard_map/all_to_all | solution.py:397
  126.2 1.8 %finish.1 = (f32[3,1024,128]{2,1,0:T(8,128)}, f32[1,16]{1,0:T(1,128)}) custom-call(f32[64,1,128]{2,1,0:T(1,128)S(1)} %all_to_all.21.got, f32[3,1024,128]{2,1,0:T(8,128)S(1)} %get-tuple-element.20.adj, f32[3,1024,128]{2,1,0:T(8,128)S(1)} %get-tuple-element.21.rhs), custom_call_target="tpu_custom_call" | custom-call | flops 786432 | bytes 4718592 | tf_op jit(solution)/shard_map/finish/pallas_call | solution.py:384
  (6 shorter events, 0.0 us)
Async XLA Ops:
  3.1 10.5 %copy-start.4 = (bf16[3,1024,128]{2,1,0:T(8,128)(2,1)S(1)}, bf16[3,1024,128]{2,1,0:T(8,128)(2,1)}, u32[]{:S(2)}) copy-start(bf16[3,1024,128]{2,1,0:T(8,128)(2,1)} %get-tuple-element.13.lows) | copy-start | bytes 2359300
  3.1 37.0 %all-to-all-start = ((bf16[8,4,128,128]{3,2,1,0:T(8,128)(2,1)}), bf16[8,4,128,128]{3,2,1,0:T(8,128)(2,1)S(1)}, u32[]{:S(2)}, u32[]{:S(2)}) async-start(bf16[8,4,128,128]{3,2,1,0:T(8,128)(2,1)} %get-tuple-element.18), calls=%async_computation | async-start | bytes 2097152 | tf_op jit(solution)/shard_map/all_to_all | solution.py:397
  13.6 44.0 %collective-permute-start = (bf16[3,1024,128]{2,1,0:T(8,128)(2,1)S(1)}, bf16[3,1024,128]{2,1,0:T(8,128)(2,1)S(1)}, u32[]{:S(2)}, u32[]{:S(2)}) collective-permute-start(bf16[3,1024,128]{2,1,0:T(8,128)(2,1)S(1)} %copy-done.4), channel_id=1, source_target_pairs={{0,8},{8,0},{16,24},{24,16},{32,40},{40,32},{48,56},{56,48},{64,72... | collective-permute-start | bytes 2359304 | tf_op jit(solution)/shard_map/ppermute | solution.py:421
  40.0 0.7 copy-start.1
  44.0 33.6 %copy-start = (f32[2]{0:T(128)S(1)}, f32[2]{0:T(128)}, u32[]{:S(2)}) copy-start(f32[2]{0:T(128)} %pad_maximum_fusion.scal) | copy-start | bytes 28
  44.0 33.6 %copy-start.2 = (f32[1,128]{1,0:T(1,128)S(1)}, f32[1,128]{1,0:T(1,128)}, u32[]{:S(2)}) copy-start(f32[1,128]{1,0:T(1,128)} %get-tuple-element.14.early.after) | copy-start | bytes 1540
  44.0 38.6 %all-to-all-start.1 = ((bf16[8,3,128,128]{3,2,1,0:T(8,128)(2,1)}), bf16[8,3,128,128]{3,2,1,0:T(8,128)(2,1)S(1)}, u32[]{:S(2)}, u32[]{:S(2)}) async-start(bf16[8,3,128,128]{3,2,1,0:T(8,128)(2,1)} %y_part.1), calls=%async_computation.1 | async-start | bytes 1572864 | tf_op jit(solution)/shard_map/all_to_all | solution.py:397
  57.6 19.1 %copy-start.3 = (bf16[3,1024,128]{2,1,0:T(8,128)(2,1)}, bf16[3,1024,128]{2,1,0:T(8,128)(2,1)S(1)}, u32[]{:S(2)}) copy-start(bf16[3,1024,128]{2,1,0:T(8,128)(2,1)S(1)} %collective-permute-done.near) | copy-start | bytes 2359300
  57.6 19.1 %collective-permute-start.1 = (bf16[3,1024,128]{2,1,0:T(8,128)(2,1)S(1)}, bf16[3,1024,128]{2,1,0:T(8,128)(2,1)S(1)}, u32[]{:S(2)}, u32[]{:S(2)}) collective-permute-start(bf16[3,1024,128]{2,1,0:T(8,128)(2,1)S(1)} %collective-permute-done.near), channel_id=1, source_target_pairs={{0,16},{16,32},{32,48},{48,64},{64,80},{80,96},{96,112},{112,128},... | collective-permute-start | bytes 2359304 | tf_op jit(solution)/shard_map/ppermute | solution.py:422
  76.7 0.9 copy-start.5

commit v3 on v2

--- a/solution.py
+++ b/solution.py
@@ -56,6 +56,7 @@
 
 
 CHUNKS = 4
+GATE_FLOPS = 10**10
 
 
 def params(mib=VMEM_MIB, **more):
@@ -89,7 +90,7 @@
     return jnp.dot(a, b, preferred_element_type=f32)
 
 
-def pack_kernel(adj, wind, send, lows, adj_v, wind_v, send_v, lows_v, sem_in, sem_out):
+def pack_kernel(adj, wind, send, l0, l1, l2, adj_v, wind_v, send_v, lows_v, sem_in, sem_out):
     parts, _, rows, _ = send.shape
     per = parts // CHUNKS
     loads, stores = [], []
@@ -106,7 +107,8 @@
                 lows_v[c, at] = low
             send_v[s, 3] = wind_v[at]
         at, part = pl.ds(k * per * rows, per * rows), pl.ds(k * per, per)
-        stores += begin([(send_v.at[part], send.at[part]), (lows_v.at[:, at], lows.at[:, at])], sem_out, 2 * k)
+        stores += begin([(send_v.at[part], send.at[part])]
+                        + [(lows_v.at[c, at], low.at[at]) for c, low in enumerate((l0, l1, l2))], sem_out, 4 * k)
     finish_all(stores)
 
 
@@ -117,10 +119,10 @@
     return pl.pallas_call(
         pack_kernel,
         in_specs=[HBM, HBM],
-        out_specs=[HBM, HBM],
-        out_shape=[pltpu.HBM(sent, bf16), pltpu.HBM(kept, bf16)],
+        out_specs=[HBM] * 4,
+        out_shape=[pltpu.HBM(sent, bf16)] + [pltpu.HBM((nx, ny), bf16)] * 3,
         scratch_shapes=[pltpu.VMEM(kept, f32), pltpu.VMEM((nx, ny), bf16), pltpu.VMEM(sent, bf16), pltpu.VMEM(kept, bf16),
-                        pltpu.SemaphoreType.DMA((2 * CHUNKS,)), pltpu.SemaphoreType.DMA((2 * CHUNKS,))],
+                        pltpu.SemaphoreType.DMA((2 * CHUNKS,)), pltpu.SemaphoreType.DMA((4 * CHUNKS,))],
         compiler_params=params(),
         cost_estimate=pl.CostEstimate(flops=0, bytes_accessed=nx * ny * 32, transcendentals=0),
         name="pack",
@@ -141,14 +143,14 @@
     return jnp.sum(jnp.where(lane == row + offset, per, 0.0), axis=0, keepdims=True)
 
 
-def x_kernel(steps, count, scal, coef, fwd, inv, lows, adj, wind, cls_ref, rhs, sums, low, spec, acc, top):
+def x_kernel(steps, count, scal, coef, fwd, inv, l0, l1, l2, adj, wind, cls_ref, rhs, sums, low, spec, acc, top):
     i = pl.program_id(0)
-    ny = lows.shape[2]
+    ny = l0.shape[1]
 
     @pl.when(i == 0)
     def _():
-        for c in range(3):
-            low[:, c * ny:(c + 1) * ny] = lows[c]
+        for c, ref in enumerate((l0, l1, l2)):
+            low[:, c * ny:(c + 1) * ny] = ref[...]
         acc[...] = jnp.zeros_like(acc)
         top[...] = jnp.zeros_like(top)
 
@@ -196,18 +198,18 @@
         in_specs=[SMEM, SMEM,
                   pl.BlockSpec((TILE, nx), lambda i: (jnp.minimum(i, steps - 1), 0)),
                   pl.BlockSpec((1, 2 * TILE, nx), lambda i: (late(i), 0, 0))]
-        + [full((3, nx, ny))]
+        + [full((nx, ny))] * 3
         + [pl.BlockSpec((3, TILE, ny), lambda i: (0, late(i), 0)),
            pl.BlockSpec((3, TILE, ny), lambda i: (0, late(i), 0)),
            pl.BlockSpec((TILE, ny), lambda i: (late(i), 0))],
         out_specs=[pl.BlockSpec((3, TILE, ny), lambda i: (0, late(i), 0)), full((1, LANES))],
-        out_shape=[pltpu.HBM((3, nx, ny), f32), jax.ShapeDtypeStruct((1, LANES), f32)],
+        out_shape=[pltpu.HBM((3, nx, ny), f32), pltpu.HBM((1, LANES), f32)],
         scratch_shapes=[pltpu.VMEM((nx, 3 * ny), bf16), pltpu.VMEM((nx, 3 * ny), bf16),
                         pltpu.VMEM((count, 8, ny), f32), pltpu.VMEM((8, ny), f32)],
         compiler_params=params(60, dimension_semantics=("arbitrary",)),
         cost_estimate=pl.CostEstimate(flops=6 * nx * nx * 3 * ny, bytes_accessed=12 * 1024 * 1024, transcendentals=0),
         name="x_part",
-    )(scal, coef, fwd, inv, far_off(lows), adj, wind, classes)
+    )(scal, coef, fwd, inv, *[far_off(low) for low in lows], adj, wind, classes)
 
 
 def y_kernel(after, recv, table, out, plus, minus, table_v, out_v, sem_t, sem_o):
@@ -245,7 +247,7 @@
     dma = pltpu.SemaphoreType.DMA
     return pl.pallas_call(
         y_kernel,
-        in_specs=[SMALL, SMALL, HBM],
+        in_specs=[HBM, SMALL, HBM],
         out_specs=HBM,
         out_shape=pltpu.HBM(sent, bf16),
         scratch_shapes=[pltpu.VMEM((3 * rows, n // 2), bf16), pltpu.VMEM((3 * rows, n // 2), bf16),
@@ -253,61 +255,40 @@
         compiler_params=params(),
         cost_estimate=pl.CostEstimate(flops=2 * n * n * 3 * rows, bytes_accessed=4 * 1024 * 1024, transcendentals=0),
         name="y_part",
-    )(after, near_by(recv), far_off(table))
+    )(far_off(after), near_by(recv), far_off(table))
 
 
 def speed_of(w):
     return jnp.sqrt(w[0] * w[0] + w[1] * w[1] + w[2] * w[2])
 
 
-def z_kernel(count, scal, early, part, wind, cls_ref, near, far, rhs, sums, acc):
-    i = pl.program_id(0)
-
-    @pl.when(i == 0)
-    def _():
-        acc[...] = jnp.zeros_like(acc)
-
-    w = [wind[c].astype(f32) for c in range(3)]
-    slope = (0.5 * scal[1]) * w[2]
-    total = jnp.zeros_like(slope)
-    for c in range(3):
-        p, q = near[c].astype(f32), far[c].astype(f32)
-        r = part[c] + slope * (p - q) + viscosity * (p + q)
-        rhs[c] = r
-        total += r * w[c]
-    class_sums(scal[0] * speed_of(w) * total, cls_ref[...], acc, count)
-
-    @pl.when(i == pl.num_programs(0) - 1)
-    def _():
-        sums[...] = early[...] + to_lanes(acc, count, count)
-
-
-def z_part(scal, early, part, wind, classes, near, far, count):
-    _, nx, ny = part.shape
-    rows = nx // CHUNKS
-    three = pl.BlockSpec((3, rows, ny), lambda i: (0, i, 0))
-    return pl.pallas_call(
-        functools.partial(z_kernel, count),
-        grid=(CHUNKS,),
-        in_specs=[SMEM, full((1, LANES)), three, three, pl.BlockSpec((rows, ny), lambda i: (i, 0)), three, three],
-        out_specs=[three, full((1, LANES))],
-        out_shape=[pltpu.HBM((3, nx, ny), f32), jax.ShapeDtypeStruct((1, LANES), f32)],
-        scratch_shapes=[pltpu.VMEM((count, 8, ny), f32)],
-        compiler_params=params(dimension_semantics=("arbitrary",)),
-        cost_estimate=pl.CostEstimate(flops=100 * nx * ny, bytes_accessed=8 * 1024 * 1024, transcendentals=0),
-        name="z_part",
-    )(scal, early, far_off(part), far_off(wind), far_off(classes), far_off(near), far_off(far))
-
-
-def join_kernel(count, scal, early, part, wind, classes, adj, drift, rhs, adj_v, sums,
-                part_v, wind_v, cls_v, acc, sem_in, sem_adj):
+def gate_kernel(early, q0, q1, q2, out):
+    out[...] = early[...]
+
+
+def gate(early, far):
+    return pl.pallas_call(
+        gate_kernel,
+        in_specs=[SMALL, HBM, HBM, HBM],
+        out_specs=SMALL,
+        out_shape=jax.ShapeDtypeStruct(early.shape, f32),
+        compiler_params=params(4),
+        cost_estimate=pl.CostEstimate(flops=GATE_FLOPS, bytes_accessed=1024, transcendentals=0),
+        name="gate",
+    )(early, *[far_off(q) for q in far])
+
+
+def join_kernel(count, scal, early, part, wind, classes, adj, p0, p1, p2, q0, q1, q2, drift, rhs, adj_v, sums,
+                part_v, wind_v, cls_v, near_v, far_v, acc, sem_in, sem_adj):
     parts, _, rows, _ = drift.shape
     per = parts // CHUNKS
     loads = []
     for k in range(CHUNKS):
         at = pl.ds(k * per * rows, per * rows)
         loads.append(begin([(wind.at[:, at], wind_v.at[:, at]), (classes.at[at], cls_v.at[at]),
-                            (part.at[:, at], part_v.at[:, at])], sem_in, 3 * k))
+                            (part.at[:, at], part_v.at[:, at])]
+                           + [(p.at[at], near_v.at[c, at]) for c, p in enumerate((p0, p1, p2))]
+                           + [(q.at[at], far_v.at[c, at]) for c, q in enumerate((q0, q1, q2))], sem_in, 9 * k))
     kept = begin([(adj, adj_v)], sem_adj)
     acc[...] = jnp.zeros_like(acc)
     for k in range(CHUNKS):
@@ -315,32 +296,37 @@
         for s in range(k * per, (k + 1) * per):
             at = slice(s * rows, (s + 1) * rows)
             w = [wind_v[c, at].astype(f32) for c in range(3)]
-            total = jnp.zeros_like(w[0])
+            slope = (0.5 * scal[1]) * w[2]
+            up, down = viscosity + slope, viscosity - slope
+            total = jnp.zeros_like(slope)
             for c in range(3):
-                d = drift[s, c].astype(f32)
-                rhs[c, at] = part_v[c, at] + d
-                total += d * w[c]
+                r = part_v[c, at] + drift[s, c].astype(f32)
+                r += up * near_v[c, at].astype(f32) + down * far_v[c, at].astype(f32)
+                rhs[c, at] = r
+                total += r * w[c]
             class_sums(scal[0] * speed_of(w) * total, cls_v[at], acc, count)
     sums[...] = jnp.broadcast_to((early[...] + to_lanes(acc, count, count))[None], sums.shape)
     finish_all(kept)
 
 
-def join(scal, early, part, wind, classes, adj, drift, count):
+def join(scal, early, part, wind, classes, adj, near, far, drift, count):
     parts, _, rows, ny = drift.shape
     nx = parts * rows
     whole = (3, nx, ny)
     dma = pltpu.SemaphoreType.DMA
     return pl.pallas_call(
         functools.partial(join_kernel, count),
-        in_specs=[SMEM, SMALL, HBM, HBM, HBM, HBM, SMALL],
+        in_specs=[SMEM, SMALL] + [HBM] * 10 + [SMALL],
         out_specs=[SMALL, SMALL, SMALL],
         out_shape=[pltpu.VMEM(whole, f32), pltpu.VMEM(whole, f32), jax.ShapeDtypeStruct((parts, 1, LANES), f32)],
         scratch_shapes=[pltpu.VMEM(whole, f32), pltpu.VMEM(whole, bf16), pltpu.VMEM((nx, ny), jnp.int32),
-                        pltpu.VMEM((count, 8, ny), f32), dma((3 * CHUNKS,)), dma((1,))],
+                        pltpu.VMEM(whole, bf16), pltpu.VMEM(whole, bf16),
+                        pltpu.VMEM((count, 8, ny), f32), dma((9 * CHUNKS,)), dma((1,))],
         compiler_params=params(),
         cost_estimate=pl.CostEstimate(flops=100 * nx * ny, bytes_accessed=8 * 1024 * 1024, transcendentals=0),
         name="join",
-    )(scal, early, far_off(part), far_off(wind), far_off(classes), far_off(adj), near_by(drift))
+    )(scal, early, far_off(part), far_off(wind), far_off(classes), far_off(adj),
+      *[far_off(a) for a in near + far], near_by(drift))
 
 
 def merge(rows, count):
@@ -413,18 +399,17 @@
     sign = jnp.where(me % 2 == 0, 1.0, -1.0).astype(f32)
     scal = jnp.stack([height, sign])
 
-    send, lows = pack(adj, wnd, gy)
+    send, *lows = pack(adj, wnd, gy)
     recv = swap(send, "gy")
 
     pair = [(i, i ^ 1) for i in range(gz)]
     onward = [(i, i + 2) for i in range(0, gz - 2, 2)] + [(i, i - 2) for i in range(3, gz, 2)]
-    near = lax.ppermute(lows, "gz", pair)
-    far = lax.ppermute(near, "gz", onward)
+    near = [lax.ppermute(low, "gz", pair) for low in lows]
+    far = [lax.ppermute(low, "gz", onward) for low in near]
 
     part, early = x_part(scal, drag_coef, jnp.asarray(fx), jnp.asarray(inv_x), lows, adj, wnd, classes)
     drift = swap(y_part(early, recv, jnp.asarray(line_tables(total_y))), "gy")
-    part, early = z_part(scal, early, part, wnd, classes, near, far, count)
-    rhs, adj, sums = join(scal, early, part, wnd, classes, adj, drift, count)
+    rhs, adj, sums = join(scal, gate(early, far), part, wnd, classes, adj, near, far, drift, count)
 
     got = swap(fold(swap(sums, "gy"), gz, count), "gz")
     scale = 1.0 / math.sqrt(nx * total_y * gz / count)

time: 129 us -> 116 us (0.90)
  waiting for transfers between devices: 38.3 us -> 24 us
  starting transfers between devices: 20 us -> 31.2 us
  blocking collectives: 40.2 us -> 35.5 us
  Pallas kernels: 26.6 us -> 22.3 us
    ppermute x2 -> x6, waiting for transfers between devices: 25 us -> 10.9 us  [the longest x3 7.51 us: local(): far = [lax.ppermute(low, 'gz', onward) for low in near]]
    ppermute x2 -> x6, starting transfers between devices: 4.99 us -> 16.1 us  [the longest x3 8.95 us: local(): far = [lax.ppermute(low, 'gz', onward) for low in near]]
    pallas_call x3, Pallas kernels: 10.8 us -> 5.8 us  [the longest x1 3.29 us: y_part(): pl.pallas_call(y_kernel, in_specs=[HBM, SMALL, HBM], out_specs=HBM, out_s...]
    all_to_all x2, blocking collectives: 40.2 us -> 35.5 us  [swap(): return lax.all_to_all(x, axes, split_axis=0, concat_axis=0, tiled=True)]
  transfers between devices with their start and end apart: 4 -> 8, of which waited for: 3 -> 5; matrix products, arithmetic and copies ran while one was open for 0% -> 1% of each run, Pallas kernels for 15% -> 12%
where the time goes in v3:
time: 116 us; the launch traced here: 115 us
  blocking collectives  35.5 us (31%)
  starting transfers between devices  31.2 us (27%)
  waiting for transfers between devices  24 us (21%)
  Pallas kernels  22.3 us (19%)
    all_to_all x2, blocking collectives, swap(): return lax.all_to_all(x, axes, split_axis=0, concat_axis=0, tiled=True)  35.5 us
    all_to_all x2, starting transfers between devices, swap(): return lax.all_to_all(x, axes, split_axis=0, concat_axis=0, tiled=True)  15 us
    all_to_all x2, waiting for transfers between devices, swap(): return lax.all_to_all(x, axes, split_axis=0, concat_axis=0, tiled=True)  13.1 us
    pallas_call x1, Pallas kernels, x_part(): pl.pallas_call(functools.partial(x_kernel, steps, count), grid=(2 * steps...  10.7 us
    ppermute x3, starting transfers between devices, local(): far = [lax.ppermute(low, 'gz', onward) for low in near]  8.95 us
    ppermute x3, waiting for transfers between devices, local(): far = [lax.ppermute(low, 'gz', onward) for low in near]  7.51 us
    ppermute x3, starting transfers between devices, local(): near = [lax.ppermute(low, 'gz', pair) for low in lows]  7.19 us
    pallas_call x1, Pallas kernels, join(): pl.pallas_call(functools.partial(join_kernel, count), in_specs=[SMEM, SMA...  3.98 us
  transfers between devices with their start and end apart: 8, of which 5 were waited for; matrix products, arithmetic and copies ran while one was open for 1% of the time, Pallas kernels for 12%

profile of v3, /device:TPU:1, one launch (start us, length us, event | category | flops | bytes accessed | tf_op | source)
XLA Modules:
  0.0 115.2 jit_solution(12879276856936938343)
XLA Ops:
  0.6 2.5 %pack.1 = (bf16[8,4,128,128]{3,2,1,0:T(8,128)(2,1)}, bf16[1024,128]{1,0:T(8,128)(2,1)}, bf16[1024,128]{1,0:T(8,128)(2,1)}, bf16[1024,128]{1,0:T(8,128)(2,1)}) custom-call(f32[3,1024,128]{2,1,0:T(8,128)} %bitcast.8, bf16[3,1024,128]{2,1,0:T(8,128)(2,1)} %bitcast.11), custom_call_target="tpu_custom_call" | custom-call | bytes 4194304 | tf_op jit(solution)/shard_map/pack/pallas_call | solution.py:119
  3.2 10.5 %all-to-all-start = ((bf16[8,4,128,128]{3,2,1,0:T(8,128)(2,1)}), bf16[8,4,128,128]{3,2,1,0:T(8,128)(2,1)S(1)}, u32[]{:S(2)}, u32[]{:S(2)}) async-start(bf16[8,4,128,128]{3,2,1,0:T(8,128)(2,1)} %get-tuple-element.18), calls=%async_computation | async-start | bytes 2097152 | tf_op jit(solution)/shard_map/all_to_all | solution.py:383
  13.7 1.9 %collective-permute-start = (bf16[1024,128]{1,0:T(8,128)(2,1)S(1)}, bf16[1024,128]{1,0:T(8,128)(2,1)S(1)}, u32[]{:S(2)}, u32[]{:S(2)}) collective-permute-start(bf16[1024,128]{1,0:T(8,128)(2,1)S(1)} %copy-done.7), channel_id=1, source_target_pairs={{0,8},{8,0},{16,24},{24,16},{32,40},{40,32},{48,56},{56,48},{64,72... | collective-permute-start | bytes 786440 | tf_op jit(solution)/shard_map/ppermute | solution.py:407
  15.6 3.4 %collective-permute-start.2 = (bf16[1024,128]{1,0:T(8,128)(2,1)S(1)}, bf16[1024,128]{1,0:T(8,128)(2,1)S(1)}, u32[]{:S(2)}, u32[]{:S(2)}) collective-permute-start(bf16[1024,128]{1,0:T(8,128)(2,1)S(1)} %copy-done.6), channel_id=1, source_target_pairs={{0,8},{8,0},{16,24},{24,16},{32,40},{40,32},{48,56},{56,48},{64,72... | collective-permute-start | bytes 786440 | tf_op jit(solution)/shard_map/ppermute | solution.py:407
  19.0 1.9 %collective-permute-start.4 = (bf16[1024,128]{1,0:T(8,128)(2,1)S(1)}, bf16[1024,128]{1,0:T(8,128)(2,1)S(1)}, u32[]{:S(2)}, u32[]{:S(2)}) collective-permute-start(bf16[1024,128]{1,0:T(8,128)(2,1)S(1)} %copy-done.5), channel_id=1, source_target_pairs={{0,8},{8,0},{16,24},{24,16},{32,40},{40,32},{48,56},{56,48},{64,72... | collective-permute-start | bytes 786440 | tf_op jit(solution)/shard_map/ppermute | solution.py:407
  21.0 0.6 pad_maximum_fusion.scal
  21.5 10.7 %x_part.1 = (f32[3,1024,128]{2,1,0:T(8,128)}, f32[1,128]{1,0:T(1,128)}) custom-call(f32[2]{0:T(128)} %pad_maximum_fusion.scal, f32[16]{0:T(128)} %coef.1, bf16[1024,1024]{1,0:T(8,128)(2,1)} %constant.37.clone.fwd, bf16[4,512,1024]{2,1,0:T(8,128)(2,1)} %constant.38.clone.inv, bf16[1024,128]{1,0:T(8,128)(2,1)} %get-tuple-element.13.l0, ...), custom_call_target="tpu_custom_call" | custom-call | flops 2415919104 | bytes 12582912 | tf_op jit(solution)/shard_map/x_part/pallas_call | solution.py:195
  32.2 7.9 %all-to-all-done.recv = bf16[8,4,128,128]{3,2,1,0:T(8,128)(2,1)S(1)} async-done(((bf16[8,4,128,128]{3,2,1,0:T(8,128)(2,1)}), bf16[8,4,128,128]{3,2,1,0:T(8,128)(2,1)S(1)}, u32[]{:S(2)}, u32[]{:S(2)}) %all-to-all-start) | async-done | bytes 1048608 | tf_op jit(solution)/shard_map/all_to_all | solution.py:383
  40.1 3.3 %y_part.1 = bf16[8,3,128,128]{3,2,1,0:T(8,128)(2,1)} custom-call(f32[1,128]{1,0:T(1,128)} %get-tuple-element.16.early.after, bf16[8,4,128,128]{3,2,1,0:T(8,128)(2,1)S(1)} %all-to-all-done.recv, bf16[2,4,512,256]{3,2,1,0:T(8,128)(2,1)} %constant.39.clone.table), custom_call_target="tpu_custom_call" | custom-call | flops 805306368 | bytes 4194304 | tf_op jit(solution)/shard_map/y_part/pallas_call | solution.py:248
  43.4 0.0 copy-start.1
  43.5 4.5 %all-to-all-start.1 = ((bf16[8,3,128,128]{3,2,1,0:T(8,128)(2,1)}), bf16[8,3,128,128]{3,2,1,0:T(8,128)(2,1)S(1)}, u32[]{:S(2)}, u32[]{:S(2)}) async-start(bf16[8,3,128,128]{3,2,1,0:T(8,128)(2,1)} %y_part.1), calls=%async_computation.1 | async-start | bytes 1572864 | tf_op jit(solution)/shard_map/all_to_all | solution.py:383
  48.0 0.0 collective-permute-done.p0
  48.0 3.1 %collective-permute-start.1 = (bf16[1024,128]{1,0:T(8,128)(2,1)S(1)}, bf16[1024,128]{1,0:T(8,128)(2,1)S(1)}, u32[]{:S(2)}, u32[]{:S(2)}) collective-permute-start(bf16[1024,128]{1,0:T(8,128)(2,1)S(1)} %collective-permute-done.p0), channel_id=1, source_target_pairs={{0,16},{16,32},{32,48},{48,64},{64,80},{80,96},{96,112},{112,128},... | collective-permute-start | bytes 786440 | tf_op jit(solution)/shard_map/ppermute | solution.py:408
  51.2 3.1 %collective-permute-start.3 = (bf16[1024,128]{1,0:T(8,128)(2,1)S(1)}, bf16[1024,128]{1,0:T(8,128)(2,1)S(1)}, u32[]{:S(2)}, u32[]{:S(2)}) collective-permute-start(bf16[1024,128]{1,0:T(8,128)(2,1)S(1)} %collective-permute-done.2.p1), channel_id=1, source_target_pairs={{0,16},{16,32},{32,48},{48,64},{64,80},{80,96},{96,112},{112,128},... | collective-permute-start | bytes 786440 | tf_op jit(solution)/shard_map/ppermute | solution.py:408
  54.3 3.4 %collective-permute-done.4.p2 = bf16[1024,128]{1,0:T(8,128)(2,1)S(1)} collective-permute-done((bf16[1024,128]{1,0:T(8,128)(2,1)S(1)}, bf16[1024,128]{1,0:T(8,128)(2,1)S(1)}, u32[]{:S(2)}, u32[]{:S(2)}) %collective-permute-start.4) | collective-permute-done | bytes 262176 | tf_op jit(solution)/shard_map/ppermute | solution.py:407
  57.7 2.7 %collective-permute-start.5 = (bf16[1024,128]{1,0:T(8,128)(2,1)S(1)}, bf16[1024,128]{1,0:T(8,128)(2,1)S(1)}, u32[]{:S(2)}, u32[]{:S(2)}) collective-permute-start(bf16[1024,128]{1,0:T(8,128)(2,1)S(1)} %collective-permute-done.4.p2), channel_id=1, source_target_pairs={{0,16},{16,32},{32,48},{48,64},{64,80},{80,96},{96,112},{112,128},... | collective-permute-start | bytes 786440 | tf_op jit(solution)/shard_map/ppermute | solution.py:408
  60.4 1.9 %collective-permute-done.3.q1 = bf16[1024,128]{1,0:T(8,128)(2,1)S(1)} collective-permute-done((bf16[1024,128]{1,0:T(8,128)(2,1)S(1)}, bf16[1024,128]{1,0:T(8,128)(2,1)S(1)}, u32[]{:S(2)}, u32[]{:S(2)}) %collective-permute-start.3) | collective-permute-done | bytes 262176 | tf_op jit(solution)/shard_map/ppermute | solution.py:408
  62.3 5.6 %collective-permute-done.5.q2 = bf16[1024,128]{1,0:T(8,128)(2,1)S(1)} collective-permute-done((bf16[1024,128]{1,0:T(8,128)(2,1)S(1)}, bf16[1024,128]{1,0:T(8,128)(2,1)S(1)}, u32[]{:S(2)}, u32[]{:S(2)}) %collective-permute-start.5) | collective-permute-done | bytes 262176 | tf_op jit(solution)/shard_map/ppermute | solution.py:408
  67.9 0.7 copy-done.10
  68.6 5.2 %all-to-all-done.1.drift = bf16[8,3,128,128]{3,2,1,0:T(8,128)(2,1)S(1)} async-done(((bf16[8,3,128,128]{3,2,1,0:T(8,128)(2,1)}), bf16[8,3,128,128]{3,2,1,0:T(8,128)(2,1)S(1)}, u32[]{:S(2)}, u32[]{:S(2)}) %all-to-all-start.1) | async-done | bytes 786464 | tf_op jit(solution)/shard_map/all_to_all | solution.py:383
  73.8 4.0 %join.1 = (f32[3,1024,128]{2,1,0:T(8,128)S(1)}, f32[3,1024,128]{2,1,0:T(8,128)S(1)}, f32[8,1,128]{2,1,0:T(1,128)S(1)}) custom-call(f32[2]{0:T(128)S(1)} %copy-done, f32[1,128]{1,0:T(1,128)S(1)} %gate.1.early, f32[3,1024,128]{2,1,0:T(8,128)} %get-tuple-element.17.part, bf16[3,1024,128]{2,1,0:T(8,128)(2,1)} %bitcast.13, s32[1024,128]{1,0:T(8,128)} %classes.1, ...), custom_call_target="tpu_custom_call" | custom-call | flops 13107200 | bytes 8388608 | tf_op jit(solution)/shard_map/join/pallas_call | solution.py:317
  77.8 11.0 %all_to_all.20.got = f32[8,1,128]{2,1,0:T(1,128)S(1)} all-to-all(f32[8,1,128]{2,1,0:T(1,128)S(1)} %get-tuple-element.19), channel_id=1, replica_groups=mesh['gz'=64,'gy'=8] {'gy'}, dimensions={0} | all-to-all | bytes 8192 | tf_op jit(solution)/shard_map/all_to_all | solution.py:383
  88.9 24.4 %all_to_all.21.got = f32[64,1,128]{2,1,0:T(1,128)S(1)} all-to-all(f32[64,1,128]{2,1,0:T(1,128)S(1)} %fold.1), channel_id=1, replica_groups=mesh['gz'=64,'gy'=8] {'gz'}, dimensions={0} | all-to-all | bytes 65536 | tf_op jit(solution)/shard_map/all_to_all | solution.py:383
  113.3 1.8 %finish.1 = (f32[3,1024,128]{2,1,0:T(8,128)}, f32[1,16]{1,0:T(1,128)}) custom-call(f32[64,1,128]{2,1,0:T(1,128)S(1)} %all_to_all.21.got, f32[3,1024,128]{2,1,0:T(8,128)S(1)} %get-tuple-element.20.adj, f32[3,1024,128]{2,1,0:T(8,128)S(1)} %get-tuple-element.21.rhs), custom_call_target="tpu_custom_call" | custom-call | flops 786432 | bytes 4718592 | tf_op jit(solution)/shard_map/finish/pallas_call | solution.py:370
  (24 shorter events, 0.1 us)
Async XLA Ops:
  3.1 10.5 %copy-start.7 = (bf16[1024,128]{1,0:T(8,128)(2,1)S(1)}, bf16[1024,128]{1,0:T(8,128)(2,1)}, u32[]{:S(2)}) copy-start(bf16[1024,128]{1,0:T(8,128)(2,1)} %get-tuple-element.13.l0) | copy-start | bytes 786436
  3.2 12.4 %copy-start.6 = (bf16[1024,128]{1,0:T(8,128)(2,1)S(1)}, bf16[1024,128]{1,0:T(8,128)(2,1)}, u32[]{:S(2)}) copy-start(bf16[1024,128]{1,0:T(8,128)(2,1)} %get-tuple-element.14.l1) | copy-start | bytes 786436
  3.2 15.8 %copy-start.5 = (bf16[1024,128]{1,0:T(8,128)(2,1)S(1)}, bf16[1024,128]{1,0:T(8,128)(2,1)}, u32[]{:S(2)}) copy-start(bf16[1024,128]{1,0:T(8,128)(2,1)} %get-tuple-element.15.l2) | copy-start | bytes 786436
  3.2 37.0 %all-to-all-start = ((bf16[8,4,128,128]{3,2,1,0:T(8,128)(2,1)}), bf16[8,4,128,128]{3,2,1,0:T(8,128)(2,1)S(1)}, u32[]{:S(2)}, u32[]{:S(2)}) async-start(bf16[8,4,128,128]{3,2,1,0:T(8,128)(2,1)} %get-tuple-element.18), calls=%async_computation | async-start | bytes 2097152 | tf_op jit(solution)/shard_map/all_to_all | solution.py:383
  13.7 34.3 %collective-permute-start = (bf16[1024,128]{1,0:T(8,128)(2,1)S(1)}, bf16[1024,128]{1,0:T(8,128)(2,1)S(1)}, u32[]{:S(2)}, u32[]{:S(2)}) collective-permute-start(bf16[1024,128]{1,0:T(8,128)(2,1)S(1)} %copy-done.7), channel_id=1, source_target_pairs={{0,8},{8,0},{16,24},{24,16},{32,40},{40,32},{48,56},{56,48},{64,72... | collective-permute-start | bytes 786440 | tf_op jit(solution)/shard_map/ppermute | solution.py:407
  15.6 35.6 %collective-permute-start.2 = (bf16[1024,128]{1,0:T(8,128)(2,1)S(1)}, bf16[1024,128]{1,0:T(8,128)(2,1)S(1)}, u32[]{:S(2)}, u32[]{:S(2)}) collective-permute-start(bf16[1024,128]{1,0:T(8,128)(2,1)S(1)} %copy-done.6), channel_id=1, source_target_pairs={{0,8},{8,0},{16,24},{24,16},{32,40},{40,32},{48,56},{56,48},{64,72... | collective-permute-start | bytes 786440 | tf_op jit(solution)/shard_map/ppermute | solution.py:407
  19.0 38.7 %collective-permute-start.4 = (bf16[1024,128]{1,0:T(8,128)(2,1)S(1)}, bf16[1024,128]{1,0:T(8,128)(2,1)S(1)}, u32[]{:S(2)}, u32[]{:S(2)}) collective-permute-start(bf16[1024,128]{1,0:T(8,128)(2,1)S(1)} %copy-done.5), channel_id=1, source_target_pairs={{0,8},{8,0},{16,24},{24,16},{32,40},{40,32},{48,56},{56,48},{64,72... | collective-permute-start | bytes 786440 | tf_op jit(solution)/shard_map/ppermute | solution.py:407
  43.4 25.2 %copy-start.1 = (f32[1,128]{1,0:T(1,128)S(1)}, f32[1,128]{1,0:T(1,128)}, u32[]{:S(2)}) copy-start(f32[1,128]{1,0:T(1,128)} %get-tuple-element.16.early.after) | copy-start | bytes 1540
  43.5 30.4 %all-to-all-start.1 = ((bf16[8,3,128,128]{3,2,1,0:T(8,128)(2,1)}), bf16[8,3,128,128]{3,2,1,0:T(8,128)(2,1)S(1)}, u32[]{:S(2)}, u32[]{:S(2)}) async-start(bf16[8,3,128,128]{3,2,1,0:T(8,128)(2,1)} %y_part.1), calls=%async_computation.1 | async-start | bytes 1572864 | tf_op jit(solution)/shard_map/all_to_all | solution.py:383
  48.0 25.9 %copy-start = (f32[2]{0:T(128)S(1)}, f32[2]{0:T(128)}, u32[]{:S(2)}) copy-start(f32[2]{0:T(128)} %pad_maximum_fusion.scal) | copy-start | bytes 28
  48.0 20.6 %copy-start.2 = (bf16[1024,128]{1,0:T(8,128)(2,1)}, bf16[1024,128]{1,0:T(8,128)(2,1)S(1)}, u32[]{:S(2)}) copy-start(bf16[1024,128]{1,0:T(8,128)(2,1)S(1)} %collective-permute-done.p0) | copy-start | bytes 786436
  48.0 12.4 %collective-permute-start.1 = (bf16[1024,128]{1,0:T(8,128)(2,1)S(1)}, bf16[1024,128]{1,0:T(8,128)(2,1)S(1)}, u32[]{:S(2)}, u32[]{:S(2)}) collective-permute-start(bf16[1024,128]{1,0:T(8,128)(2,1)S(1)} %collective-permute-done.p0), channel_id=1, source_target_pairs={{0,16},{16,32},{32,48},{48,64},{64,80},{80,96},{96,112},{112,128},... | collective-permute-start | bytes 786440 | tf_op jit(solution)/shard_map/ppermute | solution.py:408
  51.1 17.5 %copy-start.3 = (bf16[1024,128]{1,0:T(8,128)(2,1)}, bf16[1024,128]{1,0:T(8,128)(2,1)S(1)}, u32[]{:S(2)}) copy-start(bf16[1024,128]{1,0:T(8,128)(2,1)S(1)} %collective-permute-done.2.p1) | copy-start | bytes 786436
  51.2 11.1 %collective-permute-start.3 = (bf16[1024,128]{1,0:T(8,128)(2,1)S(1)}, bf16[1024,128]{1,0:T(8,128)(2,1)S(1)}, u32[]{:S(2)}, u32[]{:S(2)}) collective-permute-start(bf16[1024,128]{1,0:T(8,128)(2,1)S(1)} %collective-permute-done.2.p1), channel_id=1, source_target_pairs={{0,16},{16,32},{32,48},{48,64},{64,80},{80,96},{96,112},{112,128},... | collective-permute-start | bytes 786440 | tf_op jit(solution)/shard_map/ppermute | solution.py:408
  57.7 11.0 %copy-start.4 = (bf16[1024,128]{1,0:T(8,128)(2,1)}, bf16[1024,128]{1,0:T(8,128)(2,1)S(1)}, u32[]{:S(2)}) copy-start(bf16[1024,128]{1,0:T(8,128)(2,1)S(1)} %collective-permute-done.4.p2) | copy-start | bytes 786436
  57.7 10.2 %collective-permute-start.5 = (bf16[1024,128]{1,0:T(8,128)(2,1)S(1)}, bf16[1024,128]{1,0:T(8,128)(2,1)S(1)}, u32[]{:S(2)}, u32[]{:S(2)}) collective-permute-start(bf16[1024,128]{1,0:T(8,128)(2,1)S(1)} %collective-permute-done.4.p2), channel_id=1, source_target_pairs={{0,16},{16,32},{32,48},{48,64},{64,80},{80,96},{96,112},{112,128},... | collective-permute-start | bytes 786440 | tf_op jit(solution)/shard_map/ppermute | solution.py:408
  60.4 7.5 %copy-start.8 = (bf16[1024,128]{1,0:T(8,128)(2,1)}, bf16[1024,128]{1,0:T(8,128)(2,1)S(1)}, u32[]{:S(2)}) copy-start(bf16[1024,128]{1,0:T(8,128)(2,1)S(1)} %collective-permute-done.1.q0) | copy-start | bytes 786436
  62.3 5.6 %copy-start.9 = (bf16[1024,128]{1,0:T(8,128)(2,1)}, bf16[1024,128]{1,0:T(8,128)(2,1)S(1)}, u32[]{:S(2)}) copy-start(bf16[1024,128]{1,0:T(8,128)(2,1)S(1)} %collective-permute-done.3.q1) | copy-start | bytes 786436
  67.9 0.7 copy-start.10

commit v4 on v3

--- a/solution.py
+++ b/solution.py
@@ -129,6 +129,10 @@
     )(far_off(adj), far_off(wind))
 
 
+def speed_of(w):
+    return jnp.sqrt(w[0] * w[0] + w[1] * w[1] + w[2] * w[2])
+
+
 def class_sums(column, cls, acc, count):
     for k in range(count):
         kept = jnp.where(cls == k, column, 0.0)
@@ -143,28 +147,30 @@
     return jnp.sum(jnp.where(lane == row + offset, per, 0.0), axis=0, keepdims=True)
 
 
-def x_kernel(steps, count, scal, coef, fwd, inv, l0, l1, l2, adj, wind, cls_ref, rhs, sums, low, spec, acc, top):
-    i = pl.program_id(0)
-    ny = l0.shape[1]
-
-    @pl.when(i == 0)
-    def _():
-        for c, ref in enumerate((l0, l1, l2)):
-            low[:, c * ny:(c + 1) * ny] = ref[...]
-        acc[...] = jnp.zeros_like(acc)
-        top[...] = jnp.zeros_like(top)
-
-    @pl.when(i < steps)
-    def _():
-        spec[pl.ds(pl.multiple_of(i * TILE, TILE), TILE), :] = dot(fwd[...], low[...]).astype(bf16)
-
-    @pl.when(i >= steps)
-    def _():
-        dx = dot(inv[0, :TILE], spec[...])
-        dxx = dot(inv[0, TILE:], spec[...])
-        cls = cls_ref[...]
-        w = [wind[c].astype(f32) for c in range(3)]
-        speed = jnp.sqrt(w[0] * w[0] + w[1] * w[1] + w[2] * w[2])
+def x_kernel(count, scal, coef, fwd, inv, l0, l1, l2, adj, wind, classes, rhs, sums,
+             low, spec, fwd_v, inv_v, adj_v, wind_v, cls_v, rhs_v, acc, top, sem_l, sem_f, sem_i, sem_o):
+    nx, ny = l0.shape
+    steps = nx // TILE
+    ats = [pl.ds(t * TILE, TILE) for t in range(steps)]
+    lines = begin([(ref, low.at[:, pl.ds(c * ny, ny)]) for c, ref in enumerate((l0, l1, l2))], sem_l)
+    tiles = begin([(fwd.at[at], fwd_v.at[at]) for at in ats], sem_f)
+    loads = [begin([(inv.at[t], inv_v.at[t]), (adj.at[:, at], adj_v.at[:, at]), (wind.at[:, at], wind_v.at[:, at]),
+                    (classes.at[at], cls_v.at[at])], sem_i, 4 * t) for t, at in enumerate(ats)]
+    acc[...] = jnp.zeros_like(acc)
+    top[...] = jnp.zeros_like(top)
+    finish_all(lines)
+    for t in range(0, steps, 2):
+        finish_all(tiles[t:t + 2])
+        at = slice(t * TILE, (t + 2) * TILE)
+        spec[at] = dot(fwd_v[at], low[...]).astype(bf16)
+    stores = []
+    for t, at in enumerate(ats):
+        finish_all(loads[t])
+        both = dot(inv_v[t], spec[...])
+        dx, dxx = both[:TILE], both[TILE:]
+        cls = cls_v[at]
+        w = [wind_v[c, at].astype(f32) for c in range(3)]
+        speed = speed_of(w)
         weight = scal[0] * speed
         drag = jnp.zeros_like(speed)
         for k in range(count):
@@ -172,44 +178,40 @@
         damp = drag * weight + 2.0 * viscosity
         total = jnp.zeros_like(speed)
         for c in range(3):
-            a = adj[c]
+            a = adj_v[c, at]
             total += a * w[c]
             cols = slice(c * ny, (c + 1) * ny)
-            rhs[c] = w[0] * dx[:, cols] + viscosity * dxx[:, cols] - damp * a
+            rhs_v[c, at] = w[0] * dx[:, cols] + viscosity * dxx[:, cols] - damp * a
+        stores += begin([(rhs_v.at[:, at], rhs.at[:, at])], sem_o, t)
         class_sums(weight * total, cls, acc, count)
         size = jnp.abs(w[0]) + jnp.abs(w[1]) + jnp.abs(w[2])
         top[...] = jnp.maximum(top[...], jnp.max(size.reshape(-1, 8, ny), axis=0))
-
-    @pl.when(i == pl.num_programs(0) - 1)
-    def _():
-        lane = lax.broadcasted_iota(jnp.int32, (1, LANES), 1)
-        peak = jnp.max(jnp.max(top[...], axis=0, keepdims=True), axis=1, keepdims=True)
-        sums[...] = jnp.where(lane == 2 * count, peak, to_lanes(acc, count, 0))
+    lane = lax.broadcasted_iota(jnp.int32, (1, LANES), 1)
+    peak = jnp.max(jnp.max(top[...], axis=0, keepdims=True), axis=1, keepdims=True)
+    sums[...] = jnp.where(lane == 2 * count, peak, to_lanes(acc, count, 0))
+    finish_all(stores)
 
 
 def x_part(scal, coef, fwd, inv, lows, adj, wind, classes):
     _, nx, ny = adj.shape
     count = coef.shape[0]
     steps = nx // TILE
-    late = lambda i: jnp.maximum(i - steps, 0)
-    return pl.pallas_call(
-        functools.partial(x_kernel, steps, count),
-        grid=(2 * steps,),
-        in_specs=[SMEM, SMEM,
-                  pl.BlockSpec((TILE, nx), lambda i: (jnp.minimum(i, steps - 1), 0)),
-                  pl.BlockSpec((1, 2 * TILE, nx), lambda i: (late(i), 0, 0))]
-        + [full((nx, ny))] * 3
-        + [pl.BlockSpec((3, TILE, ny), lambda i: (0, late(i), 0)),
-           pl.BlockSpec((3, TILE, ny), lambda i: (0, late(i), 0)),
-           pl.BlockSpec((TILE, ny), lambda i: (late(i), 0))],
-        out_specs=[pl.BlockSpec((3, TILE, ny), lambda i: (0, late(i), 0)), full((1, LANES))],
-        out_shape=[pltpu.HBM((3, nx, ny), f32), pltpu.HBM((1, LANES), f32)],
+    dma = pltpu.SemaphoreType.DMA
+    return pl.pallas_call(
+        functools.partial(x_kernel, count),
+        in_specs=[SMEM, SMEM] + [HBM] * 8,
+        out_specs=[HBM, SMALL],
+        out_shape=[pltpu.HBM((3, nx, ny), f32), jax.ShapeDtypeStruct((1, LANES), f32)],
         scratch_shapes=[pltpu.VMEM((nx, 3 * ny), bf16), pltpu.VMEM((nx, 3 * ny), bf16),
-                        pltpu.VMEM((count, 8, ny), f32), pltpu.VMEM((8, ny), f32)],
-        compiler_params=params(60, dimension_semantics=("arbitrary",)),
+                        pltpu.VMEM(fwd.shape, bf16), pltpu.VMEM(inv.shape, bf16),
+                        pltpu.VMEM(adj.shape, f32), pltpu.VMEM(adj.shape, bf16), pltpu.VMEM((nx, ny), jnp.int32),
+                        pltpu.VMEM(adj.shape, f32), pltpu.VMEM((count, 8, ny), f32), pltpu.VMEM((8, ny), f32),
+                        dma((3,)), dma((steps,)), dma((4 * steps,)), dma((steps,))],
+        compiler_params=params(32),
         cost_estimate=pl.CostEstimate(flops=6 * nx * nx * 3 * ny, bytes_accessed=12 * 1024 * 1024, transcendentals=0),
         name="x_part",
-    )(scal, coef, fwd, inv, *[far_off(low) for low in lows], adj, wind, classes)
+    )(scal, coef, far_off(fwd), far_off(inv), *[far_off(low) for low in lows], far_off(adj), far_off(wind),
+      far_off(classes))
 
 
 def y_kernel(after, recv, table, out, plus, minus, table_v, out_v, sem_t, sem_o):
@@ -258,10 +260,6 @@
     )(far_off(after), near_by(recv), far_off(table))
 
 
-def speed_of(w):
-    return jnp.sqrt(w[0] * w[0] + w[1] * w[1] + w[2] * w[2])
-
-
 def gate_kernel(early, q0, q1, q2, out):
     out[...] = early[...]
 
@@ -269,13 +267,13 @@
 def gate(early, far):
     return pl.pallas_call(
         gate_kernel,
-        in_specs=[SMALL, HBM, HBM, HBM],
+        in_specs=[SMALL, HBM, HBM, SMALL],
         out_specs=SMALL,
         out_shape=jax.ShapeDtypeStruct(early.shape, f32),
         compiler_params=params(4),
         cost_estimate=pl.CostEstimate(flops=GATE_FLOPS, bytes_accessed=1024, transcendentals=0),
         name="gate",
-    )(early, *[far_off(q) for q in far])
+    )(early, *[far_off(q) for q in far[:2]], near_by(far[2]))
 
 
 def join_kernel(count, scal, early, part, wind, classes, adj, p0, p1, p2, q0, q1, q2, drift, rhs, adj_v, sums,
@@ -288,7 +286,7 @@
         loads.append(begin([(wind.at[:, at], wind_v.at[:, at]), (classes.at[at], cls_v.at[at]),
                             (part.at[:, at], part_v.at[:, at])]
                            + [(p.at[at], near_v.at[c, at]) for c, p in enumerate((p0, p1, p2))]
-                           + [(q.at[at], far_v.at[c, at]) for c, q in enumerate((q0, q1, q2))], sem_in, 9 * k))
+                           + [(q.at[at], far_v.at[c, at]) for c, q in enumerate((q0, q1))], sem_in, 8 * k))
     kept = begin([(adj, adj_v)], sem_adj)
     acc[...] = jnp.zeros_like(acc)
     for k in range(CHUNKS):
@@ -300,8 +298,9 @@
             up, down = viscosity + slope, viscosity - slope
             total = jnp.zeros_like(slope)
             for c in range(3):
+                q = q2[at] if c == 2 else far_v[c, at]
                 r = part_v[c, at] + drift[s, c].astype(f32)
-                r += up * near_v[c, at].astype(f32) + down * far_v[c, at].astype(f32)
+                r += up * near_v[c, at].astype(f32) + down * q.astype(f32)
                 rhs[c, at] = r
                 total += r * w[c]
             class_sums(scal[0] * speed_of(w) * total, cls_v[at], acc, count)
@@ -316,17 +315,17 @@
     dma = pltpu.SemaphoreType.DMA
     return pl.pallas_call(
         functools.partial(join_kernel, count),
-        in_specs=[SMEM, SMALL] + [HBM] * 10 + [SMALL],
+        in_specs=[SMEM, SMALL] + [HBM] * 9 + [SMALL] * 2,
         out_specs=[SMALL, SMALL, SMALL],
-        out_shape=[pltpu.VMEM(whole, f32), pltpu.VMEM(whole, f32), jax.ShapeDtypeStruct((parts, 1, LANES), f32)],
+        out_shape=[pltpu.VMEM(whole, f32), pltpu.VMEM(whole, f32), jax.ShapeDtypeStruct((2 * parts, 1, LANES), f32)],
         scratch_shapes=[pltpu.VMEM(whole, f32), pltpu.VMEM(whole, bf16), pltpu.VMEM((nx, ny), jnp.int32),
-                        pltpu.VMEM(whole, bf16), pltpu.VMEM(whole, bf16),
-                        pltpu.VMEM((count, 8, ny), f32), dma((9 * CHUNKS,)), dma((1,))],
+                        pltpu.VMEM(whole, bf16), pltpu.VMEM((2, nx, ny), bf16),
+                        pltpu.VMEM((count, 8, ny), f32), dma((8 * CHUNKS,)), dma((1,))],
         compiler_params=params(),
         cost_estimate=pl.CostEstimate(flops=100 * nx * ny, bytes_accessed=8 * 1024 * 1024, transcendentals=0),
         name="join",
     )(scal, early, far_off(part), far_off(wind), far_off(classes), far_off(adj),
-      *[far_off(a) for a in near + far], near_by(drift))
+      *[far_off(a) for a in near + far[:2]], near_by(far[2]), near_by(drift))
 
 
 def merge(rows, count):
@@ -379,8 +378,8 @@
     )(got, near_by(adj), near_by(rhs))
 
 
-def swap(x, axes):
-    return lax.all_to_all(x, axes, split_axis=0, concat_axis=0, tiled=True)
+def swap(x, axes, groups=None):
+    return lax.all_to_all(x, axes, split_axis=0, concat_axis=0, axis_index_groups=groups, tiled=True)
 
 
 def local(adjoint, wind, classes, drag_coef):
@@ -408,10 +407,13 @@
     far = [lax.ppermute(low, "gz", onward) for low in near]
 
     part, early = x_part(scal, drag_coef, jnp.asarray(fx), jnp.asarray(inv_x), lows, adj, wnd, classes)
-    drift = swap(y_part(early, recv, jnp.asarray(line_tables(total_y))), "gy")
+    drift = swap(y_part(part, recv, jnp.asarray(line_tables(total_y))), "gy")
     rhs, adj, sums = join(scal, gate(early, far), part, wnd, classes, adj, near, far, drift, count)
 
-    got = swap(fold(swap(sums, "gy"), gz, count), "gz")
+    group, pairs = 2 * gy, gz // 2
+    within = [[k * group + i for i in range(group)] for k in range(pairs)]
+    across = [[k * group + i for k in range(pairs)] for i in range(group)]
+    got = swap(fold(swap(sums, ("gz", "gy"), within), pairs, count), ("gz", "gy"), across)
     scale = 1.0 / math.sqrt(nx * total_y * gz / count)
     new, sens = finish(got, adj, rhs, count, scale)
     return new.reshape(adjoint.shape), sens.reshape(count)

time: 116 us -> 113 us (0.974)
  blocking collectives: 35.5 us -> 32.6 us
    all_to_all x2, blocking collectives: 35.5 us -> 32.6 us  [swap(): lax.all_to_all(x, axes, split_axis=0, concat_axis=0, axis_index_groups=gr...]
  transfers between devices with their start and end apart: 8 -> 8, of which waited for: 5 -> 5; matrix products, arithmetic and copies ran while one was open for 1% -> 0% of each run, Pallas kernels for 12% -> 13%
where the time goes in v4:
time: 113 us; the launch traced here: 112 us
  blocking collectives  32.6 us (29%)
  starting transfers between devices  31.1 us (28%)
  waiting for transfers between devices  24.7 us (22%)
  Pallas kernels  22.8 us (20%)
    all_to_all x2, blocking collectives, swap(): lax.all_to_all(x, axes, split_axis=0, concat_axis=0, axis_index_groups=gr...  32.6 us
    all_to_all x2, starting transfers between devices, swap(): lax.all_to_all(x, axes, split_axis=0, concat_axis=0, axis_index_groups=gr...  15 us
    all_to_all x2, waiting for transfers between devices, swap(): lax.all_to_all(x, axes, split_axis=0, concat_axis=0, axis_index_groups=gr...  13.8 us
    pallas_call x1, Pallas kernels, x_part(): pl.pallas_call(functools.partial(x_kernel, count), in_specs=[SMEM, SMEM]...  11.3 us
    ppermute x3, starting transfers between devices, local(): far = [lax.ppermute(low, 'gz', onward) for low in near]  8.94 us
    ppermute x3, waiting for transfers between devices, local(): far = [lax.ppermute(low, 'gz', onward) for low in near]  7.48 us
    ppermute x3, starting transfers between devices, local(): near = [lax.ppermute(low, 'gz', pair) for low in lows]  7.19 us
    pallas_call x1, Pallas kernels, join(): pl.pallas_call(functools.partial(join_kernel, count), in_specs=[SMEM, SMA...  3.92 us
  transfers between devices with their start and end apart: 8, of which 5 were waited for; matrix products, arithmetic and copies ran while one was open for 0% of the time, Pallas kernels for 13%

profile of v4, /device:TPU:1, one launch (start us, length us, event | category | flops | bytes accessed | tf_op | source)
XLA Modules:
  0.0 112.2 jit_solution(13520201333197634302)
XLA Ops:
  0.6 2.5 %pack.1 = (bf16[8,4,128,128]{3,2,1,0:T(8,128)(2,1)}, bf16[1024,128]{1,0:T(8,128)(2,1)}, bf16[1024,128]{1,0:T(8,128)(2,1)}, bf16[1024,128]{1,0:T(8,128)(2,1)}) custom-call(f32[3,1024,128]{2,1,0:T(8,128)} %bitcast.8, bf16[3,1024,128]{2,1,0:T(8,128)(2,1)} %bitcast.11), custom_call_target="tpu_custom_call" | custom-call | bytes 4194304 | tf_op jit(solution)/shard_map/pack/pallas_call | solution.py:119
  3.2 0.0 copy-start
  3.2 10.5 %all-to-all-start = ((bf16[8,4,128,128]{3,2,1,0:T(8,128)(2,1)}), bf16[8,4,128,128]{3,2,1,0:T(8,128)(2,1)S(1)}, u32[]{:S(2)}, u32[]{:S(2)}) async-start(bf16[8,4,128,128]{3,2,1,0:T(8,128)(2,1)} %get-tuple-element.18), calls=%async_computation | async-start | bytes 2097152 | tf_op jit(solution)/shard_map/all_to_all | solution.py:382
  13.7 1.9 %collective-permute-start = (bf16[1024,128]{1,0:T(8,128)(2,1)S(1)}, bf16[1024,128]{1,0:T(8,128)(2,1)S(1)}, u32[]{:S(2)}, u32[]{:S(2)}) collective-permute-start(bf16[1024,128]{1,0:T(8,128)(2,1)S(1)} %copy-done.6), channel_id=1, source_target_pairs={{0,8},{8,0},{16,24},{24,16},{32,40},{40,32},{48,56},{56,48},{64,72... | collective-permute-start | bytes 786440 | tf_op jit(solution)/shard_map/ppermute | solution.py:406
  15.6 3.4 %collective-permute-start.2 = (bf16[1024,128]{1,0:T(8,128)(2,1)S(1)}, bf16[1024,128]{1,0:T(8,128)(2,1)S(1)}, u32[]{:S(2)}, u32[]{:S(2)}) collective-permute-start(bf16[1024,128]{1,0:T(8,128)(2,1)S(1)} %copy-done.5), channel_id=1, source_target_pairs={{0,8},{8,0},{16,24},{24,16},{32,40},{40,32},{48,56},{56,48},{64,72... | collective-permute-start | bytes 786440 | tf_op jit(solution)/shard_map/ppermute | solution.py:406
  19.0 1.9 %collective-permute-start.4 = (bf16[1024,128]{1,0:T(8,128)(2,1)S(1)}, bf16[1024,128]{1,0:T(8,128)(2,1)S(1)}, u32[]{:S(2)}, u32[]{:S(2)}) collective-permute-start(bf16[1024,128]{1,0:T(8,128)(2,1)S(1)} %copy-done.4), channel_id=1, source_target_pairs={{0,8},{8,0},{16,24},{24,16},{32,40},{40,32},{48,56},{56,48},{64,72... | collective-permute-start | bytes 786440 | tf_op jit(solution)/shard_map/ppermute | solution.py:406
  21.0 0.1 pad_maximum_fusion.scal
  21.0 11.3 %x_part.1 = (f32[3,1024,128]{2,1,0:T(8,128)}, f32[1,128]{1,0:T(1,128)S(1)}) custom-call(f32[2]{0:T(128)S(1)} %pad_maximum_fusion.scal, f32[16]{0:T(128)S(1)} %copy-done, bf16[1024,1024]{1,0:T(8,128)(2,1)} %constant.37.clone.fwd, bf16[4,512,1024]{2,1,0:T(8,128)(2,1)} %constant.38.clone.inv, bf16[1024,128]{1,0:T(8,128)(2,1)} %get-tuple-element.13.l0, ...), custom_call_target="tpu_custom_call" | custom-call | flops 2415919104 | bytes 12582912 | tf_op jit(solution)/shard_map/x_part/pallas_call | solution.py:200
  32.3 7.8 %all-to-all-done.recv = bf16[8,4,128,128]{3,2,1,0:T(8,128)(2,1)S(1)} async-done(((bf16[8,4,128,128]{3,2,1,0:T(8,128)(2,1)}), bf16[8,4,128,128]{3,2,1,0:T(8,128)(2,1)S(1)}, u32[]{:S(2)}, u32[]{:S(2)}) %all-to-all-start) | async-done | bytes 1048608 | tf_op jit(solution)/shard_map/all_to_all | solution.py:382
  40.1 3.3 %y_part.1 = bf16[8,3,128,128]{3,2,1,0:T(8,128)(2,1)} custom-call(f32[3,1024,128]{2,1,0:T(8,128)} %get-tuple-element.17.after.part, bf16[8,4,128,128]{3,2,1,0:T(8,128)(2,1)S(1)} %all-to-all-done.recv, bf16[2,4,512,256]{3,2,1,0:T(8,128)(2,1)} %constant.39.clone.table), custom_call_target="tpu_custom_call" | custom-call | flops 805306368 | bytes 4194304 | tf_op jit(solution)/shard_map/y_part/pallas_call | solution.py:250
  43.4 4.5 %all-to-all-start.1 = ((bf16[8,3,128,128]{3,2,1,0:T(8,128)(2,1)}), bf16[8,3,128,128]{3,2,1,0:T(8,128)(2,1)S(1)}, u32[]{:S(2)}, u32[]{:S(2)}) async-start(bf16[8,3,128,128]{3,2,1,0:T(8,128)(2,1)} %y_part.1), calls=%async_computation.1 | async-start | bytes 1572864 | tf_op jit(solution)/shard_map/all_to_all | solution.py:382
  48.0 0.0 collective-permute-done.p0
  48.0 3.1 %collective-permute-start.1 = (bf16[1024,128]{1,0:T(8,128)(2,1)S(1)}, bf16[1024,128]{1,0:T(8,128)(2,1)S(1)}, u32[]{:S(2)}, u32[]{:S(2)}) collective-permute-start(bf16[1024,128]{1,0:T(8,128)(2,1)S(1)} %collective-permute-done.p0), channel_id=1, source_target_pairs={{0,16},{16,32},{32,48},{48,64},{64,80},{80,96},{96,112},{112,128},... | collective-permute-start | bytes 786440 | tf_op jit(solution)/shard_map/ppermute | solution.py:407
  51.1 3.1 %collective-permute-start.3 = (bf16[1024,128]{1,0:T(8,128)(2,1)S(1)}, bf16[1024,128]{1,0:T(8,128)(2,1)S(1)}, u32[]{:S(2)}, u32[]{:S(2)}) collective-permute-start(bf16[1024,128]{1,0:T(8,128)(2,1)S(1)} %collective-permute-done.2.p1), channel_id=1, source_target_pairs={{0,16},{16,32},{32,48},{48,64},{64,80},{80,96},{96,112},{112,128},... | collective-permute-start | bytes 786440 | tf_op jit(solution)/shard_map/ppermute | solution.py:407
  54.3 3.4 %collective-permute-done.4.p2 = bf16[1024,128]{1,0:T(8,128)(2,1)S(1)} collective-permute-done((bf16[1024,128]{1,0:T(8,128)(2,1)S(1)}, bf16[1024,128]{1,0:T(8,128)(2,1)S(1)}, u32[]{:S(2)}, u32[]{:S(2)}) %collective-permute-start.4) | collective-permute-done | bytes 262176 | tf_op jit(solution)/shard_map/ppermute | solution.py:406
  57.7 2.7 %collective-permute-start.5 = (bf16[1024,128]{1,0:T(8,128)(2,1)S(1)}, bf16[1024,128]{1,0:T(8,128)(2,1)S(1)}, u32[]{:S(2)}, u32[]{:S(2)}) collective-permute-start(bf16[1024,128]{1,0:T(8,128)(2,1)S(1)} %collective-permute-done.4.p2), channel_id=1, source_target_pairs={{0,16},{16,32},{32,48},{48,64},{64,80},{80,96},{96,112},{112,128},... | collective-permute-start | bytes 786440 | tf_op jit(solution)/shard_map/ppermute | solution.py:407
  60.4 0.0 collective-permute-done.1.q0
  60.4 1.9 %collective-permute-done.3.q1 = bf16[1024,128]{1,0:T(8,128)(2,1)S(1)} collective-permute-done((bf16[1024,128]{1,0:T(8,128)(2,1)S(1)}, bf16[1024,128]{1,0:T(8,128)(2,1)S(1)}, u32[]{:S(2)}, u32[]{:S(2)}) %collective-permute-start.3) | collective-permute-done | bytes 262176 | tf_op jit(solution)/shard_map/ppermute | solution.py:407
  62.3 5.6 %collective-permute-done.5.q2 = bf16[1024,128]{1,0:T(8,128)(2,1)S(1)} collective-permute-done((bf16[1024,128]{1,0:T(8,128)(2,1)S(1)}, bf16[1024,128]{1,0:T(8,128)(2,1)S(1)}, u32[]{:S(2)}, u32[]{:S(2)}) %collective-permute-start.5) | collective-permute-done | bytes 262176 | tf_op jit(solution)/shard_map/ppermute | solution.py:407
  67.9 5.9 %all-to-all-done.1.drift = bf16[8,3,128,128]{3,2,1,0:T(8,128)(2,1)S(1)} async-done(((bf16[8,3,128,128]{3,2,1,0:T(8,128)(2,1)}), bf16[8,3,128,128]{3,2,1,0:T(8,128)(2,1)S(1)}, u32[]{:S(2)}, u32[]{:S(2)}) %all-to-all-start.1) | async-done | bytes 786464 | tf_op jit(solution)/shard_map/all_to_all | solution.py:382
  73.9 3.9 %join.1 = (f32[3,1024,128]{2,1,0:T(8,128)S(1)}, f32[3,1024,128]{2,1,0:T(8,128)S(1)}, f32[16,1,128]{2,1,0:T(1,128)S(1)}) custom-call(f32[2]{0:T(128)S(1)} %pad_maximum_fusion.scal, f32[1,128]{1,0:T(1,128)S(1)} %gate.1.early, f32[3,1024,128]{2,1,0:T(8,128)} %get-tuple-element.17.after.part, bf16[3,1024,128]{2,1,0:T(8,128)(2,1)} %bitcast.13, ...), custom_call_target="tpu_custom_call" | custom-call | flops 13107200 | bytes 8388608 | tf_op jit(solution)/shard_map/join/pallas_call | solution.py:316
  77.8 11.1 %all_to_all.20.got = f32[16,1,128]{2,1,0:T(1,128)S(1)} all-to-all(f32[16,1,128]{2,1,0:T(1,128)S(1)} %get-tuple-element.19), channel_id=1, replica_groups={{0,1,2,3,4,5,6,7,8,9,10,11,12,13,14,15},{16,17,18,19,20,21,22,23,24,25,..., dimensions={0} | all-to-all | bytes 16384 | tf_op jit(solution)/shard_map/all_to_all | solution.py:382
  88.9 21.5 %all_to_all.21.got = f32[32,1,128]{2,1,0:T(1,128)S(1)} all-to-all(f32[32,1,128]{2,1,0:T(1,128)S(1)} %fold.1), channel_id=1, replica_groups={{0,16,32,48,64,80,96,112,128,144,160,176,192,208,224,240,256,272,288,30..., dimensions={0} | all-to-all | bytes 32768 | tf_op jit(solution)/shard_map/all_to_all | solution.py:382
  110.4 1.8 %finish.1 = (f32[3,1024,128]{2,1,0:T(8,128)}, f32[1,16]{1,0:T(1,128)}) custom-call(f32[32,1,128]{2,1,0:T(1,128)S(1)} %all_to_all.21.got, f32[3,1024,128]{2,1,0:T(8,128)S(1)} %get-tuple-element.20.adj, f32[3,1024,128]{2,1,0:T(8,128)S(1)} %get-tuple-element.21.rhs), custom_call_target="tpu_custom_call" | custom-call | flops 786432 | bytes 4718592 | tf_op jit(solution)/shard_map/finish/pallas_call | solution.py:369
  (20 shorter events, 0.1 us)
Async XLA Ops:
  3.1 10.5 %copy-start.6 = (bf16[1024,128]{1,0:T(8,128)(2,1)S(1)}, bf16[1024,128]{1,0:T(8,128)(2,1)}, u32[]{:S(2)}) copy-start(bf16[1024,128]{1,0:T(8,128)(2,1)} %get-tuple-element.13.l0) | copy-start | bytes 786436
  3.1 12.4 %copy-start.5 = (bf16[1024,128]{1,0:T(8,128)(2,1)S(1)}, bf16[1024,128]{1,0:T(8,128)(2,1)}, u32[]{:S(2)}) copy-start(bf16[1024,128]{1,0:T(8,128)(2,1)} %get-tuple-element.14.l1) | copy-start | bytes 786436
  3.2 15.8 %copy-start.4 = (bf16[1024,128]{1,0:T(8,128)(2,1)S(1)}, bf16[1024,128]{1,0:T(8,128)(2,1)}, u32[]{:S(2)}) copy-start(bf16[1024,128]{1,0:T(8,128)(2,1)} %get-tuple-element.15.l2) | copy-start | bytes 786436
  3.2 17.9 %copy-start = (f32[16]{0:T(128)S(1)}, f32[16]{0:T(128)}, u32[]{:S(2)}) copy-start(f32[16]{0:T(128)} %coef.1) | copy-start | bytes 196
  3.2 37.0 %all-to-all-start = ((bf16[8,4,128,128]{3,2,1,0:T(8,128)(2,1)}), bf16[8,4,128,128]{3,2,1,0:T(8,128)(2,1)S(1)}, u32[]{:S(2)}, u32[]{:S(2)}) async-start(bf16[8,4,128,128]{3,2,1,0:T(8,128)(2,1)} %get-tuple-element.18), calls=%async_computation | async-start | bytes 2097152 | tf_op jit(solution)/shard_map/all_to_all | solution.py:382
  13.7 34.3 %collective-permute-start = (bf16[1024,128]{1,0:T(8,128)(2,1)S(1)}, bf16[1024,128]{1,0:T(8,128)(2,1)S(1)}, u32[]{:S(2)}, u32[]{:S(2)}) collective-permute-start(bf16[1024,128]{1,0:T(8,128)(2,1)S(1)} %copy-done.6), channel_id=1, source_target_pairs={{0,8},{8,0},{16,24},{24,16},{32,40},{40,32},{48,56},{56,48},{64,72... | collective-permute-start | bytes 786440 | tf_op jit(solution)/shard_map/ppermute | solution.py:406
  15.6 35.5 %collective-permute-start.2 = (bf16[1024,128]{1,0:T(8,128)(2,1)S(1)}, bf16[1024,128]{1,0:T(8,128)(2,1)S(1)}, u32[]{:S(2)}, u32[]{:S(2)}) collective-permute-start(bf16[1024,128]{1,0:T(8,128)(2,1)S(1)} %copy-done.5), channel_id=1, source_target_pairs={{0,8},{8,0},{16,24},{24,16},{32,40},{40,32},{48,56},{56,48},{64,72... | collective-permute-start | bytes 786440 | tf_op jit(solution)/shard_map/ppermute | solution.py:406
  19.0 38.7 %collective-permute-start.4 = (bf16[1024,128]{1,0:T(8,128)(2,1)S(1)}, bf16[1024,128]{1,0:T(8,128)(2,1)S(1)}, u32[]{:S(2)}, u32[]{:S(2)}) collective-permute-start(bf16[1024,128]{1,0:T(8,128)(2,1)S(1)} %copy-done.4), channel_id=1, source_target_pairs={{0,8},{8,0},{16,24},{24,16},{32,40},{40,32},{48,56},{56,48},{64,72... | collective-permute-start | bytes 786440 | tf_op jit(solution)/shard_map/ppermute | solution.py:406
  43.4 30.4 %all-to-all-start.1 = ((bf16[8,3,128,128]{3,2,1,0:T(8,128)(2,1)}), bf16[8,3,128,128]{3,2,1,0:T(8,128)(2,1)S(1)}, u32[]{:S(2)}, u32[]{:S(2)}) async-start(bf16[8,3,128,128]{3,2,1,0:T(8,128)(2,1)} %y_part.1), calls=%async_computation.1 | async-start | bytes 1572864 | tf_op jit(solution)/shard_map/all_to_all | solution.py:382
  48.0 19.9 %copy-start.1 = (bf16[1024,128]{1,0:T(8,128)(2,1)}, bf16[1024,128]{1,0:T(8,128)(2,1)S(1)}, u32[]{:S(2)}) copy-start(bf16[1024,128]{1,0:T(8,128)(2,1)S(1)} %collective-permute-done.p0) | copy-start | bytes 786436
  48.0 12.4 %collective-permute-start.1 = (bf16[1024,128]{1,0:T(8,128)(2,1)S(1)}, bf16[1024,128]{1,0:T(8,128)(2,1)S(1)}, u32[]{:S(2)}, u32[]{:S(2)}) collective-permute-start(bf16[1024,128]{1,0:T(8,128)(2,1)S(1)} %collective-permute-done.p0), channel_id=1, source_target_pairs={{0,16},{16,32},{32,48},{48,64},{64,80},{80,96},{96,112},{112,128},... | collective-permute-start | bytes 786440 | tf_op jit(solution)/shard_map/ppermute | solution.py:407
  51.1 16.8 %copy-start.2 = (bf16[1024,128]{1,0:T(8,128)(2,1)}, bf16[1024,128]{1,0:T(8,128)(2,1)S(1)}, u32[]{:S(2)}) copy-start(bf16[1024,128]{1,0:T(8,128)(2,1)S(1)} %collective-permute-done.2.p1) | copy-start | bytes 786436
  51.1 11.1 %collective-permute-start.3 = (bf16[1024,128]{1,0:T(8,128)(2,1)S(1)}, bf16[1024,128]{1,0:T(8,128)(2,1)S(1)}, u32[]{:S(2)}, u32[]{:S(2)}) collective-permute-start(bf16[1024,128]{1,0:T(8,128)(2,1)S(1)} %collective-permute-done.2.p1), channel_id=1, source_target_pairs={{0,16},{16,32},{32,48},{48,64},{64,80},{80,96},{96,112},{112,128},... | collective-permute-start | bytes 786440 | tf_op jit(solution)/shard_map/ppermute | solution.py:407
  57.7 10.2 %copy-start.3 = (bf16[1024,128]{1,0:T(8,128)(2,1)}, bf16[1024,128]{1,0:T(8,128)(2,1)S(1)}, u32[]{:S(2)}) copy-start(bf16[1024,128]{1,0:T(8,128)(2,1)S(1)} %collective-permute-done.4.p2) | copy-start | bytes 786436
  57.7 10.2 %collective-permute-start.5 = (bf16[1024,128]{1,0:T(8,128)(2,1)S(1)}, bf16[1024,128]{1,0:T(8,128)(2,1)S(1)}, u32[]{:S(2)}, u32[]{:S(2)}) collective-permute-start(bf16[1024,128]{1,0:T(8,128)(2,1)S(1)} %collective-permute-done.4.p2), channel_id=1, source_target_pairs={{0,16},{16,32},{32,48},{48,64},{64,80},{80,96},{96,112},{112,128},... | collective-permute-start | bytes 786440 | tf_op jit(solution)/shard_map/ppermute | solution.py:407
  60.4 7.5 %copy-start.7 = (bf16[1024,128]{1,0:T(8,128)(2,1)}, bf16[1024,128]{1,0:T(8,128)(2,1)S(1)}, u32[]{:S(2)}) copy-start(bf16[1024,128]{1,0:T(8,128)(2,1)S(1)} %collective-permute-done.1.q0) | copy-start | bytes 786436
  62.3 5.6 %copy-start.8 = (bf16[1024,128]{1,0:T(8,128)(2,1)}, bf16[1024,128]{1,0:T(8,128)(2,1)S(1)}, u32[]{:S(2)}) copy-start(bf16[1024,128]{1,0:T(8,128)(2,1)S(1)} %collective-permute-done.3.q1) | copy-start | bytes 786436

commit v5 on v4

--- a/solution.py
+++ b/solution.py
@@ -56,6 +56,7 @@
 
 
 CHUNKS = 4
+SUB = 64
 GATE_FLOPS = 10**10
 
 
@@ -147,17 +148,13 @@
     return jnp.sum(jnp.where(lane == row + offset, per, 0.0), axis=0, keepdims=True)
 
 
-def x_kernel(count, scal, coef, fwd, inv, l0, l1, l2, adj, wind, classes, rhs, sums,
-             low, spec, fwd_v, inv_v, adj_v, wind_v, cls_v, rhs_v, acc, top, sem_l, sem_f, sem_i, sem_o):
+def x_kernel(after, fwd, inv, l0, l1, l2, wind, rhs, low, spec, fwd_v, inv_v, wind_v, rhs_v, sem_l, sem_f, sem_i, sem_o):
     nx, ny = l0.shape
     steps = nx // TILE
     ats = [pl.ds(t * TILE, TILE) for t in range(steps)]
     lines = begin([(ref, low.at[:, pl.ds(c * ny, ny)]) for c, ref in enumerate((l0, l1, l2))], sem_l)
     tiles = begin([(fwd.at[at], fwd_v.at[at]) for at in ats], sem_f)
-    loads = [begin([(inv.at[t], inv_v.at[t]), (adj.at[:, at], adj_v.at[:, at]), (wind.at[:, at], wind_v.at[:, at]),
-                    (classes.at[at], cls_v.at[at])], sem_i, 4 * t) for t, at in enumerate(ats)]
-    acc[...] = jnp.zeros_like(acc)
-    top[...] = jnp.zeros_like(top)
+    loads = [begin([(inv.at[t], inv_v.at[t]), (wind.at[0, at], wind_v.at[at])], sem_i, 2 * t) for t, at in enumerate(ats)]
     finish_all(lines)
     for t in range(0, steps, 2):
         finish_all(tiles[t:t + 2])
@@ -167,51 +164,33 @@
     for t, at in enumerate(ats):
         finish_all(loads[t])
         both = dot(inv_v[t], spec[...])
-        dx, dxx = both[:TILE], both[TILE:]
-        cls = cls_v[at]
-        w = [wind_v[c, at].astype(f32) for c in range(3)]
-        speed = speed_of(w)
-        weight = scal[0] * speed
-        drag = jnp.zeros_like(speed)
-        for k in range(count):
-            drag = jnp.where(cls == k, coef[k], drag)
-        damp = drag * weight + 2.0 * viscosity
-        total = jnp.zeros_like(speed)
-        for c in range(3):
-            a = adj_v[c, at]
-            total += a * w[c]
-            cols = slice(c * ny, (c + 1) * ny)
-            rhs_v[c, at] = w[0] * dx[:, cols] + viscosity * dxx[:, cols] - damp * a
+        for r in range(0, TILE, SUB):
+            sub = slice(t * TILE + r, t * TILE + r + SUB)
+            w0 = wind_v[sub].astype(f32)
+            for c in range(3):
+                cols = slice(c * ny, (c + 1) * ny)
+                rhs_v[c, sub] = w0 * both[r:r + SUB, cols] + viscosity * both[TILE + r:TILE + r + SUB, cols]
         stores += begin([(rhs_v.at[:, at], rhs.at[:, at])], sem_o, t)
-        class_sums(weight * total, cls, acc, count)
-        size = jnp.abs(w[0]) + jnp.abs(w[1]) + jnp.abs(w[2])
-        top[...] = jnp.maximum(top[...], jnp.max(size.reshape(-1, 8, ny), axis=0))
-    lane = lax.broadcasted_iota(jnp.int32, (1, LANES), 1)
-    peak = jnp.max(jnp.max(top[...], axis=0, keepdims=True), axis=1, keepdims=True)
-    sums[...] = jnp.where(lane == 2 * count, peak, to_lanes(acc, count, 0))
     finish_all(stores)
 
 
-def x_part(scal, coef, fwd, inv, lows, adj, wind, classes):
-    _, nx, ny = adj.shape
-    count = coef.shape[0]
+def x_part(after, fwd, inv, lows, wind):
+    _, nx, ny = wind.shape
     steps = nx // TILE
     dma = pltpu.SemaphoreType.DMA
     return pl.pallas_call(
-        functools.partial(x_kernel, count),
-        in_specs=[SMEM, SMEM] + [HBM] * 8,
-        out_specs=[HBM, SMALL],
-        out_shape=[pltpu.HBM((3, nx, ny), f32), jax.ShapeDtypeStruct((1, LANES), f32)],
+        x_kernel,
+        in_specs=[SMEM] + [HBM] * 6,
+        out_specs=HBM,
+        out_shape=pltpu.HBM((3, nx, ny), f32),
         scratch_shapes=[pltpu.VMEM((nx, 3 * ny), bf16), pltpu.VMEM((nx, 3 * ny), bf16),
                         pltpu.VMEM(fwd.shape, bf16), pltpu.VMEM(inv.shape, bf16),
-                        pltpu.VMEM(adj.shape, f32), pltpu.VMEM(adj.shape, bf16), pltpu.VMEM((nx, ny), jnp.int32),
-                        pltpu.VMEM(adj.shape, f32), pltpu.VMEM((count, 8, ny), f32), pltpu.VMEM((8, ny), f32),
-                        dma((3,)), dma((steps,)), dma((4 * steps,)), dma((steps,))],
+                        pltpu.VMEM((nx, ny), bf16), pltpu.VMEM((3, nx, ny), f32),
+                        dma((3,)), dma((steps,)), dma((2 * steps,)), dma((steps,))],
         compiler_params=params(32),
         cost_estimate=pl.CostEstimate(flops=6 * nx * nx * 3 * ny, bytes_accessed=12 * 1024 * 1024, transcendentals=0),
         name="x_part",
-    )(scal, coef, far_off(fwd), far_off(inv), *[far_off(low) for low in lows], far_off(adj), far_off(wind),
-      far_off(classes))
+    )(after, far_off(fwd), far_off(inv), *[far_off(low) for low in lows], far_off(wind))
 
 
 def y_kernel(after, recv, table, out, plus, minus, table_v, out_v, sem_t, sem_o):
@@ -228,15 +207,19 @@
     stores = []
     for t in range(steps):
         tiles[t].wait()
-        for c in range(3):
-            at = slice(c * rows, (c + 1) * rows)
-            p1, q1 = dot(plus[at], table_v[t, 0]), dot(minus[at], table_v[t, 1])
-            p2, q2 = dot(plus[at], table_v[t, 2]), dot(minus[at], table_v[t, 3])
-            for dy, dyy, base in ((p1 + q1, p2 + q2, t * per), (p1 - q1, p2 - q2, half + t * per)):
-                for s in range(per):
-                    cols = slice(s * ny, (s + 1) * ny)
-                    w1 = recv[base + s, 3].astype(f32)
-                    out_v[base + s, c] = (w1 * dy[:, cols] + viscosity * dyy[:, cols]).astype(bf16)
+        p1, q1 = dot(plus[...], table_v[t, 0]), dot(minus[...], table_v[t, 1])
+        p2, q2 = dot(plus[...], table_v[t, 2]), dot(minus[...], table_v[t, 3])
+        for s in range(per):
+            cols = slice(s * ny, (s + 1) * ny)
+            a, b = t * per + s, half + t * per + s
+            for r in range(0, rows, SUB):
+                sub = slice(r, r + SUB)
+                wa, wb = recv[a, 3, sub].astype(f32), recv[b, 3, sub].astype(f32)
+                for c in range(3):
+                    at = slice(c * rows + r, c * rows + r + SUB)
+                    u1, v1, u2, v2 = (m[at, cols] for m in (p1, q1, p2, q2))
+                    out_v[a, c, sub] = (wa * (u1 + v1) + viscosity * (u2 + v2)).astype(bf16)
+                    out_v[b, c, sub] = (wb * (u1 - v1) + viscosity * (u2 - v2)).astype(bf16)
         ends = [pl.ds(base, per) for base in (t * per, half + t * per)]
         stores += begin([(out_v.at[e], out.at[e]) for e in ends], sem_o, 2 * t)
     finish_all(stores)
@@ -276,56 +259,118 @@
     )(early, *[far_off(q) for q in far[:2]], near_by(far[2]))
 
 
-def join_kernel(count, scal, early, part, wind, classes, adj, p0, p1, p2, q0, q1, q2, drift, rhs, adj_v, sums,
-                part_v, wind_v, cls_v, near_v, far_v, acc, sem_in, sem_adj):
+def local_kernel(count, scal, coef, part, wind, classes, adj, p0, p1, p2, q0, rhs, sums,
+                 part_v, wind_v, cls_v, adj_v, near_v, far_v, first, second, top, sem_in, sem_out):
+    nx, ny = classes.shape
+    rows = nx // CHUNKS
+    loads, stores = [], []
+    for k in range(CHUNKS):
+        at = pl.ds(k * rows, rows)
+        loads.append(begin([(a.at[:, at], b.at[:, at]) for a, b in ((wind, wind_v), (part, part_v), (adj, adj_v))]
+                           + [(classes.at[at], cls_v.at[at]), (q0.at[at], far_v.at[at])]
+                           + [(p.at[at], near_v.at[c, at]) for c, p in enumerate((p0, p1, p2))], sem_in, 8 * k))
+    for ref in (first, second, top):
+        ref[...] = jnp.zeros_like(ref)
+    for k in range(CHUNKS):
+        finish_all(loads[k])
+        for n in range(k * rows // SUB, (k + 1) * rows // SUB):
+            at = slice(n * SUB, (n + 1) * SUB)
+            cls = cls_v[at]
+            w = [wind_v[c, at].astype(f32) for c in range(3)]
+            size = jnp.abs(w[0]) + jnp.abs(w[1]) + jnp.abs(w[2])
+            top[...] = jnp.maximum(top[...], jnp.max(size.reshape(-1, 8, ny), axis=0))
+            weight = scal[0] * speed_of(w)
+            drag = jnp.zeros_like(weight)
+            for m in range(count):
+                drag = jnp.where(cls == m, coef[m], drag)
+            damp = drag * weight + 2.0 * viscosity
+            slope = (0.5 * scal[1]) * w[2]
+            held, moved = jnp.zeros_like(weight), jnp.zeros_like(weight)
+            for c in range(3):
+                a = adj_v[c, at]
+                r = part_v[c, at] - damp * a + (viscosity + slope) * near_v[c, at].astype(f32)
+                if c == 0:
+                    r += (viscosity - slope) * far_v[at].astype(f32)
+                part_v[c, at] = r
+                held += a * w[c]
+                moved += r * w[c]
+            class_sums(weight * held, cls, first, count)
+            class_sums(weight * moved, cls, second, count)
+        at = pl.ds(k * rows, rows)
+        stores += begin([(part_v.at[:, at], rhs.at[:, at])], sem_out, k)
+    lane = lax.broadcasted_iota(jnp.int32, (1, LANES), 1)
+    peak = jnp.max(jnp.max(top[...], axis=0, keepdims=True), axis=1, keepdims=True)
+    both = to_lanes(first, count, 0) + to_lanes(second, count, count)
+    sums[...] = jnp.where(lane == 2 * count, peak, both)
+    finish_all(stores)
+
+
+def local_part(scal, coef, part, wind, classes, adj, near, far):
+    _, nx, ny = part.shape
+    count = coef.shape[0]
+    whole = (3, nx, ny)
+    dma = pltpu.SemaphoreType.DMA
+    return pl.pallas_call(
+        functools.partial(local_kernel, count),
+        in_specs=[SMEM, SMEM] + [HBM] * 8,
+        out_specs=[HBM, SMALL],
+        out_shape=[pltpu.HBM(whole, f32), jax.ShapeDtypeStruct((1, LANES), f32)],
+        scratch_shapes=[pltpu.VMEM(whole, f32), pltpu.VMEM(whole, bf16), pltpu.VMEM((nx, ny), jnp.int32),
+                        pltpu.VMEM(whole, f32), pltpu.VMEM(whole, bf16), pltpu.VMEM((nx, ny), bf16),
+                        pltpu.VMEM((count, 8, ny), f32), pltpu.VMEM((count, 8, ny), f32), pltpu.VMEM((8, ny), f32),
+                        dma((8 * CHUNKS,)), dma((CHUNKS,))],
+        compiler_params=params(),
+        cost_estimate=pl.CostEstimate(flops=200 * nx * ny, bytes_accessed=8 * 1024 * 1024, transcendentals=0),
+        name="local_part",
+    )(scal, coef, *[far_off(a) for a in (part, wind, classes, adj, *near, far)])
+
+
+def join_kernel(count, scal, early, part, wind, classes, adj, q1, q2, drift, rhs, adj_v, sums,
+                wind_v, cls_v, far_v, acc, sem_in, sem_adj):
     parts, _, rows, _ = drift.shape
     per = parts // CHUNKS
     loads = []
     for k in range(CHUNKS):
         at = pl.ds(k * per * rows, per * rows)
         loads.append(begin([(wind.at[:, at], wind_v.at[:, at]), (classes.at[at], cls_v.at[at]),
-                            (part.at[:, at], part_v.at[:, at])]
-                           + [(p.at[at], near_v.at[c, at]) for c, p in enumerate((p0, p1, p2))]
-                           + [(q.at[at], far_v.at[c, at]) for c, q in enumerate((q0, q1))], sem_in, 8 * k))
+                            (part.at[:, at], rhs.at[:, at]), (q1.at[at], far_v.at[at])], sem_in, 4 * k))
     kept = begin([(adj, adj_v)], sem_adj)
     acc[...] = jnp.zeros_like(acc)
     for k in range(CHUNKS):
         finish_all(loads[k])
-        for s in range(k * per, (k + 1) * per):
-            at = slice(s * rows, (s + 1) * rows)
+        for n in range(k * per * rows // SUB, (k + 1) * per * rows // SUB):
+            at = slice(n * SUB, (n + 1) * SUB)
+            s, sub = n * SUB // rows, slice(n * SUB % rows, n * SUB % rows + SUB)
             w = [wind_v[c, at].astype(f32) for c in range(3)]
-            slope = (0.5 * scal[1]) * w[2]
-            up, down = viscosity + slope, viscosity - slope
-            total = jnp.zeros_like(slope)
+            down = viscosity - (0.5 * scal[1]) * w[2]
+            total = jnp.zeros_like(down)
             for c in range(3):
-                q = q2[at] if c == 2 else far_v[c, at]
-                r = part_v[c, at] + drift[s, c].astype(f32)
-                r += up * near_v[c, at].astype(f32) + down * q.astype(f32)
-                rhs[c, at] = r
+                r = drift[s, c, sub].astype(f32)
+                if c > 0:
+                    r += down * (far_v[at] if c == 1 else q2[at]).astype(f32)
+                rhs[c, at] = rhs[c, at] + r
                 total += r * w[c]
             class_sums(scal[0] * speed_of(w) * total, cls_v[at], acc, count)
     sums[...] = jnp.broadcast_to((early[...] + to_lanes(acc, count, count))[None], sums.shape)
     finish_all(kept)
 
 
-def join(scal, early, part, wind, classes, adj, near, far, drift, count):
+def join(scal, early, part, wind, classes, adj, far, drift, count):
     parts, _, rows, ny = drift.shape
     nx = parts * rows
     whole = (3, nx, ny)
     dma = pltpu.SemaphoreType.DMA
     return pl.pallas_call(
         functools.partial(join_kernel, count),
-        in_specs=[SMEM, SMALL] + [HBM] * 9 + [SMALL] * 2,
+        in_specs=[SMEM, SMALL] + [HBM] * 5 + [SMALL] * 2,
         out_specs=[SMALL, SMALL, SMALL],
         out_shape=[pltpu.VMEM(whole, f32), pltpu.VMEM(whole, f32), jax.ShapeDtypeStruct((2 * parts, 1, LANES), f32)],
-        scratch_shapes=[pltpu.VMEM(whole, f32), pltpu.VMEM(whole, bf16), pltpu.VMEM((nx, ny), jnp.int32),
-                        pltpu.VMEM(whole, bf16), pltpu.VMEM((2, nx, ny), bf16),
-                        pltpu.VMEM((count, 8, ny), f32), dma((8 * CHUNKS,)), dma((1,))],
+        scratch_shapes=[pltpu.VMEM(whole, bf16), pltpu.VMEM((nx, ny), jnp.int32), pltpu.VMEM((nx, ny), bf16),
+                        pltpu.VMEM((count, 8, ny), f32), dma((4 * CHUNKS,)), dma((1,))],
         compiler_params=params(),
         cost_estimate=pl.CostEstimate(flops=100 * nx * ny, bytes_accessed=8 * 1024 * 1024, transcendentals=0),
         name="join",
-    )(scal, early, far_off(part), far_off(wind), far_off(classes), far_off(adj),
-      *[far_off(a) for a in near + far[:2]], near_by(far[2]), near_by(drift))
+    )(scal, early, *[far_off(a) for a in (part, wind, classes, adj, far[0])], near_by(far[1]), near_by(drift))
 
 
 def merge(rows, count):
@@ -406,9 +451,10 @@
     near = [lax.ppermute(low, "gz", pair) for low in lows]
     far = [lax.ppermute(low, "gz", onward) for low in near]
 
-    part, early = x_part(scal, drag_coef, jnp.asarray(fx), jnp.asarray(inv_x), lows, adj, wnd, classes)
+    part = x_part(scal, jnp.asarray(fx), jnp.asarray(inv_x), lows, wnd)
     drift = swap(y_part(part, recv, jnp.asarray(line_tables(total_y))), "gy")
-    rhs, adj, sums = join(scal, gate(early, far), part, wnd, classes, adj, near, far, drift, count)
+    part, early = local_part(scal, drag_coef, part, wnd, classes, adj, near, far[0])
+    rhs, adj, sums = join(scal, gate(early, far), part, wnd, classes, adj, far[1:], drift, count)
 
     group, pairs = 2 * gy, gz // 2
     within = [[k * group + i for i in range(group)] for k in range(pairs)]

time: 113 us -> 112 us (level)
  waiting for transfers between devices: 24.7 us -> 19.7 us
  Pallas kernels: 22.8 us -> 26.2 us
    ppermute x3, waiting for transfers between devices: 7.48 us -> 0.3 us  [local(): far = [lax.ppermute(low, 'gz', onward) for low in near]]
    pallas_call x1 -> x2, Pallas kernels: 11.3 us -> 15.1 us  [the longest x1 8.61 us: x_part(): pl.pallas_call(x_kernel, in_specs=[SMEM] + [HBM] * 6, out_specs=HBM, out_...]
    all_to_all x2, waiting for transfers between devices: 13.8 us -> 16 us  [swap(): lax.all_to_all(x, axes, split_axis=0, concat_axis=0, axis_index_groups=gr...]
  transfers between devices with their start and end apart: 8 -> 8, of which waited for: 5 -> 4; matrix products, arithmetic and copies ran while one was open for 0% -> 0% of each run, Pallas kernels for 13% -> 16%
where the time goes in v5:
time: 112 us
  blocking collectives  32.6 us (29%)
  starting transfers between devices  31.2 us (28%)
  Pallas kernels  26.2 us (23%)
  waiting for transfers between devices  19.7 us (18%)
  local copies, waits for them, and re-layouts  1.12 us (1%)
    all_to_all x2, blocking collectives, swap(): lax.all_to_all(x, axes, split_axis=0, concat_axis=0, axis_index_groups=gr...  32.6 us
    all_to_all x2, waiting for transfers between devices, swap(): lax.all_to_all(x, axes, split_axis=0, concat_axis=0, axis_index_groups=gr...  16 us
    all_to_all x2, starting transfers between devices, swap(): lax.all_to_all(x, axes, split_axis=0, concat_axis=0, axis_index_groups=gr...  15 us
    ppermute x3, starting transfers between devices, local(): far = [lax.ppermute(low, 'gz', onward) for low in near]  8.95 us
    pallas_call x1, Pallas kernels, x_part(): pl.pallas_call(x_kernel, in_specs=[SMEM] + [HBM] * 6, out_specs=HBM, out_...  8.61 us
    ppermute x3, starting transfers between devices, local(): near = [lax.ppermute(low, 'gz', pair) for low in lows]  7.19 us
    pallas_call x1, Pallas kernels, local_part(): pl.pallas_call(functools.partial(local_kernel, count), in_specs=[SMEM, SM...  6.45 us
    pallas_call x1, Pallas kernels, join(): pl.pallas_call(functools.partial(join_kernel, count), in_specs=[SMEM, SMA...  3.49 us
  transfers between devices with their start and end apart: 8, of which 4 were waited for; matrix products, arithmetic and copies ran while one was open for 0% of the time, Pallas kernels for 16%

profile of v5, /device:TPU:1, one launch (start us, length us, event | category | flops | bytes accessed | tf_op | source)
XLA Modules:
  0.0 111.7 jit_solution(15463876578655483387)
XLA Ops:
  0.6 2.5 %pack.1 = (bf16[8,4,128,128]{3,2,1,0:T(8,128)(2,1)}, bf16[1024,128]{1,0:T(8,128)(2,1)}, bf16[1024,128]{1,0:T(8,128)(2,1)}, bf16[1024,128]{1,0:T(8,128)(2,1)}) custom-call(f32[3,1024,128]{2,1,0:T(8,128)} %bitcast.8, bf16[3,1024,128]{2,1,0:T(8,128)(2,1)} %bitcast.11), custom_call_target="tpu_custom_call" | custom-call | bytes 4194304 | tf_op jit(solution)/shard_map/pack/pallas_call | solution.py:120
  3.2 10.5 %all-to-all-start = ((bf16[8,4,128,128]{3,2,1,0:T(8,128)(2,1)}), bf16[8,4,128,128]{3,2,1,0:T(8,128)(2,1)S(1)}, u32[]{:S(2)}, u32[]{:S(2)}) async-start(bf16[8,4,128,128]{3,2,1,0:T(8,128)(2,1)} %get-tuple-element.18), calls=%async_computation | async-start | bytes 2097152 | tf_op jit(solution)/shard_map/all_to_all | solution.py:427
  13.7 1.9 %collective-permute-start = (bf16[1024,128]{1,0:T(8,128)(2,1)S(1)}, bf16[1024,128]{1,0:T(8,128)(2,1)S(1)}, u32[]{:S(2)}, u32[]{:S(2)}) collective-permute-start(bf16[1024,128]{1,0:T(8,128)(2,1)S(1)} %copy-done.6), channel_id=1, source_target_pairs={{0,8},{8,0},{16,24},{24,16},{32,40},{40,32},{48,56},{56,48},{64,72... | collective-permute-start | bytes 786440 | tf_op jit(solution)/shard_map/ppermute | solution.py:451
  15.6 3.4 %collective-permute-start.1 = (bf16[1024,128]{1,0:T(8,128)(2,1)S(1)}, bf16[1024,128]{1,0:T(8,128)(2,1)S(1)}, u32[]{:S(2)}, u32[]{:S(2)}) collective-permute-start(bf16[1024,128]{1,0:T(8,128)(2,1)S(1)} %copy-done.5), channel_id=1, source_target_pairs={{0,8},{8,0},{16,24},{24,16},{32,40},{40,32},{48,56},{56,48},{64,72... | collective-permute-start | bytes 786440 | tf_op jit(solution)/shard_map/ppermute | solution.py:451
  19.0 1.9 %collective-permute-start.2 = (bf16[1024,128]{1,0:T(8,128)(2,1)S(1)}, bf16[1024,128]{1,0:T(8,128)(2,1)S(1)}, u32[]{:S(2)}, u32[]{:S(2)}) collective-permute-start(bf16[1024,128]{1,0:T(8,128)(2,1)S(1)} %copy-done.4), channel_id=1, source_target_pairs={{0,8},{8,0},{16,24},{24,16},{32,40},{40,32},{48,56},{56,48},{64,72... | collective-permute-start | bytes 786440 | tf_op jit(solution)/shard_map/ppermute | solution.py:451
  20.9 0.1 pad_maximum_fusion.after.scal
  21.0 8.6 %x_part.1.part.after = f32[3,1024,128]{2,1,0:T(8,128)} custom-call(f32[2]{0:T(128)S(1)} %pad_maximum_fusion.after.scal, bf16[1024,1024]{1,0:T(8,128)(2,1)} %constant.37.clone.fwd, bf16[4,512,1024]{2,1,0:T(8,128)(2,1)} %constant.38.clone.inv, bf16[1024,128]{1,0:T(8,128)(2,1)} %get-tuple-element.13.l0, bf16[1024,128]{1,0:T(8,128)(2,1)} %get-tuple-element.14.l1, ...), custom_call_target="tpu_custom_call" | custom-call | flops 2415919104 | bytes 12582912 | tf_op jit(solution)/shard_map/x_part/pallas_call | solution.py:181
  29.6 10.5 %all-to-all-done.recv = bf16[8,4,128,128]{3,2,1,0:T(8,128)(2,1)S(1)} async-done(((bf16[8,4,128,128]{3,2,1,0:T(8,128)(2,1)}), bf16[8,4,128,128]{3,2,1,0:T(8,128)(2,1)S(1)}, u32[]{:S(2)}, u32[]{:S(2)}) %all-to-all-start) | async-done | bytes 1048608 | tf_op jit(solution)/shard_map/all_to_all | solution.py:427
  40.1 3.3 %y_part.1 = bf16[8,3,128,128]{3,2,1,0:T(8,128)(2,1)} custom-call(f32[3,1024,128]{2,1,0:T(8,128)} %x_part.1.part.after, bf16[8,4,128,128]{3,2,1,0:T(8,128)(2,1)S(1)} %all-to-all-done.recv, bf16[2,4,512,256]{3,2,1,0:T(8,128)(2,1)} %constant.39.clone.table), custom_call_target="tpu_custom_call" | custom-call | flops 805306368 | bytes 4194304 | tf_op jit(solution)/shard_map/y_part/pallas_call | solution.py:233
  43.4 0.0 copy-start
  43.4 4.5 %all-to-all-start.1 = ((bf16[8,3,128,128]{3,2,1,0:T(8,128)(2,1)}), bf16[8,3,128,128]{3,2,1,0:T(8,128)(2,1)S(1)}, u32[]{:S(2)}, u32[]{:S(2)}) async-start(bf16[8,3,128,128]{3,2,1,0:T(8,128)(2,1)} %y_part.1), calls=%async_computation.1 | async-start | bytes 1572864 | tf_op jit(solution)/shard_map/all_to_all | solution.py:427
  48.0 3.1 %collective-permute-start.3 = (bf16[1024,128]{1,0:T(8,128)(2,1)S(1)}, bf16[1024,128]{1,0:T(8,128)(2,1)S(1)}, u32[]{:S(2)}, u32[]{:S(2)}) collective-permute-start(bf16[1024,128]{1,0:T(8,128)(2,1)S(1)} %collective-permute-done.p0), channel_id=1, source_target_pairs={{0,16},{16,32},{32,48},{48,64},{64,80},{80,96},{96,112},{112,128},... | collective-permute-start | bytes 786440 | tf_op jit(solution)/shard_map/ppermute | solution.py:452
  51.1 3.1 %collective-permute-start.4 = (bf16[1024,128]{1,0:T(8,128)(2,1)S(1)}, bf16[1024,128]{1,0:T(8,128)(2,1)S(1)}, u32[]{:S(2)}, u32[]{:S(2)}) collective-permute-start(bf16[1024,128]{1,0:T(8,128)(2,1)S(1)} %collective-permute-done.1.p1), channel_id=1, source_target_pairs={{0,16},{16,32},{32,48},{48,64},{64,80},{80,96},{96,112},{112,128},... | collective-permute-start | bytes 786440 | tf_op jit(solution)/shard_map/ppermute | solution.py:452
  54.3 3.4 %collective-permute-done.2.p2 = bf16[1024,128]{1,0:T(8,128)(2,1)S(1)} collective-permute-done((bf16[1024,128]{1,0:T(8,128)(2,1)S(1)}, bf16[1024,128]{1,0:T(8,128)(2,1)S(1)}, u32[]{:S(2)}, u32[]{:S(2)}) %collective-permute-start.2) | collective-permute-done | bytes 262176 | tf_op jit(solution)/shard_map/ppermute | solution.py:451
  57.7 2.7 %collective-permute-start.5 = (bf16[1024,128]{1,0:T(8,128)(2,1)S(1)}, bf16[1024,128]{1,0:T(8,128)(2,1)S(1)}, u32[]{:S(2)}, u32[]{:S(2)}) collective-permute-start(bf16[1024,128]{1,0:T(8,128)(2,1)S(1)} %collective-permute-done.2.p2), channel_id=1, source_target_pairs={{0,16},{16,32},{32,48},{48,64},{64,80},{80,96},{96,112},{112,128},... | collective-permute-start | bytes 786440 | tf_op jit(solution)/shard_map/ppermute | solution.py:452
  60.4 0.7 copy-done.8
  61.1 6.5 %local_part.1 = (f32[3,1024,128]{2,1,0:T(8,128)}, f32[1,128]{1,0:T(1,128)S(1)}) custom-call(f32[2]{0:T(128)S(1)} %pad_maximum_fusion.after.scal, f32[16]{0:T(128)S(1)} %copy-done, f32[3,1024,128]{2,1,0:T(8,128)} %x_part.1.part.after, bf16[3,1024,128]{2,1,0:T(8,128)(2,1)} %bitcast.13, s32[1024,128]{1,0:T(8,128)} %classes.3, f32[3,1024,128]{2,1,0:T(8,128)} %bitcast.9, ...), custom_call_target="tpu_custom_call" | custom-call | flops 26214400 | bytes 8388608 | tf_op jit(solution)/shard_map/local_part/pallas_call | solution.py:313
  67.6 0.3 collective-permute-done.5.q2
  67.9 0.4 copy-done.7
  68.3 5.5 %all-to-all-done.1.drift = bf16[8,3,128,128]{3,2,1,0:T(8,128)(2,1)S(1)} async-done(((bf16[8,3,128,128]{3,2,1,0:T(8,128)(2,1)}), bf16[8,3,128,128]{3,2,1,0:T(8,128)(2,1)S(1)}, u32[]{:S(2)}, u32[]{:S(2)}) %all-to-all-start.1) | async-done | bytes 786464 | tf_op jit(solution)/shard_map/all_to_all | solution.py:427
  73.8 3.5 %join.1 = (f32[3,1024,128]{2,1,0:T(8,128)S(1)}, f32[3,1024,128]{2,1,0:T(8,128)S(1)}, f32[16,1,128]{2,1,0:T(1,128)S(1)}) custom-call(f32[2]{0:T(128)S(1)} %pad_maximum_fusion.after.scal, f32[1,128]{1,0:T(1,128)S(1)} %gate.1.early, f32[3,1024,128]{2,1,0:T(8,128)} %get-tuple-element.17.part, bf16[3,1024,128]{2,1,0:T(8,128)(2,1)} %bitcast.14, ...), custom_call_target="tpu_custom_call" | custom-call | flops 13107200 | bytes 8388608 | tf_op jit(solution)/shard_map/join/pallas_call | solution.py:363
  77.3 11.1 %all_to_all.20.got = f32[16,1,128]{2,1,0:T(1,128)S(1)} all-to-all(f32[16,1,128]{2,1,0:T(1,128)S(1)} %get-tuple-element.19), channel_id=1, replica_groups={{0,1,2,3,4,5,6,7,8,9,10,11,12,13,14,15},{16,17,18,19,20,21,22,23,24,25,..., dimensions={0} | all-to-all | bytes 16384 | tf_op jit(solution)/shard_map/all_to_all | solution.py:427
  88.4 21.5 %all_to_all.21.got = f32[32,1,128]{2,1,0:T(1,128)S(1)} all-to-all(f32[32,1,128]{2,1,0:T(1,128)S(1)} %fold.1), channel_id=1, replica_groups={{0,16,32,48,64,80,96,112,128,144,160,176,192,208,224,240,256,272,288,30..., dimensions={0} | all-to-all | bytes 32768 | tf_op jit(solution)/shard_map/all_to_all | solution.py:427
  109.9 1.8 %finish.1 = (f32[3,1024,128]{2,1,0:T(8,128)}, f32[1,16]{1,0:T(1,128)}) custom-call(f32[32,1,128]{2,1,0:T(1,128)S(1)} %all_to_all.21.got, f32[3,1024,128]{2,1,0:T(8,128)S(1)} %get-tuple-element.20.adj, f32[3,1024,128]{2,1,0:T(8,128)S(1)} %get-tuple-element.21.rhs), custom_call_target="tpu_custom_call" | custom-call | flops 786432 | bytes 4718592 | tf_op jit(solution)/shard_map/finish/pallas_call | solution.py:414
  (21 shorter events, 0.1 us)
Async XLA Ops:
  3.1 10.5 %copy-start.6 = (bf16[1024,128]{1,0:T(8,128)(2,1)S(1)}, bf16[1024,128]{1,0:T(8,128)(2,1)}, u32[]{:S(2)}) copy-start(bf16[1024,128]{1,0:T(8,128)(2,1)} %get-tuple-element.13.l0) | copy-start | bytes 786436
  3.1 12.4 %copy-start.5 = (bf16[1024,128]{1,0:T(8,128)(2,1)S(1)}, bf16[1024,128]{1,0:T(8,128)(2,1)}, u32[]{:S(2)}) copy-start(bf16[1024,128]{1,0:T(8,128)(2,1)} %get-tuple-element.14.l1) | copy-start | bytes 786436
  3.2 15.8 %copy-start.4 = (bf16[1024,128]{1,0:T(8,128)(2,1)S(1)}, bf16[1024,128]{1,0:T(8,128)(2,1)}, u32[]{:S(2)}) copy-start(bf16[1024,128]{1,0:T(8,128)(2,1)} %get-tuple-element.15.l2) | copy-start | bytes 786436
  3.2 37.0 %all-to-all-start = ((bf16[8,4,128,128]{3,2,1,0:T(8,128)(2,1)}), bf16[8,4,128,128]{3,2,1,0:T(8,128)(2,1)S(1)}, u32[]{:S(2)}, u32[]{:S(2)}) async-start(bf16[8,4,128,128]{3,2,1,0:T(8,128)(2,1)} %get-tuple-element.18), calls=%async_computation | async-start | bytes 2097152 | tf_op jit(solution)/shard_map/all_to_all | solution.py:427
  13.7 34.3 %collective-permute-start = (bf16[1024,128]{1,0:T(8,128)(2,1)S(1)}, bf16[1024,128]{1,0:T(8,128)(2,1)S(1)}, u32[]{:S(2)}, u32[]{:S(2)}) collective-permute-start(bf16[1024,128]{1,0:T(8,128)(2,1)S(1)} %copy-done.6), channel_id=1, source_target_pairs={{0,8},{8,0},{16,24},{24,16},{32,40},{40,32},{48,56},{56,48},{64,72... | collective-permute-start | bytes 786440 | tf_op jit(solution)/shard_map/ppermute | solution.py:451
  15.6 35.5 %collective-permute-start.1 = (bf16[1024,128]{1,0:T(8,128)(2,1)S(1)}, bf16[1024,128]{1,0:T(8,128)(2,1)S(1)}, u32[]{:S(2)}, u32[]{:S(2)}) collective-permute-start(bf16[1024,128]{1,0:T(8,128)(2,1)S(1)} %copy-done.5), channel_id=1, source_target_pairs={{0,8},{8,0},{16,24},{24,16},{32,40},{40,32},{48,56},{56,48},{64,72... | collective-permute-start | bytes 786440 | tf_op jit(solution)/shard_map/ppermute | solution.py:451
  19.0 38.7 %collective-permute-start.2 = (bf16[1024,128]{1,0:T(8,128)(2,1)S(1)}, bf16[1024,128]{1,0:T(8,128)(2,1)S(1)}, u32[]{:S(2)}, u32[]{:S(2)}) collective-permute-start(bf16[1024,128]{1,0:T(8,128)(2,1)S(1)} %copy-done.4), channel_id=1, source_target_pairs={{0,8},{8,0},{16,24},{24,16},{32,40},{40,32},{48,56},{56,48},{64,72... | collective-permute-start | bytes 786440 | tf_op jit(solution)/shard_map/ppermute | solution.py:451
  43.4 17.7 %copy-start = (f32[16]{0:T(128)S(1)}, f32[16]{0:T(128)}, u32[]{:S(2)}) copy-start(f32[16]{0:T(128)} %coef.1) | copy-start | bytes 196
  43.4 30.4 %all-to-all-start.1 = ((bf16[8,3,128,128]{3,2,1,0:T(8,128)(2,1)}), bf16[8,3,128,128]{3,2,1,0:T(8,128)(2,1)S(1)}, u32[]{:S(2)}, u32[]{:S(2)}) async-start(bf16[8,3,128,128]{3,2,1,0:T(8,128)(2,1)} %y_part.1), calls=%async_computation.1 | async-start | bytes 1572864 | tf_op jit(solution)/shard_map/all_to_all | solution.py:427
  48.0 12.4 %copy-start.1 = (bf16[1024,128]{1,0:T(8,128)(2,1)}, bf16[1024,128]{1,0:T(8,128)(2,1)S(1)}, u32[]{:S(2)}) copy-start(bf16[1024,128]{1,0:T(8,128)(2,1)S(1)} %collective-permute-done.p0) | copy-start | bytes 786436
  48.0 12.4 %collective-permute-start.3 = (bf16[1024,128]{1,0:T(8,128)(2,1)S(1)}, bf16[1024,128]{1,0:T(8,128)(2,1)S(1)}, u32[]{:S(2)}, u32[]{:S(2)}) collective-permute-start(bf16[1024,128]{1,0:T(8,128)(2,1)S(1)} %collective-permute-done.p0), channel_id=1, source_target_pairs={{0,16},{16,32},{32,48},{48,64},{64,80},{80,96},{96,112},{112,128},... | collective-permute-start | bytes 786440 | tf_op jit(solution)/shard_map/ppermute | solution.py:452
  51.1 9.3 %copy-start.2 = (bf16[1024,128]{1,0:T(8,128)(2,1)}, bf16[1024,128]{1,0:T(8,128)(2,1)S(1)}, u32[]{:S(2)}) copy-start(bf16[1024,128]{1,0:T(8,128)(2,1)S(1)} %collective-permute-done.1.p1) | copy-start | bytes 786436
  51.1 16.4 %collective-permute-start.4 = (bf16[1024,128]{1,0:T(8,128)(2,1)S(1)}, bf16[1024,128]{1,0:T(8,128)(2,1)S(1)}, u32[]{:S(2)}, u32[]{:S(2)}) collective-permute-start(bf16[1024,128]{1,0:T(8,128)(2,1)S(1)} %collective-permute-done.1.p1), channel_id=1, source_target_pairs={{0,16},{16,32},{32,48},{48,64},{64,80},{80,96},{96,112},{112,128},... | collective-permute-start | bytes 786440 | tf_op jit(solution)/shard_map/ppermute | solution.py:452
  57.7 2.8 %copy-start.3 = (bf16[1024,128]{1,0:T(8,128)(2,1)}, bf16[1024,128]{1,0:T(8,128)(2,1)S(1)}, u32[]{:S(2)}) copy-start(bf16[1024,128]{1,0:T(8,128)(2,1)S(1)} %collective-permute-done.2.p2) | copy-start | bytes 786436
  57.7 10.2 %collective-permute-start.5 = (bf16[1024,128]{1,0:T(8,128)(2,1)S(1)}, bf16[1024,128]{1,0:T(8,128)(2,1)S(1)}, u32[]{:S(2)}, u32[]{:S(2)}) collective-permute-start(bf16[1024,128]{1,0:T(8,128)(2,1)S(1)} %collective-permute-done.2.p2), channel_id=1, source_target_pairs={{0,16},{16,32},{32,48},{48,64},{64,80},{80,96},{96,112},{112,128},... | collective-permute-start | bytes 786440 | tf_op jit(solution)/shard_map/ppermute | solution.py:452
  60.4 0.7 copy-start.8
  67.6 0.7 copy-start.7

commit v6 on v5

--- a/solution.py
+++ b/solution.py
@@ -193,10 +193,9 @@
     )(after, far_off(fwd), far_off(inv), *[far_off(low) for low in lows], far_off(wind))
 
 
-def y_kernel(after, recv, table, out, plus, minus, table_v, out_v, sem_t, sem_o):
+def y_kernel(after, recv, table_v, out, plus, minus, out_v, sem_o):
     parts, _, rows, ny = recv.shape
-    half, steps = parts // 2, table.shape[0]
-    tiles = begin([(table.at[t], table_v.at[t]) for t in range(steps)], sem_t)
+    half, steps = parts // 2, table_v.shape[0]
     for s in range(half):
         for c in range(3):
             u, v = recv[s, c].astype(f32), recv[s + half, c].astype(f32)
@@ -206,7 +205,6 @@
     per = TILE // ny
     stores = []
     for t in range(steps):
-        tiles[t].wait()
         p1, q1 = dot(plus[...], table_v[t, 0]), dot(minus[...], table_v[t, 1])
         p2, q2 = dot(plus[...], table_v[t, 2]), dot(minus[...], table_v[t, 3])
         for s in range(per):
@@ -232,15 +230,15 @@
     dma = pltpu.SemaphoreType.DMA
     return pl.pallas_call(
         y_kernel,
-        in_specs=[HBM, SMALL, HBM],
+        in_specs=[HBM, SMALL, SMALL],
         out_specs=HBM,
         out_shape=pltpu.HBM(sent, bf16),
         scratch_shapes=[pltpu.VMEM((3 * rows, n // 2), bf16), pltpu.VMEM((3 * rows, n // 2), bf16),
-                        pltpu.VMEM(table.shape, bf16), pltpu.VMEM(sent, bf16), dma((steps,)), dma((2 * steps,))],
+                        pltpu.VMEM(sent, bf16), dma((2 * steps,))],
         compiler_params=params(),
         cost_estimate=pl.CostEstimate(flops=2 * n * n * 3 * rows, bytes_accessed=4 * 1024 * 1024, transcendentals=0),
         name="y_part",
-    )(far_off(after), near_by(recv), far_off(table))
+    )(far_off(after), near_by(recv), near_by(table))
 
 
 def gate_kernel(early, q0, q1, q2, out):

time: 112 us -> 111 us (level)
  Pallas kernels: 26.2 us -> 24.9 us
  waiting for transfers between devices: 19.7 us -> 20.9 us
    ppermute x3, waiting for transfers between devices: 3.4 us -> 4.91 us  [local(): near = [lax.ppermute(low, 'gz', pair) for low in lows]]
    pallas_call x1, Pallas kernels: 3.29 us -> 1.89 us  [y_part(): pl.pallas_call(y_kernel, in_specs=[HBM, SMALL, SMALL], out_specs=HBM, out...]
  transfers between devices with their start and end apart: 8 -> 8, of which waited for: 4 -> 3; matrix products, arithmetic and copies ran while one was open for 0% -> 0% of each run, Pallas kernels for 16% -> 15%
where the time goes in v6:
time: 111 us
  blocking collectives  31.5 us (28%)
  starting transfers between devices  30.9 us (28%)
  Pallas kernels  24.9 us (22%)
  waiting for transfers between devices  20.9 us (19%)
  local copies, waits for them, and re-layouts  1.41 us (1%)
    all_to_all x2, blocking collectives, swap(): lax.all_to_all(x, axes, split_axis=0, concat_axis=0, axis_index_groups=gr...  31.5 us
    all_to_all x2, waiting for transfers between devices, swap(): lax.all_to_all(x, axes, split_axis=0, concat_axis=0, axis_index_groups=gr...  16 us
    all_to_all x2, starting transfers between devices, swap(): lax.all_to_all(x, axes, split_axis=0, concat_axis=0, axis_index_groups=gr...  14.9 us
    ppermute x3, starting transfers between devices, local(): far = [lax.ppermute(low, 'gz', onward) for low in near]  8.86 us
    pallas_call x1, Pallas kernels, x_part(): pl.pallas_call(x_kernel, in_specs=[SMEM] + [HBM] * 6, out_specs=HBM, out_...  8.7 us
    ppermute x3, starting transfers between devices, local(): near = [lax.ppermute(low, 'gz', pair) for low in lows]  7.19 us
    pallas_call x1, Pallas kernels, local_part(): pl.pallas_call(functools.partial(local_kernel, count), in_specs=[SMEM, SM...  6.46 us
    ppermute x3, waiting for transfers between devices, local(): near = [lax.ppermute(low, 'gz', pair) for low in lows]  4.91 us
  transfers between devices with their start and end apart: 8, of which 3 were waited for; matrix products, arithmetic and copies ran while one was open for 0% of the time, Pallas kernels for 15%

profile of v6, /device:TPU:1, one launch (start us, length us, event | category | flops | bytes accessed | tf_op | source)
XLA Modules:
  0.0 110.5 jit_solution(16055133027722057027)
XLA Ops:
  0.6 2.5 %pack.1 = (bf16[8,4,128,128]{3,2,1,0:T(8,128)(2,1)}, bf16[1024,128]{1,0:T(8,128)(2,1)}, bf16[1024,128]{1,0:T(8,128)(2,1)}, bf16[1024,128]{1,0:T(8,128)(2,1)}) custom-call(f32[3,1024,128]{2,1,0:T(8,128)} %bitcast.8, bf16[3,1024,128]{2,1,0:T(8,128)(2,1)} %bitcast.11), custom_call_target="tpu_custom_call" | custom-call | bytes 4194304 | tf_op jit(solution)/shard_map/pack/pallas_call | solution.py:120
  3.2 10.3 %all-to-all-start = ((bf16[8,4,128,128]{3,2,1,0:T(8,128)(2,1)}), bf16[8,4,128,128]{3,2,1,0:T(8,128)(2,1)S(1)}, u32[]{:S(2)}, u32[]{:S(2)}) async-start(bf16[8,4,128,128]{3,2,1,0:T(8,128)(2,1)} %get-tuple-element.18), calls=%async_computation | async-start | bytes 2097152 | tf_op jit(solution)/shard_map/all_to_all | solution.py:425
  13.5 1.9 %collective-permute-start = (bf16[1024,128]{1,0:T(8,128)(2,1)}, bf16[1024,128]{1,0:T(8,128)(2,1)S(1)}, u32[]{:S(2)}, u32[]{:S(2)}) collective-permute-start(bf16[1024,128]{1,0:T(8,128)(2,1)} %get-tuple-element.13.l0), channel_id=1, source_target_pairs={{0,8},{8,0},{16,24},{24,16},{32,40},{40,32},{48,56},{56,48},{64,72... | collective-permute-start | bytes 786440 | tf_op jit(solution)/shard_map/ppermute | solution.py:449
  15.4 3.4 %collective-permute-start.1 = (bf16[1024,128]{1,0:T(8,128)(2,1)}, bf16[1024,128]{1,0:T(8,128)(2,1)}, u32[]{:S(2)}, u32[]{:S(2)}) collective-permute-start(bf16[1024,128]{1,0:T(8,128)(2,1)} %get-tuple-element.14.l1), channel_id=1, source_target_pairs={{0,8},{8,0},{16,24},{24,16},{32,40},{40,32},{48,56},{56,48},{64,72... | collective-permute-start | bytes 786440 | tf_op jit(solution)/shard_map/ppermute | solution.py:449
  18.8 1.9 %collective-permute-start.2 = (bf16[1024,128]{1,0:T(8,128)(2,1)}, bf16[1024,128]{1,0:T(8,128)(2,1)}, u32[]{:S(2)}, u32[]{:S(2)}) collective-permute-start(bf16[1024,128]{1,0:T(8,128)(2,1)} %get-tuple-element.15.l2), channel_id=1, source_target_pairs={{0,8},{8,0},{16,24},{24,16},{32,40},{40,32},{48,56},{56,48},{64,72... | collective-permute-start | bytes 786440 | tf_op jit(solution)/shard_map/ppermute | solution.py:449
  20.8 0.1 pad_maximum_fusion.after.scal
  20.9 8.7 %x_part.1.part.after = f32[3,1024,128]{2,1,0:T(8,128)} custom-call(f32[2]{0:T(128)S(1)} %pad_maximum_fusion.after.scal, bf16[1024,1024]{1,0:T(8,128)(2,1)} %constant.37.clone.fwd, bf16[4,512,1024]{2,1,0:T(8,128)(2,1)} %constant.38.clone.inv, bf16[1024,128]{1,0:T(8,128)(2,1)} %get-tuple-element.13.l0, bf16[1024,128]{1,0:T(8,128)(2,1)} %get-tuple-element.14.l1, ...), custom_call_target="tpu_custom_call" | custom-call | flops 2415919104 | bytes 12582912 | tf_op jit(solution)/shard_map/x_part/pallas_call | solution.py:181
  29.6 10.4 %all-to-all-done.recv = bf16[8,4,128,128]{3,2,1,0:T(8,128)(2,1)S(1)} async-done(((bf16[8,4,128,128]{3,2,1,0:T(8,128)(2,1)}), bf16[8,4,128,128]{3,2,1,0:T(8,128)(2,1)S(1)}, u32[]{:S(2)}, u32[]{:S(2)}) %all-to-all-start) | async-done | bytes 1048608 | tf_op jit(solution)/shard_map/all_to_all | solution.py:425
  40.0 1.9 %y_part.1 = bf16[8,3,128,128]{3,2,1,0:T(8,128)(2,1)} custom-call(f32[3,1024,128]{2,1,0:T(8,128)} %x_part.1.part.after, bf16[8,4,128,128]{3,2,1,0:T(8,128)(2,1)S(1)} %all-to-all-done.recv, bf16[2,4,512,256]{3,2,1,0:T(8,128)(2,1)S(1)} %copy-done), custom_call_target="tpu_custom_call" | custom-call | flops 805306368 | bytes 4194304 | tf_op jit(solution)/shard_map/y_part/pallas_call | solution.py:231
  41.9 0.0 copy-start.1
  41.9 4.5 %all-to-all-start.1 = ((bf16[8,3,128,128]{3,2,1,0:T(8,128)(2,1)}), bf16[8,3,128,128]{3,2,1,0:T(8,128)(2,1)S(1)}, u32[]{:S(2)}, u32[]{:S(2)}) async-start(bf16[8,3,128,128]{3,2,1,0:T(8,128)(2,1)} %y_part.1), calls=%async_computation.1 | async-start | bytes 1572864 | tf_op jit(solution)/shard_map/all_to_all | solution.py:425
  46.5 3.1 %collective-permute-start.3 = (bf16[1024,128]{1,0:T(8,128)(2,1)S(1)}, bf16[1024,128]{1,0:T(8,128)(2,1)S(1)}, u32[]{:S(2)}, u32[]{:S(2)}) collective-permute-start(bf16[1024,128]{1,0:T(8,128)(2,1)S(1)} %collective-permute-done.p0), channel_id=1, source_target_pairs={{0,16},{16,32},{32,48},{48,64},{64,80},{80,96},{96,112},{112,128},... | collective-permute-start | bytes 786440 | tf_op jit(solution)/shard_map/ppermute | solution.py:450
  49.6 3.1 %collective-permute-start.4 = (bf16[1024,128]{1,0:T(8,128)(2,1)}, bf16[1024,128]{1,0:T(8,128)(2,1)S(1)}, u32[]{:S(2)}, u32[]{:S(2)}) collective-permute-start(bf16[1024,128]{1,0:T(8,128)(2,1)} %collective-permute-done.1.p1), channel_id=1, source_target_pairs={{0,16},{16,32},{32,48},{48,64},{64,80},{80,96},{96,112},{112,128},... | collective-permute-start | bytes 786440 | tf_op jit(solution)/shard_map/ppermute | solution.py:450
  52.7 4.9 %collective-permute-done.2.p2 = bf16[1024,128]{1,0:T(8,128)(2,1)} collective-permute-done((bf16[1024,128]{1,0:T(8,128)(2,1)}, bf16[1024,128]{1,0:T(8,128)(2,1)}, u32[]{:S(2)}, u32[]{:S(2)}) %collective-permute-start.2) | collective-permute-done | bytes 262176 | tf_op jit(solution)/shard_map/ppermute | solution.py:449
  57.6 2.6 %collective-permute-start.5 = (bf16[1024,128]{1,0:T(8,128)(2,1)}, bf16[1024,128]{1,0:T(8,128)(2,1)S(1)}, u32[]{:S(2)}, u32[]{:S(2)}) collective-permute-start(bf16[1024,128]{1,0:T(8,128)(2,1)} %collective-permute-done.2.p2), channel_id=1, source_target_pairs={{0,16},{16,32},{32,48},{48,64},{64,80},{80,96},{96,112},{112,128},... | collective-permute-start | bytes 786440 | tf_op jit(solution)/shard_map/ppermute | solution.py:450
  60.3 0.7 copy-done.4
  61.0 6.5 %local_part.1 = (f32[3,1024,128]{2,1,0:T(8,128)}, f32[1,128]{1,0:T(1,128)S(1)}) custom-call(f32[2]{0:T(128)S(1)} %pad_maximum_fusion.after.scal, f32[16]{0:T(128)S(1)} %copy-done.1, f32[3,1024,128]{2,1,0:T(8,128)} %x_part.1.part.after, bf16[3,1024,128]{2,1,0:T(8,128)(2,1)} %bitcast.13, s32[1024,128]{1,0:T(8,128)} %classes.3, f32[3,1024,128]{2,1,0:T(8,128)} %bitcast.9, ...), custom_call_target="tpu_custom_call" | custom-call | flops 26214400 | bytes 8388608 | tf_op jit(solution)/shard_map/local_part/pallas_call | solution.py:311
  67.5 0.0 copy-start.3
  67.5 0.7 copy-done.3
  68.2 5.5 %all-to-all-done.1.drift = bf16[8,3,128,128]{3,2,1,0:T(8,128)(2,1)S(1)} async-done(((bf16[8,3,128,128]{3,2,1,0:T(8,128)(2,1)}), bf16[8,3,128,128]{3,2,1,0:T(8,128)(2,1)S(1)}, u32[]{:S(2)}, u32[]{:S(2)}) %all-to-all-start.1) | async-done | bytes 786464 | tf_op jit(solution)/shard_map/all_to_all | solution.py:425
  73.7 3.5 %join.1 = (f32[3,1024,128]{2,1,0:T(8,128)S(1)}, f32[3,1024,128]{2,1,0:T(8,128)S(1)}, f32[16,1,128]{2,1,0:T(1,128)S(1)}) custom-call(f32[2]{0:T(128)S(1)} %pad_maximum_fusion.after.scal, f32[1,128]{1,0:T(1,128)S(1)} %gate.1.early, f32[3,1024,128]{2,1,0:T(8,128)} %get-tuple-element.17.part, bf16[3,1024,128]{2,1,0:T(8,128)(2,1)} %bitcast.14, ...), custom_call_target="tpu_custom_call" | custom-call | flops 13107200 | bytes 8388608 | tf_op jit(solution)/shard_map/join/pallas_call | solution.py:361
  77.2 11.1 %all_to_all.20.got = f32[16,1,128]{2,1,0:T(1,128)S(1)} all-to-all(f32[16,1,128]{2,1,0:T(1,128)S(1)} %get-tuple-element.19), channel_id=1, replica_groups={{0,1,2,3,4,5,6,7,8,9,10,11,12,13,14,15},{16,17,18,19,20,21,22,23,24,25,..., dimensions={0} | all-to-all | bytes 16384 | tf_op jit(solution)/shard_map/all_to_all | solution.py:425
  88.3 20.4 %all_to_all.21.got = f32[32,1,128]{2,1,0:T(1,128)S(1)} all-to-all(f32[32,1,128]{2,1,0:T(1,128)S(1)} %fold.1), channel_id=1, replica_groups={{0,16,32,48,64,80,96,112,128,144,160,176,192,208,224,240,256,272,288,30..., dimensions={0} | all-to-all | bytes 32768 | tf_op jit(solution)/shard_map/all_to_all | solution.py:425
  108.7 1.8 %finish.1 = (f32[3,1024,128]{2,1,0:T(8,128)}, f32[1,16]{1,0:T(1,128)}) custom-call(f32[32,1,128]{2,1,0:T(1,128)S(1)} %all_to_all.21.got, f32[3,1024,128]{2,1,0:T(8,128)S(1)} %get-tuple-element.20.adj, f32[3,1024,128]{2,1,0:T(8,128)S(1)} %get-tuple-element.21.rhs), custom_call_target="tpu_custom_call" | custom-call | flops 786432 | bytes 4718592 | tf_op jit(solution)/shard_map/finish/pallas_call | solution.py:412
  (13 shorter events, 0.1 us)
Async XLA Ops:
  3.2 36.8 %all-to-all-start = ((bf16[8,4,128,128]{3,2,1,0:T(8,128)(2,1)}), bf16[8,4,128,128]{3,2,1,0:T(8,128)(2,1)S(1)}, u32[]{:S(2)}, u32[]{:S(2)}) async-start(bf16[8,4,128,128]{3,2,1,0:T(8,128)(2,1)} %get-tuple-element.18), calls=%async_computation | async-start | bytes 2097152 | tf_op jit(solution)/shard_map/all_to_all | solution.py:425
  13.5 32.9 %collective-permute-start = (bf16[1024,128]{1,0:T(8,128)(2,1)}, bf16[1024,128]{1,0:T(8,128)(2,1)S(1)}, u32[]{:S(2)}, u32[]{:S(2)}) collective-permute-start(bf16[1024,128]{1,0:T(8,128)(2,1)} %get-tuple-element.13.l0), channel_id=1, source_target_pairs={{0,8},{8,0},{16,24},{24,16},{32,40},{40,32},{48,56},{56,48},{64,72... | collective-permute-start | bytes 786440 | tf_op jit(solution)/shard_map/ppermute | solution.py:449
  15.4 34.2 %collective-permute-start.1 = (bf16[1024,128]{1,0:T(8,128)(2,1)}, bf16[1024,128]{1,0:T(8,128)(2,1)}, u32[]{:S(2)}, u32[]{:S(2)}) collective-permute-start(bf16[1024,128]{1,0:T(8,128)(2,1)} %get-tuple-element.14.l1), channel_id=1, source_target_pairs={{0,8},{8,0},{16,24},{24,16},{32,40},{40,32},{48,56},{56,48},{64,72... | collective-permute-start | bytes 786440 | tf_op jit(solution)/shard_map/ppermute | solution.py:449
  18.8 38.8 %collective-permute-start.2 = (bf16[1024,128]{1,0:T(8,128)(2,1)}, bf16[1024,128]{1,0:T(8,128)(2,1)}, u32[]{:S(2)}, u32[]{:S(2)}) collective-permute-start(bf16[1024,128]{1,0:T(8,128)(2,1)} %get-tuple-element.15.l2), channel_id=1, source_target_pairs={{0,8},{8,0},{16,24},{24,16},{32,40},{40,32},{48,56},{56,48},{64,72... | collective-permute-start | bytes 786440 | tf_op jit(solution)/shard_map/ppermute | solution.py:449
  20.9 19.1 %copy-start = (bf16[2,4,512,256]{3,2,1,0:T(8,128)(2,1)S(1)}, bf16[2,4,512,256]{3,2,1,0:T(8,128)(2,1)}, u32[]{:S(2)}) copy-start(bf16[2,4,512,256]{3,2,1,0:T(8,128)(2,1)} %constant.39.clone.table_v) | copy-start | bytes 6291460
  41.9 19.1 %copy-start.1 = (f32[16]{0:T(128)S(1)}, f32[16]{0:T(128)}, u32[]{:S(2)}) copy-start(f32[16]{0:T(128)} %coef.1) | copy-start | bytes 196
  41.9 31.8 %all-to-all-start.1 = ((bf16[8,3,128,128]{3,2,1,0:T(8,128)(2,1)}), bf16[8,3,128,128]{3,2,1,0:T(8,128)(2,1)S(1)}, u32[]{:S(2)}, u32[]{:S(2)}) async-start(bf16[8,3,128,128]{3,2,1,0:T(8,128)(2,1)} %y_part.1), calls=%async_computation.1 | async-start | bytes 1572864 | tf_op jit(solution)/shard_map/all_to_all | solution.py:425
  46.4 13.8 %copy-start.2 = (bf16[1024,128]{1,0:T(8,128)(2,1)}, bf16[1024,128]{1,0:T(8,128)(2,1)S(1)}, u32[]{:S(2)}) copy-start(bf16[1024,128]{1,0:T(8,128)(2,1)S(1)} %collective-permute-done.p0) | copy-start | bytes 786436
  46.5 13.8 %collective-permute-start.3 = (bf16[1024,128]{1,0:T(8,128)(2,1)S(1)}, bf16[1024,128]{1,0:T(8,128)(2,1)S(1)}, u32[]{:S(2)}, u32[]{:S(2)}) collective-permute-start(bf16[1024,128]{1,0:T(8,128)(2,1)S(1)} %collective-permute-done.p0), channel_id=1, source_target_pairs={{0,16},{16,32},{32,48},{48,64},{64,80},{80,96},{96,112},{112,128},... | collective-permute-start | bytes 786440 | tf_op jit(solution)/shard_map/ppermute | solution.py:450
  49.6 17.9 %collective-permute-start.4 = (bf16[1024,128]{1,0:T(8,128)(2,1)}, bf16[1024,128]{1,0:T(8,128)(2,1)S(1)}, u32[]{:S(2)}, u32[]{:S(2)}) collective-permute-start(bf16[1024,128]{1,0:T(8,128)(2,1)} %collective-permute-done.1.p1), channel_id=1, source_target_pairs={{0,16},{16,32},{32,48},{48,64},{64,80},{80,96},{96,112},{112,128},... | collective-permute-start | bytes 786440 | tf_op jit(solution)/shard_map/ppermute | solution.py:450
  57.6 9.9 %collective-permute-start.5 = (bf16[1024,128]{1,0:T(8,128)(2,1)}, bf16[1024,128]{1,0:T(8,128)(2,1)S(1)}, u32[]{:S(2)}, u32[]{:S(2)}) collective-permute-start(bf16[1024,128]{1,0:T(8,128)(2,1)} %collective-permute-done.2.p2), channel_id=1, source_target_pairs={{0,16},{16,32},{32,48},{48,64},{64,80},{80,96},{96,112},{112,128},... | collective-permute-start | bytes 786440 | tf_op jit(solution)/shard_map/ppermute | solution.py:450
  60.3 0.7 copy-start.4
  67.5 0.7 copy-start.3

commit v7 on v6

--- a/solution.py
+++ b/solution.py
@@ -323,8 +323,8 @@
     )(scal, coef, *[far_off(a) for a in (part, wind, classes, adj, *near, far)])
 
 
-def join_kernel(count, scal, early, part, wind, classes, adj, q1, q2, drift, rhs, adj_v, sums,
-                wind_v, cls_v, far_v, acc, sem_in, sem_adj):
+def join_kernel(count, scal, early, part, wind, classes, q1, q2, drift, rhs, sums,
+                wind_v, cls_v, far_v, acc, sem_in):
     parts, _, rows, _ = drift.shape
     per = parts // CHUNKS
     loads = []
@@ -332,7 +332,6 @@
         at = pl.ds(k * per * rows, per * rows)
         loads.append(begin([(wind.at[:, at], wind_v.at[:, at]), (classes.at[at], cls_v.at[at]),
                             (part.at[:, at], rhs.at[:, at]), (q1.at[at], far_v.at[at])], sem_in, 4 * k))
-    kept = begin([(adj, adj_v)], sem_adj)
     acc[...] = jnp.zeros_like(acc)
     for k in range(CHUNKS):
         finish_all(loads[k])
@@ -350,25 +349,24 @@
                 total += r * w[c]
             class_sums(scal[0] * speed_of(w) * total, cls_v[at], acc, count)
     sums[...] = jnp.broadcast_to((early[...] + to_lanes(acc, count, count))[None], sums.shape)
-    finish_all(kept)
-
-
-def join(scal, early, part, wind, classes, adj, far, drift, count):
+
+
+def join(scal, early, part, wind, classes, far, drift, count):
     parts, _, rows, ny = drift.shape
     nx = parts * rows
     whole = (3, nx, ny)
     dma = pltpu.SemaphoreType.DMA
     return pl.pallas_call(
         functools.partial(join_kernel, count),
-        in_specs=[SMEM, SMALL] + [HBM] * 5 + [SMALL] * 2,
-        out_specs=[SMALL, SMALL, SMALL],
-        out_shape=[pltpu.VMEM(whole, f32), pltpu.VMEM(whole, f32), jax.ShapeDtypeStruct((2 * parts, 1, LANES), f32)],
+        in_specs=[SMEM, SMALL] + [HBM] * 4 + [SMALL] * 2,
+        out_specs=[SMALL, SMALL],
+        out_shape=[pltpu.VMEM(whole, f32), jax.ShapeDtypeStruct((2 * parts, 1, LANES), f32)],
         scratch_shapes=[pltpu.VMEM(whole, bf16), pltpu.VMEM((nx, ny), jnp.int32), pltpu.VMEM((nx, ny), bf16),
-                        pltpu.VMEM((count, 8, ny), f32), dma((4 * CHUNKS,)), dma((1,))],
+                        pltpu.VMEM((count, 8, ny), f32), dma((4 * CHUNKS,))],
         compiler_params=params(),
         cost_estimate=pl.CostEstimate(flops=100 * nx * ny, bytes_accessed=8 * 1024 * 1024, transcendentals=0),
         name="join",
-    )(scal, early, *[far_off(a) for a in (part, wind, classes, adj, far[0])], near_by(far[1]), near_by(drift))
+    )(scal, early, *[far_off(a) for a in (part, wind, classes, far[0])], near_by(far[1]), near_by(drift))
 
 
 def merge(rows, count):
@@ -452,7 +450,7 @@
     part = x_part(scal, jnp.asarray(fx), jnp.asarray(inv_x), lows, wnd)
     drift = swap(y_part(part, recv, jnp.asarray(line_tables(total_y))), "gy")
     part, early = local_part(scal, drag_coef, part, wnd, classes, adj, near, far[0])
-    rhs, adj, sums = join(scal, gate(early, far), part, wnd, classes, adj, far[1:], drift, count)
+    rhs, sums = join(scal, gate(early, far), part, wnd, classes, far[1:], drift, count)
 
     group, pairs = 2 * gy, gz // 2
     within = [[k * group + i for i in range(group)] for k in range(pairs)]

time: 111 us -> 111 us (level)
  no operation moved by 1% of the time
where the time goes in v7:
time: 111 us
  blocking collectives  31.5 us (28%)
  starting transfers between devices  30.9 us (28%)
  Pallas kernels  24.9 us (22%)
  waiting for transfers between devices  20.9 us (19%)
  local copies, waits for them, and re-layouts  1.4 us (1%)
    all_to_all x2, blocking collectives, swap(): lax.all_to_all(x, axes, split_axis=0, concat_axis=0, axis_index_groups=gr...  31.5 us
    all_to_all x2, waiting for transfers between devices, swap(): lax.all_to_all(x, axes, split_axis=0, concat_axis=0, axis_index_groups=gr...  16 us
    all_to_all x2, starting transfers between devices, swap(): lax.all_to_all(x, axes, split_axis=0, concat_axis=0, axis_index_groups=gr...  14.9 us
    ppermute x3, starting transfers between devices, local(): far = [lax.ppermute(low, 'gz', onward) for low in near]  8.86 us
    pallas_call x1, Pallas kernels, x_part(): pl.pallas_call(x_kernel, in_specs=[SMEM] + [HBM] * 6, out_specs=HBM, out_...  8.7 us
    ppermute x3, starting transfers between devices, local(): near = [lax.ppermute(low, 'gz', pair) for low in lows]  7.19 us
    pallas_call x1, Pallas kernels, local_part(): pl.pallas_call(functools.partial(local_kernel, count), in_specs=[SMEM, SM...  6.46 us
    ppermute x3, waiting for transfers between devices, local(): near = [lax.ppermute(low, 'gz', pair) for low in lows]  4.91 us
  transfers between devices with their start and end apart: 8, of which 3 were waited for; matrix products, arithmetic and copies ran while one was open for 0% of the time, Pallas kernels for 15%

profile of v7, /device:TPU:1, one launch (start us, length us, event | category | flops | bytes accessed | tf_op | source)
XLA Modules:
  0.0 110.5 jit_solution(16595023767422215074)
XLA Ops:
  0.6 2.5 %pack.1 = (bf16[8,4,128,128]{3,2,1,0:T(8,128)(2,1)}, bf16[1024,128]{1,0:T(8,128)(2,1)}, bf16[1024,128]{1,0:T(8,128)(2,1)}, bf16[1024,128]{1,0:T(8,128)(2,1)}) custom-call(f32[3,1024,128]{2,1,0:T(8,128)} %bitcast.8, bf16[3,1024,128]{2,1,0:T(8,128)(2,1)} %bitcast.11), custom_call_target="tpu_custom_call" | custom-call | bytes 4194304 | tf_op jit(solution)/shard_map/pack/pallas_call | solution.py:120
  3.2 10.3 %all-to-all-start = ((bf16[8,4,128,128]{3,2,1,0:T(8,128)(2,1)}), bf16[8,4,128,128]{3,2,1,0:T(8,128)(2,1)S(1)}, u32[]{:S(2)}, u32[]{:S(2)}) async-start(bf16[8,4,128,128]{3,2,1,0:T(8,128)(2,1)} %get-tuple-element.17), calls=%async_computation | async-start | bytes 2097152 | tf_op jit(solution)/shard_map/all_to_all | solution.py:423
  13.5 1.9 %collective-permute-start = (bf16[1024,128]{1,0:T(8,128)(2,1)}, bf16[1024,128]{1,0:T(8,128)(2,1)S(1)}, u32[]{:S(2)}, u32[]{:S(2)}) collective-permute-start(bf16[1024,128]{1,0:T(8,128)(2,1)} %get-tuple-element.12.l0), channel_id=1, source_target_pairs={{0,8},{8,0},{16,24},{24,16},{32,40},{40,32},{48,56},{56,48},{64,72... | collective-permute-start | bytes 786440 | tf_op jit(solution)/shard_map/ppermute | solution.py:447
  15.4 3.4 %collective-permute-start.1 = (bf16[1024,128]{1,0:T(8,128)(2,1)}, bf16[1024,128]{1,0:T(8,128)(2,1)}, u32[]{:S(2)}, u32[]{:S(2)}) collective-permute-start(bf16[1024,128]{1,0:T(8,128)(2,1)} %get-tuple-element.13.l1), channel_id=1, source_target_pairs={{0,8},{8,0},{16,24},{24,16},{32,40},{40,32},{48,56},{56,48},{64,72... | collective-permute-start | bytes 786440 | tf_op jit(solution)/shard_map/ppermute | solution.py:447
  18.8 1.9 %collective-permute-start.2 = (bf16[1024,128]{1,0:T(8,128)(2,1)}, bf16[1024,128]{1,0:T(8,128)(2,1)}, u32[]{:S(2)}, u32[]{:S(2)}) collective-permute-start(bf16[1024,128]{1,0:T(8,128)(2,1)} %get-tuple-element.14.l2), channel_id=1, source_target_pairs={{0,8},{8,0},{16,24},{24,16},{32,40},{40,32},{48,56},{56,48},{64,72... | collective-permute-start | bytes 786440 | tf_op jit(solution)/shard_map/ppermute | solution.py:447
  20.8 0.1 pad_maximum_fusion.after.scal
  20.9 8.7 %x_part.1.part.after = f32[3,1024,128]{2,1,0:T(8,128)} custom-call(f32[2]{0:T(128)S(1)} %pad_maximum_fusion.after.scal, bf16[1024,1024]{1,0:T(8,128)(2,1)} %constant.37.clone.fwd, bf16[4,512,1024]{2,1,0:T(8,128)(2,1)} %constant.38.clone.inv, bf16[1024,128]{1,0:T(8,128)(2,1)} %get-tuple-element.12.l0, bf16[1024,128]{1,0:T(8,128)(2,1)} %get-tuple-element.13.l1, ...), custom_call_target="tpu_custom_call" | custom-call | flops 2415919104 | bytes 12582912 | tf_op jit(solution)/shard_map/x_part/pallas_call | solution.py:181
  29.6 10.4 %all-to-all-done.recv = bf16[8,4,128,128]{3,2,1,0:T(8,128)(2,1)S(1)} async-done(((bf16[8,4,128,128]{3,2,1,0:T(8,128)(2,1)}), bf16[8,4,128,128]{3,2,1,0:T(8,128)(2,1)S(1)}, u32[]{:S(2)}, u32[]{:S(2)}) %all-to-all-start) | async-done | bytes 1048608 | tf_op jit(solution)/shard_map/all_to_all | solution.py:423
  40.0 1.9 %y_part.1 = bf16[8,3,128,128]{3,2,1,0:T(8,128)(2,1)} custom-call(f32[3,1024,128]{2,1,0:T(8,128)} %x_part.1.part.after, bf16[8,4,128,128]{3,2,1,0:T(8,128)(2,1)S(1)} %all-to-all-done.recv, bf16[2,4,512,256]{3,2,1,0:T(8,128)(2,1)S(1)} %copy-done.1), custom_call_target="tpu_custom_call" | custom-call | flops 805306368 | bytes 4194304 | tf_op jit(solution)/shard_map/y_part/pallas_call | solution.py:231
  41.9 0.0 copy-start.2
  41.9 4.5 %all-to-all-start.1 = ((bf16[8,3,128,128]{3,2,1,0:T(8,128)(2,1)}), bf16[8,3,128,128]{3,2,1,0:T(8,128)(2,1)S(1)}, u32[]{:S(2)}, u32[]{:S(2)}) async-start(bf16[8,3,128,128]{3,2,1,0:T(8,128)(2,1)} %y_part.1), calls=%async_computation.1 | async-start | bytes 1572864 | tf_op jit(solution)/shard_map/all_to_all | solution.py:423
  46.5 3.1 %collective-permute-start.3 = (bf16[1024,128]{1,0:T(8,128)(2,1)S(1)}, bf16[1024,128]{1,0:T(8,128)(2,1)S(1)}, u32[]{:S(2)}, u32[]{:S(2)}) collective-permute-start(bf16[1024,128]{1,0:T(8,128)(2,1)S(1)} %collective-permute-done.p0), channel_id=1, source_target_pairs={{0,16},{16,32},{32,48},{48,64},{64,80},{80,96},{96,112},{112,128},... | collective-permute-start | bytes 786440 | tf_op jit(solution)/shard_map/ppermute | solution.py:448
  49.6 3.1 %collective-permute-start.4 = (bf16[1024,128]{1,0:T(8,128)(2,1)}, bf16[1024,128]{1,0:T(8,128)(2,1)S(1)}, u32[]{:S(2)}, u32[]{:S(2)}) collective-permute-start(bf16[1024,128]{1,0:T(8,128)(2,1)} %collective-permute-done.1.p1), channel_id=1, source_target_pairs={{0,16},{16,32},{32,48},{48,64},{64,80},{80,96},{96,112},{112,128},... | collective-permute-start | bytes 786440 | tf_op jit(solution)/shard_map/ppermute | solution.py:448
  52.7 4.9 %collective-permute-done.2.p2 = bf16[1024,128]{1,0:T(8,128)(2,1)} collective-permute-done((bf16[1024,128]{1,0:T(8,128)(2,1)}, bf16[1024,128]{1,0:T(8,128)(2,1)}, u32[]{:S(2)}, u32[]{:S(2)}) %collective-permute-start.2) | collective-permute-done | bytes 262176 | tf_op jit(solution)/shard_map/ppermute | solution.py:447
  57.6 2.6 %collective-permute-start.5 = (bf16[1024,128]{1,0:T(8,128)(2,1)}, bf16[1024,128]{1,0:T(8,128)(2,1)S(1)}, u32[]{:S(2)}, u32[]{:S(2)}) collective-permute-start(bf16[1024,128]{1,0:T(8,128)(2,1)} %collective-permute-done.2.p2), channel_id=1, source_target_pairs={{0,16},{16,32},{32,48},{48,64},{64,80},{80,96},{96,112},{112,128},... | collective-permute-start | bytes 786440 | tf_op jit(solution)/shard_map/ppermute | solution.py:448
  60.3 0.7 copy-done.5
  61.0 6.5 %local_part.1 = (f32[3,1024,128]{2,1,0:T(8,128)}, f32[1,128]{1,0:T(1,128)S(1)}) custom-call(f32[2]{0:T(128)S(1)} %pad_maximum_fusion.after.scal, f32[16]{0:T(128)S(1)} %copy-done.2, f32[3,1024,128]{2,1,0:T(8,128)} %x_part.1.part.after, bf16[3,1024,128]{2,1,0:T(8,128)(2,1)} %bitcast.13, s32[1024,128]{1,0:T(8,128)} %classes.3, f32[3,1024,128]{2,1,0:T(8,128)} %bitcast.9, ...), custom_call_target="tpu_custom_call" | custom-call | flops 26214400 | bytes 8388608 | tf_op jit(solution)/shard_map/local_part/pallas_call | solution.py:311
  67.5 0.0 copy-start.4
  67.5 0.7 copy-done.4
  68.2 5.5 %all-to-all-done.1.drift = bf16[8,3,128,128]{3,2,1,0:T(8,128)(2,1)S(1)} async-done(((bf16[8,3,128,128]{3,2,1,0:T(8,128)(2,1)}), bf16[8,3,128,128]{3,2,1,0:T(8,128)(2,1)S(1)}, u32[]{:S(2)}, u32[]{:S(2)}) %all-to-all-start.1) | async-done | bytes 786464 | tf_op jit(solution)/shard_map/all_to_all | solution.py:423
  73.7 3.5 %join.1 = (f32[3,1024,128]{2,1,0:T(8,128)S(1)}, f32[16,1,128]{2,1,0:T(1,128)S(1)}) custom-call(f32[2]{0:T(128)S(1)} %pad_maximum_fusion.after.scal, f32[1,128]{1,0:T(1,128)S(1)} %gate.1.early, f32[3,1024,128]{2,1,0:T(8,128)} %get-tuple-element.16.part, bf16[3,1024,128]{2,1,0:T(8,128)(2,1)} %bitcast.14, s32[1024,128]{1,0:T(8,128)} %classes.3, ...), custom_call_target="tpu_custom_call" | custom-call | flops 13107200 | bytes 8388608 | tf_op jit(solution)/shard_map/join/pallas_call | solution.py:359
  77.2 11.1 %all_to_all.20.got = f32[16,1,128]{2,1,0:T(1,128)S(1)} all-to-all(f32[16,1,128]{2,1,0:T(1,128)S(1)} %get-tuple-element.18), channel_id=1, replica_groups={{0,1,2,3,4,5,6,7,8,9,10,11,12,13,14,15},{16,17,18,19,20,21,22,23,24,25,..., dimensions={0} | all-to-all | bytes 16384 | tf_op jit(solution)/shard_map/all_to_all | solution.py:423
  88.3 20.4 %all_to_all.21.got = f32[32,1,128]{2,1,0:T(1,128)S(1)} all-to-all(f32[32,1,128]{2,1,0:T(1,128)S(1)} %fold.1), channel_id=1, replica_groups={{0,16,32,48,64,80,96,112,128,144,160,176,192,208,224,240,256,272,288,30..., dimensions={0} | all-to-all | bytes 32768 | tf_op jit(solution)/shard_map/all_to_all | solution.py:423
  108.7 1.8 %finish.1 = (f32[3,1024,128]{2,1,0:T(8,128)}, f32[1,16]{1,0:T(1,128)}) custom-call(f32[32,1,128]{2,1,0:T(1,128)S(1)} %all_to_all.21.got, f32[3,1024,128]{2,1,0:T(8,128)S(1)} %bitcast.10, f32[3,1024,128]{2,1,0:T(8,128)S(1)} %get-tuple-element.19.rhs), custom_call_target="tpu_custom_call" | custom-call | flops 786432 | bytes 4718592 | tf_op jit(solution)/shard_map/finish/pallas_call | solution.py:410
  (15 shorter events, 0.1 us)
Async XLA Ops:
  3.2 36.8 %all-to-all-start = ((bf16[8,4,128,128]{3,2,1,0:T(8,128)(2,1)}), bf16[8,4,128,128]{3,2,1,0:T(8,128)(2,1)S(1)}, u32[]{:S(2)}, u32[]{:S(2)}) async-start(bf16[8,4,128,128]{3,2,1,0:T(8,128)(2,1)} %get-tuple-element.17), calls=%async_computation | async-start | bytes 2097152 | tf_op jit(solution)/shard_map/all_to_all | solution.py:423
  13.5 32.9 %collective-permute-start = (bf16[1024,128]{1,0:T(8,128)(2,1)}, bf16[1024,128]{1,0:T(8,128)(2,1)S(1)}, u32[]{:S(2)}, u32[]{:S(2)}) collective-permute-start(bf16[1024,128]{1,0:T(8,128)(2,1)} %get-tuple-element.12.l0), channel_id=1, source_target_pairs={{0,8},{8,0},{16,24},{24,16},{32,40},{40,32},{48,56},{56,48},{64,72... | collective-permute-start | bytes 786440 | tf_op jit(solution)/shard_map/ppermute | solution.py:447
  15.4 34.2 %collective-permute-start.1 = (bf16[1024,128]{1,0:T(8,128)(2,1)}, bf16[1024,128]{1,0:T(8,128)(2,1)}, u32[]{:S(2)}, u32[]{:S(2)}) collective-permute-start(bf16[1024,128]{1,0:T(8,128)(2,1)} %get-tuple-element.13.l1), channel_id=1, source_target_pairs={{0,8},{8,0},{16,24},{24,16},{32,40},{40,32},{48,56},{56,48},{64,72... | collective-permute-start | bytes 786440 | tf_op jit(solution)/shard_map/ppermute | solution.py:447
  18.8 38.8 %collective-permute-start.2 = (bf16[1024,128]{1,0:T(8,128)(2,1)}, bf16[1024,128]{1,0:T(8,128)(2,1)}, u32[]{:S(2)}, u32[]{:S(2)}) collective-permute-start(bf16[1024,128]{1,0:T(8,128)(2,1)} %get-tuple-element.14.l2), channel_id=1, source_target_pairs={{0,8},{8,0},{16,24},{24,16},{32,40},{40,32},{48,56},{56,48},{64,72... | collective-permute-start | bytes 786440 | tf_op jit(solution)/shard_map/ppermute | solution.py:447
  20.9 19.1 %copy-start.1 = (bf16[2,4,512,256]{3,2,1,0:T(8,128)(2,1)S(1)}, bf16[2,4,512,256]{3,2,1,0:T(8,128)(2,1)}, u32[]{:S(2)}) copy-start(bf16[2,4,512,256]{3,2,1,0:T(8,128)(2,1)} %constant.39.clone.table_v) | copy-start | bytes 6291460
  41.9 19.1 %copy-start.2 = (f32[16]{0:T(128)S(1)}, f32[16]{0:T(128)}, u32[]{:S(2)}) copy-start(f32[16]{0:T(128)} %coef.1) | copy-start | bytes 196
  41.9 31.8 %all-to-all-start.1 = ((bf16[8,3,128,128]{3,2,1,0:T(8,128)(2,1)}), bf16[8,3,128,128]{3,2,1,0:T(8,128)(2,1)S(1)}, u32[]{:S(2)}, u32[]{:S(2)}) async-start(bf16[8,3,128,128]{3,2,1,0:T(8,128)(2,1)} %y_part.1), calls=%async_computation.1 | async-start | bytes 1572864 | tf_op jit(solution)/shard_map/all_to_all | solution.py:423
  46.5 13.8 %copy-start.3 = (bf16[1024,128]{1,0:T(8,128)(2,1)}, bf16[1024,128]{1,0:T(8,128)(2,1)S(1)}, u32[]{:S(2)}) copy-start(bf16[1024,128]{1,0:T(8,128)(2,1)S(1)} %collective-permute-done.p0) | copy-start | bytes 786436
  46.5 13.8 %collective-permute-start.3 = (bf16[1024,128]{1,0:T(8,128)(2,1)S(1)}, bf16[1024,128]{1,0:T(8,128)(2,1)S(1)}, u32[]{:S(2)}, u32[]{:S(2)}) collective-permute-start(bf16[1024,128]{1,0:T(8,128)(2,1)S(1)} %collective-permute-done.p0), channel_id=1, source_target_pairs={{0,16},{16,32},{32,48},{48,64},{64,80},{80,96},{96,112},{112,128},... | collective-permute-start | bytes 786440 | tf_op jit(solution)/shard_map/ppermute | solution.py:448
  49.6 17.9 %collective-permute-start.4 = (bf16[1024,128]{1,0:T(8,128)(2,1)}, bf16[1024,128]{1,0:T(8,128)(2,1)S(1)}, u32[]{:S(2)}, u32[]{:S(2)}) collective-permute-start(bf16[1024,128]{1,0:T(8,128)(2,1)} %collective-permute-done.1.p1), channel_id=1, source_target_pairs={{0,16},{16,32},{32,48},{48,64},{64,80},{80,96},{96,112},{112,128},... | collective-permute-start | bytes 786440 | tf_op jit(solution)/shard_map/ppermute | solution.py:448
  57.6 9.8 %collective-permute-start.5 = (bf16[1024,128]{1,0:T(8,128)(2,1)}, bf16[1024,128]{1,0:T(8,128)(2,1)S(1)}, u32[]{:S(2)}, u32[]{:S(2)}) collective-permute-start(bf16[1024,128]{1,0:T(8,128)(2,1)} %collective-permute-done.2.p2), channel_id=1, source_target_pairs={{0,16},{16,32},{32,48},{48,64},{64,80},{80,96},{96,112},{112,128},... | collective-permute-start | bytes 786440 | tf_op jit(solution)/shard_map/ppermute | solution.py:448
  60.3 0.7 copy-start.5
  67.5 0.7 copy-start.4
  73.7 35.0 %copy-start = (f32[3,1,1024,128]{3,2,1,0:T(8,128)S(1)}, f32[3,1,1024,128]{3,2,1,0:T(8,128)}, u32[]{:S(2)}) copy-start(f32[3,1,1024,128]{3,2,1,0:T(8,128)} %param.7) | copy-start | bytes 4718596

commit v8 on v7

--- a/solution.py
+++ b/solution.py
@@ -323,15 +323,14 @@
     )(scal, coef, *[far_off(a) for a in (part, wind, classes, adj, *near, far)])
 
 
-def join_kernel(count, scal, early, part, wind, classes, q1, q2, drift, rhs, sums,
-                wind_v, cls_v, far_v, acc, sem_in):
+def join_kernel(count, scal, early, part, wind, cls_v, q1, q2, drift, rhs, sums,
+                wind_v, far_v, acc, sem_in):
     parts, _, rows, _ = drift.shape
     per = parts // CHUNKS
     loads = []
     for k in range(CHUNKS):
         at = pl.ds(k * per * rows, per * rows)
-        loads.append(begin([(wind.at[:, at], wind_v.at[:, at]), (classes.at[at], cls_v.at[at]),
-                            (part.at[:, at], rhs.at[:, at]), (q1.at[at], far_v.at[at])], sem_in, 4 * k))
+        loads.append(begin([(wind.at[:, at], wind_v.at[:, at]), (part.at[:, at], rhs.at[:, at]), (q1.at[at], far_v.at[at])], sem_in, 3 * k))
     acc[...] = jnp.zeros_like(acc)
     for k in range(CHUNKS):
         finish_all(loads[k])
@@ -358,15 +357,15 @@
     dma = pltpu.SemaphoreType.DMA
     return pl.pallas_call(
         functools.partial(join_kernel, count),
-        in_specs=[SMEM, SMALL] + [HBM] * 4 + [SMALL] * 2,
+        in_specs=[SMEM, SMALL, HBM, HBM, SMALL, HBM, SMALL, SMALL],
         out_specs=[SMALL, SMALL],
         out_shape=[pltpu.VMEM(whole, f32), jax.ShapeDtypeStruct((2 * parts, 1, LANES), f32)],
-        scratch_shapes=[pltpu.VMEM(whole, bf16), pltpu.VMEM((nx, ny), jnp.int32), pltpu.VMEM((nx, ny), bf16),
-                        pltpu.VMEM((count, 8, ny), f32), dma((4 * CHUNKS,))],
+        scratch_shapes=[pltpu.VMEM(whole, bf16), pltpu.VMEM((nx, ny), bf16),
+                        pltpu.VMEM((count, 8, ny), f32), dma((3 * CHUNKS,))],
         compiler_params=params(),
         cost_estimate=pl.CostEstimate(flops=100 * nx * ny, bytes_accessed=8 * 1024 * 1024, transcendentals=0),
         name="join",
-    )(scal, early, *[far_off(a) for a in (part, wind, classes, far[0])], near_by(far[1]), near_by(drift))
+    )(scal, early, far_off(part), far_off(wind), near_by(classes), far_off(far[0]), near_by(far[1]), near_by(drift))
 
 
 def merge(rows, count):

time: 111 us -> 112 us (level)
  no operation moved by 1% of the time
where the time goes in v8:
time: 112 us; the launch traced here: 111 us
  blocking collectives  32.2 us (29%)
  starting transfers between devices  30.9 us (28%)
  Pallas kernels  24.8 us (22%)
  waiting for transfers between devices  20.9 us (19%)
  local copies, waits for them, and re-layouts  1.4 us (1%)
    all_to_all x2, blocking collectives, swap(): lax.all_to_all(x, axes, split_axis=0, concat_axis=0, axis_index_groups=gr...  32.2 us
    all_to_all x2, waiting for transfers between devices, swap(): lax.all_to_all(x, axes, split_axis=0, concat_axis=0, axis_index_groups=gr...  15.9 us
    all_to_all x2, starting transfers between devices, swap(): lax.all_to_all(x, axes, split_axis=0, concat_axis=0, axis_index_groups=gr...  14.9 us
    ppermute x3, starting transfers between devices, local(): far = [lax.ppermute(low, 'gz', onward) for low in near]  8.86 us
    pallas_call x1, Pallas kernels, x_part(): pl.pallas_call(x_kernel, in_specs=[SMEM] + [HBM] * 6, out_specs=HBM, out_...  8.7 us
    ppermute x3, starting transfers between devices, local(): near = [lax.ppermute(low, 'gz', pair) for low in lows]  7.19 us
    pallas_call x1, Pallas kernels, local_part(): pl.pallas_call(functools.partial(local_kernel, count), in_specs=[SMEM, SM...  6.48 us
    ppermute x3, waiting for transfers between devices, local(): near = [lax.ppermute(low, 'gz', pair) for low in lows]  4.91 us
  transfers between devices with their start and end apart: 8, of which 3 were waited for; matrix products, arithmetic and copies ran while one was open for 0% of the time, Pallas kernels for 15%

profile of v8, /device:TPU:1, one launch (start us, length us, event | category | flops | bytes accessed | tf_op | source)
XLA Modules:
  0.0 111.1 jit_solution(818471417785910105)
XLA Ops:
  0.6 2.5 %pack.1 = (bf16[8,4,128,128]{3,2,1,0:T(8,128)(2,1)}, bf16[1024,128]{1,0:T(8,128)(2,1)}, bf16[1024,128]{1,0:T(8,128)(2,1)}, bf16[1024,128]{1,0:T(8,128)(2,1)}) custom-call(f32[3,1024,128]{2,1,0:T(8,128)} %bitcast.8, bf16[3,1024,128]{2,1,0:T(8,128)(2,1)} %bitcast.11), custom_call_target="tpu_custom_call" | custom-call | bytes 4194304 | tf_op jit(solution)/shard_map/pack/pallas_call | solution.py:120
  3.1 10.3 %all-to-all-start = ((bf16[8,4,128,128]{3,2,1,0:T(8,128)(2,1)}), bf16[8,4,128,128]{3,2,1,0:T(8,128)(2,1)S(1)}, u32[]{:S(2)}, u32[]{:S(2)}) async-start(bf16[8,4,128,128]{3,2,1,0:T(8,128)(2,1)} %get-tuple-element.17), calls=%async_computation | async-start | bytes 2097152 | tf_op jit(solution)/shard_map/all_to_all | solution.py:422
  13.5 1.9 %collective-permute-start = (bf16[1024,128]{1,0:T(8,128)(2,1)}, bf16[1024,128]{1,0:T(8,128)(2,1)S(1)}, u32[]{:S(2)}, u32[]{:S(2)}) collective-permute-start(bf16[1024,128]{1,0:T(8,128)(2,1)} %get-tuple-element.12.l0), channel_id=1, source_target_pairs={{0,8},{8,0},{16,24},{24,16},{32,40},{40,32},{48,56},{56,48},{64,72... | collective-permute-start | bytes 786440 | tf_op jit(solution)/shard_map/ppermute | solution.py:446
  15.4 3.4 %collective-permute-start.1 = (bf16[1024,128]{1,0:T(8,128)(2,1)}, bf16[1024,128]{1,0:T(8,128)(2,1)}, u32[]{:S(2)}, u32[]{:S(2)}) collective-permute-start(bf16[1024,128]{1,0:T(8,128)(2,1)} %get-tuple-element.13.l1), channel_id=1, source_target_pairs={{0,8},{8,0},{16,24},{24,16},{32,40},{40,32},{48,56},{56,48},{64,72... | collective-permute-start | bytes 786440 | tf_op jit(solution)/shard_map/ppermute | solution.py:446
  18.8 1.9 %collective-permute-start.2 = (bf16[1024,128]{1,0:T(8,128)(2,1)}, bf16[1024,128]{1,0:T(8,128)(2,1)}, u32[]{:S(2)}, u32[]{:S(2)}) collective-permute-start(bf16[1024,128]{1,0:T(8,128)(2,1)} %get-tuple-element.14.l2), channel_id=1, source_target_pairs={{0,8},{8,0},{16,24},{24,16},{32,40},{40,32},{48,56},{56,48},{64,72... | collective-permute-start | bytes 786440 | tf_op jit(solution)/shard_map/ppermute | solution.py:446
  20.8 0.1 pad_maximum_fusion.after.scal
  20.8 8.7 %x_part.1.part.after = f32[3,1024,128]{2,1,0:T(8,128)} custom-call(f32[2]{0:T(128)S(1)} %pad_maximum_fusion.after.scal, bf16[1024,1024]{1,0:T(8,128)(2,1)} %constant.37.clone.fwd, bf16[4,512,1024]{2,1,0:T(8,128)(2,1)} %constant.38.clone.inv, bf16[1024,128]{1,0:T(8,128)(2,1)} %get-tuple-element.12.l0, bf16[1024,128]{1,0:T(8,128)(2,1)} %get-tuple-element.13.l1, ...), custom_call_target="tpu_custom_call" | custom-call | flops 2415919104 | bytes 12582912 | tf_op jit(solution)/shard_map/x_part/pallas_call | solution.py:181
  29.6 10.4 %all-to-all-done.recv = bf16[8,4,128,128]{3,2,1,0:T(8,128)(2,1)S(1)} async-done(((bf16[8,4,128,128]{3,2,1,0:T(8,128)(2,1)}), bf16[8,4,128,128]{3,2,1,0:T(8,128)(2,1)S(1)}, u32[]{:S(2)}, u32[]{:S(2)}) %all-to-all-start) | async-done | bytes 1048608 | tf_op jit(solution)/shard_map/all_to_all | solution.py:422
  40.0 1.9 %y_part.1 = bf16[8,3,128,128]{3,2,1,0:T(8,128)(2,1)} custom-call(f32[3,1024,128]{2,1,0:T(8,128)} %x_part.1.part.after, bf16[8,4,128,128]{3,2,1,0:T(8,128)(2,1)S(1)} %all-to-all-done.recv, bf16[2,4,512,256]{3,2,1,0:T(8,128)(2,1)S(1)} %copy-done.2), custom_call_target="tpu_custom_call" | custom-call | flops 805306368 | bytes 4194304 | tf_op jit(solution)/shard_map/y_part/pallas_call | solution.py:231
  41.9 0.0 copy-start.3
  41.9 4.5 %all-to-all-start.1 = ((bf16[8,3,128,128]{3,2,1,0:T(8,128)(2,1)}), bf16[8,3,128,128]{3,2,1,0:T(8,128)(2,1)S(1)}, u32[]{:S(2)}, u32[]{:S(2)}) async-start(bf16[8,3,128,128]{3,2,1,0:T(8,128)(2,1)} %y_part.1), calls=%async_computation.1 | async-start | bytes 1572864 | tf_op jit(solution)/shard_map/all_to_all | solution.py:422
  46.4 3.1 %collective-permute-start.3 = (bf16[1024,128]{1,0:T(8,128)(2,1)S(1)}, bf16[1024,128]{1,0:T(8,128)(2,1)S(1)}, u32[]{:S(2)}, u32[]{:S(2)}) collective-permute-start(bf16[1024,128]{1,0:T(8,128)(2,1)S(1)} %collective-permute-done.p0), channel_id=1, source_target_pairs={{0,16},{16,32},{32,48},{48,64},{64,80},{80,96},{96,112},{112,128},... | collective-permute-start | bytes 786440 | tf_op jit(solution)/shard_map/ppermute | solution.py:447
  49.6 3.1 %collective-permute-start.4 = (bf16[1024,128]{1,0:T(8,128)(2,1)}, bf16[1024,128]{1,0:T(8,128)(2,1)S(1)}, u32[]{:S(2)}, u32[]{:S(2)}) collective-permute-start(bf16[1024,128]{1,0:T(8,128)(2,1)} %collective-permute-done.1.p1), channel_id=1, source_target_pairs={{0,16},{16,32},{32,48},{48,64},{64,80},{80,96},{96,112},{112,128},... | collective-permute-start | bytes 786440 | tf_op jit(solution)/shard_map/ppermute | solution.py:447
  52.7 4.9 %collective-permute-done.2.p2 = bf16[1024,128]{1,0:T(8,128)(2,1)} collective-permute-done((bf16[1024,128]{1,0:T(8,128)(2,1)}, bf16[1024,128]{1,0:T(8,128)(2,1)}, u32[]{:S(2)}, u32[]{:S(2)}) %collective-permute-start.2) | collective-permute-done | bytes 262176 | tf_op jit(solution)/shard_map/ppermute | solution.py:446
  57.6 2.6 %collective-permute-start.5 = (bf16[1024,128]{1,0:T(8,128)(2,1)}, bf16[1024,128]{1,0:T(8,128)(2,1)S(1)}, u32[]{:S(2)}, u32[]{:S(2)}) collective-permute-start(bf16[1024,128]{1,0:T(8,128)(2,1)} %collective-permute-done.2.p2), channel_id=1, source_target_pairs={{0,16},{16,32},{32,48},{48,64},{64,80},{80,96},{96,112},{112,128},... | collective-permute-start | bytes 786440 | tf_op jit(solution)/shard_map/ppermute | solution.py:447
  60.3 0.7 copy-done.6
  61.0 6.5 %local_part.1 = (f32[3,1024,128]{2,1,0:T(8,128)}, f32[1,128]{1,0:T(1,128)S(1)}) custom-call(f32[2]{0:T(128)S(1)} %pad_maximum_fusion.after.scal, f32[16]{0:T(128)S(1)} %copy-done.3, f32[3,1024,128]{2,1,0:T(8,128)} %x_part.1.part.after, bf16[3,1024,128]{2,1,0:T(8,128)(2,1)} %bitcast.13, s32[1024,128]{1,0:T(8,128)} %cls_v.1, f32[3,1024,128]{2,1,0:T(8,128)} %bitcast.9, ...), custom_call_target="tpu_custom_call" | custom-call | flops 26214400 | bytes 8388608 | tf_op jit(solution)/shard_map/local_part/pallas_call | solution.py:311
  67.5 0.0 copy-start.5
  67.5 0.7 copy-done.5
  68.2 5.5 %all-to-all-done.1.drift = bf16[8,3,128,128]{3,2,1,0:T(8,128)(2,1)S(1)} async-done(((bf16[8,3,128,128]{3,2,1,0:T(8,128)(2,1)}), bf16[8,3,128,128]{3,2,1,0:T(8,128)(2,1)S(1)}, u32[]{:S(2)}, u32[]{:S(2)}) %all-to-all-start.1) | async-done | bytes 786464 | tf_op jit(solution)/shard_map/all_to_all | solution.py:422
  73.7 3.3 %join.1 = (f32[3,1024,128]{2,1,0:T(8,128)S(1)}, f32[16,1,128]{2,1,0:T(1,128)S(1)}) custom-call(f32[2]{0:T(128)S(1)} %pad_maximum_fusion.after.scal, f32[1,128]{1,0:T(1,128)S(1)} %gate.1.early, f32[3,1024,128]{2,1,0:T(8,128)} %get-tuple-element.16.part, bf16[3,1024,128]{2,1,0:T(8,128)(2,1)} %bitcast.14, s32[1024,128]{1,0:T(8,128)S(1)} %copy-done.1, ...), custom_call_target="tpu_custom_call" | custom-call | flops 13107200 | bytes 8388608 | tf_op jit(solution)/shard_map/join/pallas_call | solution.py:358
  77.0 11.1 %all_to_all.20.got = f32[16,1,128]{2,1,0:T(1,128)S(1)} all-to-all(f32[16,1,128]{2,1,0:T(1,128)S(1)} %get-tuple-element.18), channel_id=1, replica_groups={{0,1,2,3,4,5,6,7,8,9,10,11,12,13,14,15},{16,17,18,19,20,21,22,23,24,25,..., dimensions={0} | all-to-all | bytes 16384 | tf_op jit(solution)/shard_map/all_to_all | solution.py:422
  88.1 21.1 %all_to_all.21.got = f32[32,1,128]{2,1,0:T(1,128)S(1)} all-to-all(f32[32,1,128]{2,1,0:T(1,128)S(1)} %fold.1), channel_id=1, replica_groups={{0,16,32,48,64,80,96,112,128,144,160,176,192,208,224,240,256,272,288,30..., dimensions={0} | all-to-all | bytes 32768 | tf_op jit(solution)/shard_map/all_to_all | solution.py:422
  109.3 1.8 %finish.1 = (f32[3,1024,128]{2,1,0:T(8,128)}, f32[1,16]{1,0:T(1,128)}) custom-call(f32[32,1,128]{2,1,0:T(1,128)S(1)} %all_to_all.21.got, f32[3,1024,128]{2,1,0:T(8,128)S(1)} %bitcast.10, f32[3,1024,128]{2,1,0:T(8,128)S(1)} %get-tuple-element.19.rhs), custom_call_target="tpu_custom_call" | custom-call | flops 786432 | bytes 4718592 | tf_op jit(solution)/shard_map/finish/pallas_call | solution.py:409
  (17 shorter events, 0.1 us)
Async XLA Ops:
  3.1 36.8 %all-to-all-start = ((bf16[8,4,128,128]{3,2,1,0:T(8,128)(2,1)}), bf16[8,4,128,128]{3,2,1,0:T(8,128)(2,1)S(1)}, u32[]{:S(2)}, u32[]{:S(2)}) async-start(bf16[8,4,128,128]{3,2,1,0:T(8,128)(2,1)} %get-tuple-element.17), calls=%async_computation | async-start | bytes 2097152 | tf_op jit(solution)/shard_map/all_to_all | solution.py:422
  13.5 32.9 %collective-permute-start = (bf16[1024,128]{1,0:T(8,128)(2,1)}, bf16[1024,128]{1,0:T(8,128)(2,1)S(1)}, u32[]{:S(2)}, u32[]{:S(2)}) collective-permute-start(bf16[1024,128]{1,0:T(8,128)(2,1)} %get-tuple-element.12.l0), channel_id=1, source_target_pairs={{0,8},{8,0},{16,24},{24,16},{32,40},{40,32},{48,56},{56,48},{64,72... | collective-permute-start | bytes 786440 | tf_op jit(solution)/shard_map/ppermute | solution.py:446
  15.4 34.2 %collective-permute-start.1 = (bf16[1024,128]{1,0:T(8,128)(2,1)}, bf16[1024,128]{1,0:T(8,128)(2,1)}, u32[]{:S(2)}, u32[]{:S(2)}) collective-permute-start(bf16[1024,128]{1,0:T(8,128)(2,1)} %get-tuple-element.13.l1), channel_id=1, source_target_pairs={{0,8},{8,0},{16,24},{24,16},{32,40},{40,32},{48,56},{56,48},{64,72... | collective-permute-start | bytes 786440 | tf_op jit(solution)/shard_map/ppermute | solution.py:446
  18.8 38.8 %collective-permute-start.2 = (bf16[1024,128]{1,0:T(8,128)(2,1)}, bf16[1024,128]{1,0:T(8,128)(2,1)}, u32[]{:S(2)}, u32[]{:S(2)}) collective-permute-start(bf16[1024,128]{1,0:T(8,128)(2,1)} %get-tuple-element.14.l2), channel_id=1, source_target_pairs={{0,8},{8,0},{16,24},{24,16},{32,40},{40,32},{48,56},{56,48},{64,72... | collective-permute-start | bytes 786440 | tf_op jit(solution)/shard_map/ppermute | solution.py:446
  20.8 19.1 %copy-start.2 = (bf16[2,4,512,256]{3,2,1,0:T(8,128)(2,1)S(1)}, bf16[2,4,512,256]{3,2,1,0:T(8,128)(2,1)}, u32[]{:S(2)}) copy-start(bf16[2,4,512,256]{3,2,1,0:T(8,128)(2,1)} %constant.39.clone.table_v) | copy-start | bytes 6291460
  41.9 19.1 %copy-start.3 = (f32[16]{0:T(128)S(1)}, f32[16]{0:T(128)}, u32[]{:S(2)}) copy-start(f32[16]{0:T(128)} %coef.1) | copy-start | bytes 196
  41.9 31.8 %all-to-all-start.1 = ((bf16[8,3,128,128]{3,2,1,0:T(8,128)(2,1)}), bf16[8,3,128,128]{3,2,1,0:T(8,128)(2,1)S(1)}, u32[]{:S(2)}, u32[]{:S(2)}) async-start(bf16[8,3,128,128]{3,2,1,0:T(8,128)(2,1)} %y_part.1), calls=%async_computation.1 | async-start | bytes 1572864 | tf_op jit(solution)/shard_map/all_to_all | solution.py:422
  46.4 13.8 %copy-start.4 = (bf16[1024,128]{1,0:T(8,128)(2,1)}, bf16[1024,128]{1,0:T(8,128)(2,1)S(1)}, u32[]{:S(2)}) copy-start(bf16[1024,128]{1,0:T(8,128)(2,1)S(1)} %collective-permute-done.p0) | copy-start | bytes 786436
  46.4 13.8 %collective-permute-start.3 = (bf16[1024,128]{1,0:T(8,128)(2,1)S(1)}, bf16[1024,128]{1,0:T(8,128)(2,1)S(1)}, u32[]{:S(2)}, u32[]{:S(2)}) collective-permute-start(bf16[1024,128]{1,0:T(8,128)(2,1)S(1)} %collective-permute-done.p0), channel_id=1, source_target_pairs={{0,16},{16,32},{32,48},{48,64},{64,80},{80,96},{96,112},{112,128},... | collective-permute-start | bytes 786440 | tf_op jit(solution)/shard_map/ppermute | solution.py:447
  49.6 17.9 %collective-permute-start.4 = (bf16[1024,128]{1,0:T(8,128)(2,1)}, bf16[1024,128]{1,0:T(8,128)(2,1)S(1)}, u32[]{:S(2)}, u32[]{:S(2)}) collective-permute-start(bf16[1024,128]{1,0:T(8,128)(2,1)} %collective-permute-done.1.p1), channel_id=1, source_target_pairs={{0,16},{16,32},{32,48},{48,64},{64,80},{80,96},{96,112},{112,128},... | collective-permute-start | bytes 786440 | tf_op jit(solution)/shard_map/ppermute | solution.py:447
  57.6 9.9 %collective-permute-start.5 = (bf16[1024,128]{1,0:T(8,128)(2,1)}, bf16[1024,128]{1,0:T(8,128)(2,1)S(1)}, u32[]{:S(2)}, u32[]{:S(2)}) collective-permute-start(bf16[1024,128]{1,0:T(8,128)(2,1)} %collective-permute-done.2.p2), channel_id=1, source_target_pairs={{0,16},{16,32},{32,48},{48,64},{64,80},{80,96},{96,112},{112,128},... | collective-permute-start | bytes 786440 | tf_op jit(solution)/shard_map/ppermute | solution.py:447
  60.3 0.7 copy-start.6
  67.5 0.7 copy-start.5
  68.2 5.5 %copy-start.1 = (s32[1024,128]{1,0:T(8,128)S(1)}, s32[1024,128]{1,0:T(8,128)}, u32[]{:S(2)}) copy-start(s32[1024,128]{1,0:T(8,128)} %cls_v.1) | copy-start | bytes 1572868
  73.7 35.6 %copy-start = (f32[3,1,1024,128]{3,2,1,0:T(8,128)S(1)}, f32[3,1,1024,128]{3,2,1,0:T(8,128)}, u32[]{:S(2)}) copy-start(f32[3,1,1024,128]{3,2,1,0:T(8,128)} %param.7) | copy-start | bytes 4718596
